TPU v7x, 256 devices: a whole 4x4x8 slice. The times are simulated.
256 devices in a mesh: dp: 4 (over x), tm: 16 (over z, core), head: 4 (over y).
Axes of the slice: x: 4, y: 4, z: 8, core: 2. Of those that a mesh axis runs over, the one named last changes fastest.
Arguments:
- query_in: bfloat16 [4, 1024, 1280], P('dp', 'tm'), may hold values from -60 to 60
- grad_out: bfloat16 [4, 1024, 1280], P('dp', 'tm'), may hold values from -6 to 6
- encoder_states: bfloat16 [4, 4096, 1280], P('dp', 'tm'), may hold values from -24 to 24
- frame_lengths: int32 [4], P('dp'), may hold values from 2048 to 4096, as said below
- w_query: bfloat16 [1280, 1280], P(None, 'head'), may hold values from -0.15625 to 0.15625
- w_key: bfloat16 [1280, 1280], P(None, 'head'), may hold values from -0.15625 to 0.15625
- w_value: bfloat16 [1280, 1280], P(None, 'head'), may hold values from -0.15625 to 0.15625
- w_out: bfloat16 [1280, 1280], P('head'), may hold values from -0.15625 to 0.15625
Outputs:
- grad_query_in: bfloat16 [4, 1024, 1280], P('dp', 'tm', 'head')
- grad_encoder: bfloat16 [4, 4096, 1280], P('dp', 'tm', 'head')
- grad_w_query: float32 [1280, 1280], P(('dp', 'tm'), 'head')
- grad_w_key: float32 [1280, 1280], P(('dp', 'tm'), 'head')
- grad_w_value: float32 [1280, 1280], P(('dp', 'tm'), 'head')
- grad_w_out: float32 [1280, 1280], P('head', ('dp', 'tm'))
Inputs may be any that keep to these rules, and one draw needn't show every extreme that they name: `frame_lengths`: multiples of 128; some recording has all 4096 frames valid and another exactly half of them.
All inputs are finite; a program needn't handle non-finite values.
Results may differ from a plain program's by a relative error of at most 0.024.
The roundings to bfloat16 on the way count: a program that leaves them out, or rounds other values in their place, can miss the bound.
Values may be sent and summed in bfloat16 or wider, within the bound.
No kernel may reach another device: no remote copies, remote signals or barrier semaphores. Data moves between devices by JAX's collectives and lax.ppermute only.
A program may use at most 128 MiB of HBM per device.

v0:
```python
import functools
import math

import jax
import jax.numpy as jnp
from jax import lax
from jax.experimental import pallas as pl
from jax.experimental.pallas import tpu as pltpu
from jax.sharding import Mesh, PartitionSpec as P

HD = 64
BF = jnp.bfloat16
F32 = jnp.float32
SCALE = HD ** (-0.5)
LOG2 = SCALE * math.log2(math.e)
LOW = -1e30
NT = (((1,), (1,)), ((), ()))
TN = (((0,), (0,)), ((), ()))


def mm(left, right, dims=None):
    if dims is None:
        dims = (((1,), (0,)), ((), ()))
    return lax.dot_general(left, right, dims, preferred_element_type=F32)


def flip(x, axis, size, bits):
    return lax.ppermute(x, axis, [(i, i ^ bits) for i in range(size)])


def swap(x, axis):
    return flip(x, axis, 2, 1)


def frame_bias(valid_ref, block, rows):
    positions = lax.broadcasted_iota(jnp.int32, (rows, 1), 0)
    return jnp.where(positions < valid_ref[block], 0.0, LOW)


def stats_kernel(heads, valid_ref, *refs):
    rows_refs, frame_refs, out_ref = refs[:4], refs[4:8], refs[8]
    width = heads * HD
    rows = jnp.concatenate([r[...] for r in rows_refs], axis=0)
    blocks = [r[...] for r in frame_refs]
    biases = [frame_bias(valid_ref, j, b.shape[0]) for j, b in enumerate(blocks)]
    out_ref[...] = jnp.zeros_like(out_ref)
    for h in range(heads):
        cut = slice(h * HD, (h + 1) * HD)
        cut2 = slice(width + h * HD, width + (h + 1) * HD)
        query, dout = rows[:, cut], rows[:, cut2]
        scores = [
            mm(b[:, cut], query, NT) * LOG2 + bias for b, bias in zip(blocks, biases)
        ]
        top = functools.reduce(
            jnp.maximum, [jnp.max(s, axis=0, keepdims=True) for s in scores]
        )
        top = jnp.maximum(top, 0.1 * LOW)
        total = jnp.zeros_like(top)
        delta = jnp.zeros_like(top)
        for s, b in zip(scores, blocks):
            weight = jnp.exp2(s - top)
            dprobs = mm(b[:, cut2], dout, NT)
            total += jnp.sum(weight, axis=0, keepdims=True)
            delta += jnp.sum(weight * dprobs, axis=0, keepdims=True)
        total = jnp.maximum(total, 1.0)
        out_ref[h : h + 1, :] = top + jnp.log2(total)
        out_ref[8 + h : 9 + h, :] = delta / total


def in_own_order(x, k, own):
    if k & 2:
        x = pltpu.roll(x, 2 * own, 1)
    if k & 1:
        lane = lax.broadcasted_iota(jnp.int32, x.shape, 1)
        x = jnp.where(
            lane % (2 * own) < own, pltpu.roll(x, 3 * own, 1), pltpu.roll(x, own, 1)
        )
    return x


def grads_kernel(heads, valid_ref, *refs):
    rows_refs, frame_refs, stat_refs = refs[:4], refs[4:8], refs[8:12]
    dkv_ref, dq_refs = refs[12], refs[13:17]
    width = heads * HD
    rows = jnp.concatenate([r[...] for r in rows_refs], axis=0)
    blocks = [r[...] for r in frame_refs]
    part = blocks[0].shape[0]
    own = rows_refs[0].shape[0]
    stats = [in_own_order(stat_refs[k][...], k, own) for k in range(4)]
    tops = [s[:8] for s in stats]
    top = functools.reduce(jnp.maximum, tops)
    shares = [jnp.exp2(t - top) for t in tops]
    total = functools.reduce(jnp.add, shares)
    lse = top + jnp.log2(total)
    delta = functools.reduce(
        jnp.add, [w * s[8:] for w, s in zip(shares, stats)]
    ) / total
    biases = [frame_bias(valid_ref, j, part) for j in range(4)]
    dq_t, att_t = [], []
    for h in range(heads):
        cut = slice(h * HD, (h + 1) * HD)
        cut2 = slice(width + h * HD, width + (h + 1) * HD)
        query, dout = rows[:, cut], rows[:, cut2]
        dq_sum = jnp.zeros((HD, rows.shape[0]), F32)
        att_sum = jnp.zeros((HD, rows.shape[0]), F32)
        for j, (b, bias) in enumerate(zip(blocks, biases)):
            key, value = b[:, cut], b[:, cut2]
            scores = mm(key, query, NT) * LOG2 + bias
            probs = jnp.exp2(scores - lse[h : h + 1])
            dprobs = mm(value, dout, NT)
            dscores = (probs * (dprobs - delta[h : h + 1])).astype(BF)
            probs = probs.astype(BF)
            dkey = mm(dscores, query) * SCALE
            dvalue = mm(probs, dout)
            span = slice(j * part, (j + 1) * part)
            dkv_ref[span, cut] = dkey.astype(dkv_ref.dtype)
            dkv_ref[span, cut2] = dvalue.astype(dkv_ref.dtype)
            dq_sum += mm(key, dscores, TN)
            att_sum += mm(value, probs, TN)
        dq_t.append(dq_sum * SCALE)
        att_t.append(att_sum)
    joined = jnp.concatenate(dq_t + att_t, axis=0).T
    for k in range(4):
        dq_refs[k][...] = joined[k * own : (k + 1) * own].astype(dq_refs[k].dtype)


def fetch(pairs, sems):
    copies = [
        pltpu.make_async_copy(source, target, sems.at[i])
        for i, (source, target) in enumerate(pairs)
    ]
    for copy in copies:
        copy.start()
    return copies


def project_kernel(
    left_ref, right_ref, frames_ref, wq_ref, wo_ref, wk_ref, wv_ref, rows_ref, kv_ref,
    left, right, frames, wq, wo, wk, wv, sems,
):
    width = wq.shape[0]
    half = width // 2
    pairs = [(left_ref, left)]
    for source, target in ((wq_ref, wq), (wo_ref, wo), (wk_ref, wk), (wv_ref, wv)):
        pairs += [
            (source.at[:half], target.at[:half]),
            (source.at[half:], target.at[half:]),
        ]
        if source is wq_ref:
            pairs.append((right_ref, right))
        if source is wo_ref:
            pairs.append((frames_ref, frames))
    copies = fetch(pairs, sems)
    for i, (x, w, out, side) in enumerate(
        ((left, wq, rows_ref, 0), (right, wo, rows_ref, 1), (frames, wk, kv_ref, 0), (frames, wv, kv_ref, 1))
    ):
        for copy in copies[3 * i : 3 * i + 3]:
            copy.wait()
        out[:, side * width : (side + 1) * width] = mm(x[...], w[...], NT).astype(BF)


def kv_weights_kernel(xt_ref, xt2_ref, xp_ref, xp2_ref, y_ref, y2_ref, *out_refs):
    part = y_ref.shape[0] // 4
    step = out_refs[0].shape[0]
    sums = []
    for j in range(4):
        near = slice(j * part, (j + 1) * part)
        far = slice((j ^ 1) * part, ((j ^ 1) + 1) * part)
        total = y_ref[near].astype(F32) + y2_ref[far].astype(F32)
        if j == 0:
            out_refs[4][...] = total
        sums.append(total.astype(BF))
    out_refs[5][...] = sums[2]
    for k in (2, 3, 1, 0):
        span = slice(k * step, (k + 1) * step)
        total = mm(xt_ref[span, :part], sums[0]) + mm(xt2_ref[span, :part], sums[1])
        total += mm(xp_ref[span], sums[2]) + mm(xp2_ref[span], sums[3])
        out_refs[k][...] = total.astype(out_refs[k].dtype)


def qo_weights_kernel(xt_ref, xt2_ref, y_ref, y2_ref, *out_refs):
    own = y_ref.shape[0]
    half = y_ref.shape[1] // 2
    step = out_refs[0].shape[0]
    first = xt_ref.shape[1] - 2 * own
    for k in (2, 3, 1, 0):
        span = slice(k * step, (k + 1) * step)
        for side in (0, 1):
            cols = slice(side * half, (side + 1) * half)
            at = slice(first + side * own, first + (side + 1) * own)
            total = mm(xt_ref[span, at], y_ref[:, cols]) + mm(xt2_ref[span, at], y2_ref[:, cols])
            out_refs[k][:, cols] = total.astype(out_refs[k].dtype)


def inputs_kernel(where_ref, near_ref, pair_ref, dq_ref, wk_ref, wv_ref, wq_ref, own_ref, *refs):
    send_refs, scratch = refs[:3], refs[3]
    width = wk_ref.shape[0]
    part = near_ref.shape[0]
    dkv = (near_ref[...] + pair_ref[...].astype(F32)).astype(BF)
    dkey, dvalue, dquery = dkv[:, :width], dkv[:, width:], dq_ref[:, :width]
    for t in range(4):
        span = slice(t * width, (t + 1) * width)
        scratch[t, :part] = mm(dkey, wk_ref[:, span]) + mm(dvalue, wv_ref[:, span])
        scratch[t, part:] = mm(dquery, wq_ref[:, span])
    own_ref[...] = scratch[where_ref[0]]
    for k in (1, 2, 3):
        send_refs[k - 1][...] = scratch[where_ref[0] ^ k].astype(BF)


VMEM = pl.BlockSpec(memory_space=pltpu.VMEM)
SMEM = pl.BlockSpec(memory_space=pltpu.SMEM)


def per_device(query_in, grad_out, encoder_states, frame_lengths, w_query, w_key, w_value, w_out):
    rows_in, rows_grad, frames = query_in[0], grad_out[0], encoder_states[0]
    width = w_query.shape[1]
    heads = width // HD
    model = w_query.shape[0]
    inner = model // 64
    own, slab = rows_in.shape[0], frames.shape[0]
    quarter = slab // 4
    xi, zi, ci, yi = (lax.axis_index(n) for n in ("dp", "z", "core", "head"))
    wq_t, wk_t, wv_t = w_query.T, w_key.T, w_value.T
    where = yi.reshape(1).astype(jnp.int32)

    def call(kernel, outs, ins, scalar=False, scratch=(), work=2):
        shapes = [jax.ShapeDtypeStruct(shape, kind) for shape, kind in outs]
        specs = [SMEM] * scalar + [VMEM] * (len(ins) - scalar)
        return pl.pallas_call(
            kernel,
            out_shape=shapes,
            in_specs=specs,
            out_specs=[VMEM] * len(outs),
            scratch_shapes=scratch,
            compiler_params=pltpu.CompilerParams(vmem_limit_bytes=24 * 1024 * 1024),
            cost_estimate=pl.CostEstimate(
                flops=int(work * 1e9), bytes_accessed=0, transcendentals=0
            ),
        )(*ins)

    hbm = pl.BlockSpec(memory_space=pl.ANY)
    weights = [pltpu.VMEM((width, model), BF)] * 4
    rows0, kv = pl.pallas_call(
        project_kernel,
        out_shape=[
            jax.ShapeDtypeStruct((own, 2 * width), BF),
            jax.ShapeDtypeStruct((slab, 2 * width), BF),
        ],
        in_specs=[hbm] * 7,
        out_specs=[VMEM] * 2,
        scratch_shapes=[pltpu.VMEM((rows, model), BF) for rows in (own, own, slab)]
        + weights
        + [pltpu.SemaphoreType.DMA((12,))],
        compiler_params=pltpu.CompilerParams(vmem_limit_bytes=56 * 1024 * 1024),
    )(rows_in, rows_grad, frames, wq_t, w_out, wk_t, wv_t)

    kv_pair = flip(kv, "z", 8, 1)
    kv_core = swap(kv, "core")
    row_blocks = [rows0] + [flip(rows0, "z", 8, 2 * j) for j in (1, 2, 3)]

    def turn(stacked, other):
        place = jnp.arange(model, dtype=jnp.int32)
        unit, rest = place % inner, place // inner
        a_rel, b_rel = rest % 4, ((rest // 4) % 2) ^ other
        x_rel, c_rel = (rest // 8) % 4, rest // 32
        target = (
            (x_rel ^ xi) * 16 + ((2 * a_rel + b_rel) ^ zi) * 2 + (c_rel ^ ci)
        ) * inner + unit
        pick = (place[:, None] == target[None, :]).astype(BF)
        return mm(pick, stacked, (((0,), (1,)), ((), ()))).astype(BF)

    turned = turn(jnp.concatenate([frames, rows_in, rows_grad], axis=0), 0)
    for_pair = turn(frames, 1)
    row_blocks[1:], kv_pair, kv_core, for_pair, turned = lax.optimization_barrier(
        (row_blocks[1:], kv_pair, kv_core, for_pair, turned)
    )
    xt, xt_other = turned[: model // 2], swap(turned[model // 2 :], "core")
    frame_blocks = [kv, kv_core, kv_pair, swap(kv_pair, "core")]
    from_pair = flip(for_pair, "z", 8, 1)
    starts = [
        slab * (2 * (zi ^ db) + (ci ^ dc)) for db in (0, 1) for dc in (0, 1)
    ]
    valid = jnp.stack([frame_lengths[0] - s for s in starts]).astype(jnp.int32)

    (stats,) = call(
        functools.partial(stats_kernel, heads),
        [((16, 4 * own), F32)],
        (valid, *row_blocks, *frame_blocks),
        True,
        work=3,
    )
    all_stats = [stats] + [flip(stats, "z", 8, 2 * j) for j in (1, 2, 3)]

    all_stats[1:], from_pair, xt_other = lax.optimization_barrier(
        (all_stats[1:], from_pair, xt_other)
    )
    xp, xp_other = from_pair[: model // 2], swap(from_pair[model // 2 :], "core")

    dkv, dq0, *dq_sends = call(
        functools.partial(grads_kernel, heads),
        [((4 * slab, 2 * width), BF), ((own, 2 * width), F32)]
        + [((own, 2 * width), BF)] * 3,
        (valid, *row_blocks, *frame_blocks, *all_stats),
        True,
        work=8,
    )

    dkv_other = swap(dkv, "core")
    dq_recv = [flip(d, "z", 8, 2 * k) for k, d in zip((1, 2, 3), dq_sends)]

    part = model // 8
    kv_own, *kv_sends, near, pair = call(
        kv_weights_kernel,
        [((part, 2 * width), F32)]
        + [((part, 2 * width), BF)] * 3
        + [((slab, 2 * width), F32), ((slab, 2 * width), BF)],
        (xt, xt_other, xp, xp_other, dkv, dkv_other),
    )
    kv_x = [flip(kv_sends[k - 1], "dp", 4, k) for k in (2, 1, 3)]
    pair_recv = flip(pair, "z", 8, 1)

    dq_recv, kv_own = lax.optimization_barrier((dq_recv, kv_own))
    dqo = (dq0 + sum(d.astype(F32) for d in dq_recv)).astype(BF)
    dqo_other = swap(dqo, "core")
    qo_own, *qo_sends = call(
        qo_weights_kernel,
        [((part, 2 * width), F32)] + [((part, 2 * width), BF)] * 3,
        (xt, xt_other, dqo, dqo_other),
    )
    qo_x = [flip(qo_sends[k - 1], "dp", 4, k) for k in (2, 1, 3)]

    own_part, *sends = call(
        inputs_kernel,
        [((slab + own, width), F32)] + [((slab + own, width), BF)] * 3,
        (where, near, pair_recv, dqo, wk_t, wv_t, wq_t),
        True,
        [pltpu.VMEM((4, slab + own, width), F32)],
    )
    arrived = [flip(sends[k - 1], "head", 4, k) for k in (2, 1, 3)]
    inputs = (own_part + sum(p.astype(F32) for p in arrived)).astype(BF)
    dframes, dinput = inputs[:slab], inputs[slab:]

    kv_sum = kv_own + sum(k.astype(F32) for k in kv_x)
    qo_sum = qo_own + sum(k.astype(F32) for k in qo_x)
    total = jnp.concatenate([kv_sum, qo_sum], axis=1)
    cut = part // 2
    total = total[:cut] + flip(total[cut:].astype(BF), "z", 8, 1).astype(F32)
    low = total.astype(BF)
    over = [flip(low[k * inner : (k + 1) * inner], "z", 8, 2 * k) for k in (2, 1, 3)]
    total = total[:inner] + sum(p.astype(F32) for p in over)
    return (
        dinput[None],
        dframes[None],
        total[:, 2 * width : 3 * width],
        total[:, :width],
        total[:, width : 2 * width],
        total[:, 3 * width :].T,
    )


def solution(mesh):
    dp, tm, head = mesh.devices.shape
    fine = Mesh(mesh.devices.reshape(dp, tm // 2, 2, head), ("dp", "z", "core", "head"))
    tm = ("z", "core")
    placed = (
        P("dp", tm, None),
        P("dp", tm, None),
        P("dp", tm, None),
        P("dp"),
        P(None, "head"),
        P(None, "head"),
        P(None, "head"),
        P("head", None),
    )
    every = ("dp",) + tm
    return jax.shard_map(
        per_device,
        mesh=fine,
        in_specs=placed,
        out_specs=(
            P("dp", tm, "head"),
            P("dp", tm, "head"),
            P(every, "head"),
            P(every, "head"),
            P(every, "head"),
            P("head", every),
        ),
        check_vma=False,
    )
```

profile of v0, /device:TPU:8, one launch (start us, length us, event | category | flops | bytes accessed | tf_op | source)
XLA Modules:
  0.0 113.9 jit_solution(17006363321704766896)
XLA Ops:
  0.7 4.4 %shard_map.127 = (bf16[64,640]{1,0:T(8,128)(2,1)}, bf16[256,640]{1,0:T(8,128)(2,1)}) custom-call(bf16[64,1280]{1,0:T(8,128)(2,1)} %bitcast.34, bf16[64,1280]{1,0:T(8,128)(2,1)} %bitcast.32, bf16[256,1280]{1,0:T(8,128)(2,1)} %bitcast.30, bf16[320,1280]{1,0:T(8,128)(2,1)} %bitcast.24, bf16[320,1280]{1,0:T(8,128)(2,1)} %wo_ref.1, bf16[320,1280]{1,0:T(8,128)(2,1)} %bitcast.26, ...), custom_call_target="tpu_custom_call" | custom-call | tf_op jit(solution)/shard_map/pallas_call | solution.py:243
  5.0 6.4 %collective-permute-start.2 = (bf16[64,640]{1,0:T(8,128)(2,1)}, bf16[64,640]{1,0:T(8,128)(2,1)S(1)}, u32[]{:S(2)}, u32[]{:S(2)}) collective-permute-start(bf16[64,640]{1,0:T(8,128)(2,1)} %get-tuple-element.43.refs_0_), channel_id=1, source_target_pairs={{0,48},{8,56},{16,32},{24,40},{32,16},{40,24},{48,0},{56,8},{1,49}... | collective-permute-start | bytes 245768 | tf_op jit(solution)/shard_map/ppermute | solution.py:28
  11.4 1.0 collective-permute-start.1
  12.4 1.5 %collective-permute-start = (bf16[64,640]{1,0:T(8,128)(2,1)}, bf16[64,640]{1,0:T(8,128)(2,1)S(1)}, u32[]{:S(2)}, u32[]{:S(2)}) collective-permute-start(bf16[64,640]{1,0:T(8,128)(2,1)} %get-tuple-element.43.refs_0_), channel_id=1, source_target_pairs={{0,16},{8,24},{16,0},{24,8},{32,48},{40,56},{48,32},{56,40},{1,17}... | collective-permute-start | bytes 245768 | tf_op jit(solution)/shard_map/ppermute | solution.py:28
  13.9 1.0 collective-permute-start.3
  15.0 1.9 %fusion.8 = bf16[1280,384]{1,0:T(8,128)(2,1)S(1)} fusion(s32[1280]{0:T(1024)S(1)} %get-tuple-element.99, bf16[64,1280]{1,0:T(8,128)(2,1)S(1)} %bitcast.33, bf16[64,1280]{1,0:T(8,128)(2,1)S(1)} %bitcast.35, bf16[256,1280]{1,0:T(8,128)(2,1)S(1)} %bitcast.31), kind=kOutput, calls=%fused_computation.8 | convolution fusion | flops 1265008640 | bytes 1971200 | tf_op jit(solution)/shard_map/dot_general | solution.py:24
  16.9 1.9 %fusion.11 = bf16[1280,256]{1,0:T(8,128)(2,1)} fusion(s32[1280]{0:T(1024)S(1)} %get-tuple-element.100, bf16[1,256,1280]{2,1,0:T(8,128)(2,1)S(1)} %copy-done.11), kind=kOutput, calls=%fused_computation.9 | convolution fusion | flops 842465280 | bytes 1315840 | tf_op jit(solution)/shard_map/dot_general | solution.py:24
  18.8 3.9 %collective-permute-done.1.refs_2_ = bf16[64,640]{1,0:T(8,128)(2,1)S(1)} collective-permute-done((bf16[64,640]{1,0:T(8,128)(2,1)}, bf16[64,640]{1,0:T(8,128)(2,1)S(1)}, u32[]{:S(2)}, u32[]{:S(2)}) %collective-permute-start.1) | collective-permute-done | bytes 81952 | tf_op jit(solution)/shard_map/ppermute | solution.py:28
  22.8 4.5 %collective-permute-done.3.refs_6_ = bf16[256,640]{1,0:T(8,128)(2,1)S(1)} collective-permute-done((bf16[256,640]{1,0:T(8,128)(2,1)}, bf16[256,640]{1,0:T(8,128)(2,1)S(1)}, u32[]{:S(2)}, u32[]{:S(2)}) %collective-permute-start.3) | collective-permute-done | bytes 327712 | tf_op jit(solution)/shard_map/ppermute | solution.py:28
  27.3 1.2 %collective-permute-start.9 = (bf16[1280,256]{1,0:T(8,128)(2,1)}, bf16[1280,256]{1,0:T(8,128)(2,1)S(1)}, u32[]{:S(2)}, u32[]{:S(2)}) collective-permute-start(bf16[1280,256]{1,0:T(8,128)(2,1)} %fusion.11), channel_id=1, source_target_pairs={{0,8},{8,0},{16,24},{24,16},{32,40},{40,32},{48,56},{56,48},{1,9},... | collective-permute-start | bytes 1966088 | tf_op jit(solution)/shard_map/ppermute | solution.py:28
  28.6 0.9 fusion.46
  30.4 2.5 %shard_map.128.refs_8_ = f32[16,256]{1,0:T(8,128)S(1)} custom-call(s32[4]{0:T(128)S(1)} %pad_add_fusion.valid_ref, bf16[64,640]{1,0:T(8,128)(2,1)S(1)} %copy-done.4, bf16[64,640]{1,0:T(8,128)(2,1)S(1)} %collective-permute-done.refs_1_, bf16[64,640]{1,0:T(8,128)(2,1)S(1)} %collective-permute-done.1.refs_2_, ...), custom_call_target="tpu_custom_call" | custom-call | flops 3000000000 | tf_op jit(solution)/shard_map/pallas_call | solution.py:229
  33.0 2.9 %collective-permute-start.8 = (f32[16,256]{1,0:T(8,128)S(1)}, f32[16,256]{1,0:T(8,128)S(1)}, u32[]{:S(2)}, u32[]{:S(2)}) collective-permute-start(f32[16,256]{1,0:T(8,128)S(1)} %shard_map.128.refs_8_), channel_id=1, source_target_pairs={{0,48},{8,56},{16,32},{24,40},{32,16},{40,24},{48,0},{56,8},{1,49}... | collective-permute-start | bytes 49160 | tf_op jit(solution)/shard_map/ppermute | solution.py:28
  35.9 1.8 %collective-permute-start.7 = (f32[16,256]{1,0:T(8,128)S(1)}, f32[16,256]{1,0:T(8,128)S(1)}, u32[]{:S(2)}, u32[]{:S(2)}) collective-permute-start(f32[16,256]{1,0:T(8,128)S(1)} %shard_map.128.refs_8_), channel_id=1, source_target_pairs={{0,32},{8,40},{16,48},{24,56},{32,0},{40,8},{48,16},{56,24},{1,33}... | collective-permute-start | bytes 49160 | tf_op jit(solution)/shard_map/ppermute | solution.py:28
  37.7 1.8 %collective-permute-start.6 = (f32[16,256]{1,0:T(8,128)S(1)}, f32[16,256]{1,0:T(8,128)S(1)}, u32[]{:S(2)}, u32[]{:S(2)}) collective-permute-start(f32[16,256]{1,0:T(8,128)S(1)} %shard_map.128.refs_8_), channel_id=1, source_target_pairs={{0,16},{8,24},{16,0},{24,8},{32,48},{40,56},{48,32},{56,40},{1,17}... | collective-permute-start | bytes 49160 | tf_op jit(solution)/shard_map/ppermute | solution.py:28
  39.5 8.1 %collective-permute-done.8.refs_11_ = f32[16,256]{1,0:T(8,128)S(1)} collective-permute-done((f32[16,256]{1,0:T(8,128)S(1)}, f32[16,256]{1,0:T(8,128)S(1)}, u32[]{:S(2)}, u32[]{:S(2)}) %collective-permute-start.8) | collective-permute-done | bytes 16416 | tf_op jit(solution)/shard_map/ppermute | solution.py:28
  47.6 1.9 %collective-permute-done.7.refs_10_ = f32[16,256]{1,0:T(8,128)S(1)} collective-permute-done((f32[16,256]{1,0:T(8,128)S(1)}, f32[16,256]{1,0:T(8,128)S(1)}, u32[]{:S(2)}, u32[]{:S(2)}) %collective-permute-start.7) | collective-permute-done | bytes 16416 | tf_op jit(solution)/shard_map/ppermute | solution.py:28
  49.6 6.3 %shard_map.129 = (bf16[1024,640]{1,0:T(8,128)(2,1)S(1)}, f32[64,640]{1,0:T(8,128)S(1)}, bf16[64,640]{1,0:T(8,128)(2,1)S(1)}, bf16[64,640]{1,0:T(8,128)(2,1)S(1)}, bf16[64,640]{1,0:T(8,128)(2,1)S(1)}) custom-call(s32[4]{0:T(128)S(1)} %pad_add_fusion.valid_ref, bf16[64,640]{1,0:T(8,128)(2,1)S(1)} %copy-done.4, ...), custom_call_target="tpu_custom_call" | custom-call | flops 8000000000 | tf_op jit(solution)/shard_map/pallas_call | solution.py:229
  56.6 0.6 collective-permute-start.14
  57.2 2.5 %collective-permute-start.15 = (bf16[64,640]{1,0:T(8,128)(2,1)S(1)}, bf16[64,640]{1,0:T(8,128)(2,1)S(1)}, u32[]{:S(2)}, u32[]{:S(2)}) collective-permute-start(bf16[64,640]{1,0:T(8,128)(2,1)S(1)} %get-tuple-element.62), channel_id=1, source_target_pairs={{0,32},{8,40},{16,48},{24,56},{32,0},{40,8},{48,16},{56,24},{1,33}... | collective-permute-start | bytes 245768 | tf_op jit(solution)/shard_map/ppermute | solution.py:28
  59.7 3.4 %collective-permute-start.16 = (bf16[64,640]{1,0:T(8,128)(2,1)S(1)}, bf16[64,640]{1,0:T(8,128)(2,1)S(1)}, u32[]{:S(2)}, u32[]{:S(2)}) collective-permute-start(bf16[64,640]{1,0:T(8,128)(2,1)S(1)} %get-tuple-element.63), channel_id=1, source_target_pairs={{0,48},{8,56},{16,32},{24,40},{32,16},{40,24},{48,0},{56,8},{1,49}... | collective-permute-start | bytes 245768 | tf_op jit(solution)/shard_map/ppermute | solution.py:28
  63.1 1.3 %shard_map.130 = (f32[160,640]{1,0:T(8,128)S(1)}, bf16[160,640]{1,0:T(8,128)(2,1)S(1)}, bf16[160,640]{1,0:T(8,128)(2,1)S(1)}, bf16[160,640]{1,0:T(8,128)(2,1)S(1...) custom-call(bf16[640,384]{1,0:T(8,128)(2,1)S(1)} %get-tuple-element.89.xt_ref, ...), custom_call_target="tpu_custom_call" | custom-call | flops 2000000000 | tf_op jit(solution)/shard_map/pallas_call | solution.py:229
  64.5 0.7 collective-permute-done.14
  65.1 1.3 %collective-permute-done.15 = bf16[64,640]{1,0:T(8,128)(2,1)S(1)} collective-permute-done((bf16[64,640]{1,0:T(8,128)(2,1)S(1)}, bf16[64,640]{1,0:T(8,128)(2,1)S(1)}, u32[]{:S(2)}, u32[]{:S(2)}) %collective-permute-start.15) | collective-permute-done | bytes 81952 | tf_op jit(solution)/shard_map/ppermute | solution.py:28
  66.4 2.5 %collective-permute-done.16 = bf16[64,640]{1,0:T(8,128)(2,1)S(1)} collective-permute-done((bf16[64,640]{1,0:T(8,128)(2,1)S(1)}, bf16[64,640]{1,0:T(8,128)(2,1)S(1)}, u32[]{:S(2)}, u32[]{:S(2)}) %collective-permute-start.16) | collective-permute-done | bytes 81952 | tf_op jit(solution)/shard_map/ppermute | solution.py:28
  69.0 3.1 %collective-permute-start.20 = (bf16[160,640]{1,0:T(8,128)(2,1)S(1)}, bf16[160,640]{1,0:T(8,128)(2,1)S(1)}, u32[]{:S(2)}, u32[]{:S(2)}) collective-permute-start(bf16[160,640]{1,0:T(8,128)(2,1)S(1)} %get-tuple-element.73), channel_id=1, source_target_pairs={{0,128},{64,192},{128,0},{192,64},{1,129},{65,193},{129,1},{193,65... | collective-permute-start | bytes 614408 | tf_op jit(solution)/shard_map/ppermute | solution.py:28
  72.2 0.6 collective-permute-start.21
  73.3 2.3 %collective-permute-start.13 = (bf16[256,640]{1,0:T(8,128)(2,1)S(1)}, bf16[256,640]{1,0:T(8,128)(2,1)S(1)}, u32[]{:S(2)}, u32[]{:S(2)}) collective-permute-start(bf16[256,640]{1,0:T(8,128)(2,1)S(1)} %get-tuple-element.59), channel_id=1, source_target_pairs={{0,8},{8,0},{16,24},{24,16},{32,40},{40,32},{48,56},{56,48},{1,9},... | collective-permute-start | bytes 983048 | tf_op jit(solution)/shard_map/ppermute | solution.py:28
  75.6 0.8 shard_map.132
  76.4 3.0 %collective-permute-start.24 = (bf16[160,640]{1,0:T(8,128)(2,1)S(1)}, bf16[160,640]{1,0:T(8,128)(2,1)S(1)}, u32[]{:S(2)}, u32[]{:S(2)}) collective-permute-start(bf16[160,640]{1,0:T(8,128)(2,1)S(1)} %get-tuple-element.77), channel_id=1, source_target_pairs={{0,128},{64,192},{128,0},{192,64},{1,129},{65,193},{129,1},{193,65... | collective-permute-start | bytes 614408 | tf_op jit(solution)/shard_map/ppermute | solution.py:28
  79.4 0.6 collective-permute-start.25
  80.1 3.0 %collective-permute-done.21 = bf16[160,640]{1,0:T(8,128)(2,1)S(1)} collective-permute-done((bf16[160,640]{1,0:T(8,128)(2,1)S(1)}, bf16[160,640]{1,0:T(8,128)(2,1)S(1)}, u32[]{:S(2)}, u32[]{:S(2)}) %collective-permute-start.21) | collective-permute-done | bytes 204832 | tf_op jit(solution)/shard_map/ppermute | solution.py:28
  83.6 3.7 %collective-permute-done.24 = bf16[160,640]{1,0:T(8,128)(2,1)S(1)} collective-permute-done((bf16[160,640]{1,0:T(8,128)(2,1)S(1)}, bf16[160,640]{1,0:T(8,128)(2,1)S(1)}, u32[]{:S(2)}, u32[]{:S(2)}) %collective-permute-start.24) | collective-permute-done | bytes 204832 | tf_op jit(solution)/shard_map/ppermute | solution.py:28
  87.3 4.1 %collective-permute-done.25 = bf16[160,640]{1,0:T(8,128)(2,1)S(1)} collective-permute-done((bf16[160,640]{1,0:T(8,128)(2,1)S(1)}, bf16[160,640]{1,0:T(8,128)(2,1)S(1)}, u32[]{:S(2)}, u32[]{:S(2)}) %collective-permute-start.25) | collective-permute-done | bytes 204832 | tf_op jit(solution)/shard_map/ppermute | solution.py:28
  91.5 0.8 fusion.21
  92.3 2.3 %collective-permute-start.27 = (bf16[80,1280]{1,0:T(8,128)(2,1)}, bf16[80,1280]{1,0:T(8,128)(2,1)S(1)}, u32[]{:S(2)}, u32[]{:S(2)}) collective-permute-start(bf16[80,1280]{1,0:T(8,128)(2,1)} %fusion.21), channel_id=1, source_target_pairs={{0,8},{8,0},{16,24},{24,16},{32,40},{40,32},{48,56},{56,48},{1,9},... | collective-permute-start | bytes 614408 | tf_op jit(solution)/shard_map/ppermute | solution.py:28
  94.7 1.1 copy-done.6
  95.7 1.4 %shard_map.131 = (f32[320,320]{1,0:T(8,128)S(1)}, bf16[320,320]{1,0:T(8,128)(2,1)S(1)}, bf16[320,320]{1,0:T(8,128)(2,1)S(1)}, bf16[320,320]{1,0:T(8,128)(2,1)S(1)}) custom-call(s32[1]{0:T(128)} %bitcast.where_ref, f32[256,640]{1,0:T(8,128)S(1)} %copy-done.6, bf16[256,640]{1,0:T(8,128)(2,1)S(1)} %collective-permute-done.13.pair_ref, ...), custom_call_target="tpu_custom_call" | custom-call | flops 2000000000 | tf_op jit(solution)/shard_map/pallas_call | solution.py:229
  97.2 2.4 %collective-permute-start.17 = (bf16[320,320]{1,0:T(8,128)(2,1)S(1)}, bf16[320,320]{1,0:T(8,128)(2,1)S(1)}, u32[]{:S(2)}, u32[]{:S(2)}) collective-permute-start(bf16[320,320]{1,0:T(8,128)(2,1)S(1)} %get-tuple-element.69), channel_id=1, source_target_pairs={{0,2},{1,3},{2,0},{3,1},{4,6},{5,7},{6,4},{7,5},{8,10},{9,11},{10,... | collective-permute-start | bytes 614408 | tf_op jit(solution)/shard_map/ppermute | solution.py:28
  99.5 1.3 %collective-permute-start.18 = (bf16[320,320]{1,0:T(8,128)(2,1)S(1)}, bf16[320,320]{1,0:T(8,128)(2,1)S(1)}, u32[]{:S(2)}, u32[]{:S(2)}) collective-permute-start(bf16[320,320]{1,0:T(8,128)(2,1)S(1)} %get-tuple-element.70), channel_id=1, source_target_pairs={{0,1},{1,0},{2,3},{3,2},{4,5},{5,4},{6,7},{7,6},{8,9},{9,8},{10,11... | collective-permute-start | bytes 614408 | tf_op jit(solution)/shard_map/ppermute | solution.py:28
  101.5 3.0 %collective-permute-start.28 = (bf16[20,1280]{1,0:T(8,128)(2,1)S(1)}, bf16[20,1280]{1,0:T(8,128)(2,1)S(1)}, u32[]{:S(2)}, u32[]{:S(2)}) collective-permute-start(bf16[20,1280]{1,0:T(8,128)(2,1)S(1)} %get-tuple-element.92), channel_id=1, source_target_pairs={{0,32},{8,40},{16,48},{24,56},{32,0},{40,8},{48,16},{56,24},{1,33}... | collective-permute-start | bytes 153608 | tf_op jit(solution)/shard_map/ppermute | solution.py:28
  104.4 1.6 %collective-permute-start.30 = (bf16[20,1280]{1,0:T(8,128)(2,1)S(1)}, bf16[20,1280]{1,0:T(8,128)(2,1)S(1)}, u32[]{:S(2)}, u32[]{:S(2)}) collective-permute-start(bf16[20,1280]{1,0:T(8,128)(2,1)S(1)} %get-tuple-element.93), channel_id=1, source_target_pairs={{0,48},{8,56},{16,32},{24,40},{32,16},{40,24},{48,0},{56,8},{1,49}... | collective-permute-start | bytes 153608 | tf_op jit(solution)/shard_map/ppermute | solution.py:28
  106.0 1.7 %collective-permute-done.17 = bf16[320,320]{1,0:T(8,128)(2,1)S(1)} collective-permute-done((bf16[320,320]{1,0:T(8,128)(2,1)S(1)}, bf16[320,320]{1,0:T(8,128)(2,1)S(1)}, u32[]{:S(2)}, u32[]{:S(2)}) %collective-permute-start.17) | collective-permute-done | bytes 204832 | tf_op jit(solution)/shard_map/ppermute | solution.py:28
  107.7 0.8 collective-permute-start.29
  108.5 2.9 %collective-permute-done.18 = bf16[320,320]{1,0:T(8,128)(2,1)S(1)} collective-permute-done((bf16[320,320]{1,0:T(8,128)(2,1)S(1)}, bf16[320,320]{1,0:T(8,128)(2,1)S(1)}, u32[]{:S(2)}, u32[]{:S(2)}) %collective-permute-start.18) | collective-permute-done | bytes 204832 | tf_op jit(solution)/shard_map/ppermute | solution.py:28
  111.6 0.6 slice_bitcast_fusion.1
  112.2 0.8 copy.14
  113.2 0.7 slice_bitcast_fusion.2
  (66 shorter events, 3.4 us)
Async XLA Ops:
  0.6 14.3 %copy-start.11 = (bf16[1,256,1280]{2,1,0:T(8,128)(2,1)S(1)}, bf16[1,256,1280]{2,1,0:T(8,128)(2,1)}, u32[]{:S(2)}) copy-start(bf16[1,256,1280]{2,1,0:T(8,128)(2,1)} %param.10) | copy-start | bytes 1966084
  0.6 14.3 %copy-start.12 = (bf16[1,64,1280]{2,1,0:T(8,128)(2,1)S(1)}, bf16[1,64,1280]{2,1,0:T(8,128)(2,1)}, u32[]{:S(2)}) copy-start(bf16[1,64,1280]{2,1,0:T(8,128)(2,1)} %param.9) | copy-start | bytes 491524
  0.7 14.3 %copy-start.13 = (bf16[1,64,1280]{2,1,0:T(8,128)(2,1)S(1)}, bf16[1,64,1280]{2,1,0:T(8,128)(2,1)}, u32[]{:S(2)}) copy-start(bf16[1,64,1280]{2,1,0:T(8,128)(2,1)} %param.8) | copy-start | bytes 491524
  5.0 13.8 %collective-permute-start.2 = (bf16[64,640]{1,0:T(8,128)(2,1)}, bf16[64,640]{1,0:T(8,128)(2,1)S(1)}, u32[]{:S(2)}, u32[]{:S(2)}) collective-permute-start(bf16[64,640]{1,0:T(8,128)(2,1)} %get-tuple-element.43.refs_0_), channel_id=1, source_target_pairs={{0,48},{8,56},{16,32},{24,40},{32,16},{40,24},{48,0},{56,8},{1,49}... | collective-permute-start | bytes 245768 | tf_op jit(solution)/shard_map/ppermute | solution.py:28
  11.4 11.4 %collective-permute-start.1 = (bf16[64,640]{1,0:T(8,128)(2,1)}, bf16[64,640]{1,0:T(8,128)(2,1)S(1)}, u32[]{:S(2)}, u32[]{:S(2)}) collective-permute-start(bf16[64,640]{1,0:T(8,128)(2,1)} %get-tuple-element.43.refs_0_), channel_id=1, source_target_pairs={{0,32},{8,40},{16,48},{24,56},{32,0},{40,8},{48,16},{56,24},{1,33}... | collective-permute-start | bytes 245768 | tf_op jit(solution)/shard_map/ppermute | solution.py:28
  12.4 10.4 %collective-permute-start = (bf16[64,640]{1,0:T(8,128)(2,1)}, bf16[64,640]{1,0:T(8,128)(2,1)S(1)}, u32[]{:S(2)}, u32[]{:S(2)}) collective-permute-start(bf16[64,640]{1,0:T(8,128)(2,1)} %get-tuple-element.43.refs_0_), channel_id=1, source_target_pairs={{0,16},{8,24},{16,0},{24,8},{32,48},{40,56},{48,32},{56,40},{1,17}... | collective-permute-start | bytes 245768 | tf_op jit(solution)/shard_map/ppermute | solution.py:28
  13.9 8.9 %collective-permute-start.4 = (bf16[256,640]{1,0:T(8,128)(2,1)}, bf16[256,640]{1,0:T(8,128)(2,1)S(1)}, u32[]{:S(2)}, u32[]{:S(2)}) collective-permute-start(bf16[256,640]{1,0:T(8,128)(2,1)} %get-tuple-element.44.refs_4_), channel_id=1, source_target_pairs={{0,4},{4,0},{1,5},{5,1},{2,6},{6,2},{3,7},{7,3},{8,12},{12,8},{9,1... | collective-permute-start | bytes 983048 | tf_op jit(solution)/shard_map/ppermute | solution.py:28
  13.9 13.5 %collective-permute-start.3 = (bf16[256,640]{1,0:T(8,128)(2,1)}, bf16[256,640]{1,0:T(8,128)(2,1)S(1)}, u32[]{:S(2)}, u32[]{:S(2)}) collective-permute-start(bf16[256,640]{1,0:T(8,128)(2,1)} %get-tuple-element.44.refs_4_), channel_id=1, source_target_pairs={{0,8},{8,0},{16,24},{24,16},{32,40},{40,32},{48,56},{56,48},{1,9},... | collective-permute-start | bytes 983048 | tf_op jit(solution)/shard_map/ppermute | solution.py:28
  18.8 11.6 %copy-start.3 = (bf16[256,640]{1,0:T(8,128)(2,1)S(1)}, bf16[256,640]{1,0:T(8,128)(2,1)}, u32[]{:S(2)}) copy-start(bf16[256,640]{1,0:T(8,128)(2,1)} %get-tuple-element.44.refs_4_) | copy-start | bytes 983044
  18.8 11.6 %copy-start.4 = (bf16[64,640]{1,0:T(8,128)(2,1)S(1)}, bf16[64,640]{1,0:T(8,128)(2,1)}, u32[]{:S(2)}) copy-start(bf16[64,640]{1,0:T(8,128)(2,1)} %get-tuple-element.43.refs_0_) | copy-start | bytes 245764
  27.3 3.1 %collective-permute-start.5 = (bf16[256,640]{1,0:T(8,128)(2,1)S(1)}, bf16[256,640]{1,0:T(8,128)(2,1)S(1)}, u32[]{:S(2)}, u32[]{:S(2)}) collective-permute-start(bf16[256,640]{1,0:T(8,128)(2,1)S(1)} %collective-permute-done.3.refs_6_), channel_id=1, source_target_pairs={{0,4},{4,0},{1,5},{5,1},{2,6},{6,2},{3,7},{7,3},{8,12},{12,8},{9,1... | collective-permute-start | bytes 983048 | tf_op jit(solution)/shard_map/ppermute | solution.py:28
  27.3 22.2 %collective-permute-start.9 = (bf16[1280,256]{1,0:T(8,128)(2,1)}, bf16[1280,256]{1,0:T(8,128)(2,1)S(1)}, u32[]{:S(2)}, u32[]{:S(2)}) collective-permute-start(bf16[1280,256]{1,0:T(8,128)(2,1)} %fusion.11), channel_id=1, source_target_pairs={{0,8},{8,0},{16,24},{24,16},{32,40},{40,32},{48,56},{56,48},{1,9},... | collective-permute-start | bytes 1966088 | tf_op jit(solution)/shard_map/ppermute | solution.py:28
  29.5 20.1 %collective-permute-start.10 = (bf16[640,384]{1,0:T(8,128)(2,1)}, bf16[640,384]{1,0:T(8,128)(2,1)S(1)}, u32[]{:S(2)}, u32[]{:S(2)}) collective-permute-start(bf16[640,384]{1,0:T(8,128)(2,1)} %get-tuple-element.88), channel_id=1, source_target_pairs={{0,4},{4,0},{1,5},{5,1},{2,6},{6,2},{3,7},{7,3},{8,12},{12,8},{9,1... | collective-permute-start | bytes 1474568 | tf_op jit(solution)/shard_map/ppermute | solution.py:28
  33.0 14.7 %collective-permute-start.8 = (f32[16,256]{1,0:T(8,128)S(1)}, f32[16,256]{1,0:T(8,128)S(1)}, u32[]{:S(2)}, u32[]{:S(2)}) collective-permute-start(f32[16,256]{1,0:T(8,128)S(1)} %shard_map.128.refs_8_), channel_id=1, source_target_pairs={{0,48},{8,56},{16,32},{24,40},{32,16},{40,24},{48,0},{56,8},{1,49}... | collective-permute-start | bytes 49160 | tf_op jit(solution)/shard_map/ppermute | solution.py:28
  35.9 13.7 %collective-permute-start.7 = (f32[16,256]{1,0:T(8,128)S(1)}, f32[16,256]{1,0:T(8,128)S(1)}, u32[]{:S(2)}, u32[]{:S(2)}) collective-permute-start(f32[16,256]{1,0:T(8,128)S(1)} %shard_map.128.refs_8_), channel_id=1, source_target_pairs={{0,32},{8,40},{16,48},{24,56},{32,0},{40,8},{48,16},{56,24},{1,33}... | collective-permute-start | bytes 49160 | tf_op jit(solution)/shard_map/ppermute | solution.py:28
  37.7 11.9 %collective-permute-start.6 = (f32[16,256]{1,0:T(8,128)S(1)}, f32[16,256]{1,0:T(8,128)S(1)}, u32[]{:S(2)}, u32[]{:S(2)}) collective-permute-start(f32[16,256]{1,0:T(8,128)S(1)} %shard_map.128.refs_8_), channel_id=1, source_target_pairs={{0,16},{8,24},{16,0},{24,8},{32,48},{40,56},{48,32},{56,40},{1,17}... | collective-permute-start | bytes 49160 | tf_op jit(solution)/shard_map/ppermute | solution.py:28
  55.9 7.2 %collective-permute-start.12 = (bf16[1024,640]{1,0:T(8,128)(2,1)S(1)}, bf16[1024,640]{1,0:T(8,128)(2,1)S(1)}, u32[]{:S(2)}, u32[]{:S(2)}) collective-permute-start(bf16[1024,640]{1,0:T(8,128)(2,1)S(1)} %get-tuple-element.57.y_ref), channel_id=1, source_target_pairs={{0,4},{4,0},{1,5},{5,1},{2,6},{6,2},{3,7},{7,3},{8,12},{12,8},{9,1... | collective-permute-start | bytes 3932168 | tf_op jit(solution)/shard_map/ppermute | solution.py:28
  56.1 7.1 %collective-permute-start.11 = (bf16[640,256]{1,0:T(8,128)(2,1)S(1)}, bf16[640,256]{1,0:T(8,128)(2,1)S(1)}, u32[]{:S(2)}, u32[]{:S(2)}) collective-permute-start(bf16[640,256]{1,0:T(8,128)(2,1)S(1)} %get-tuple-element.90), channel_id=1, source_target_pairs={{0,4},{4,0},{1,5},{5,1},{2,6},{6,2},{3,7},{7,3},{8,12},{12,8},{9,1... | collective-permute-start | bytes 983048 | tf_op jit(solution)/shard_map/ppermute | solution.py:28
  56.6 8.5 %collective-permute-start.14 = (bf16[64,640]{1,0:T(8,128)(2,1)S(1)}, bf16[64,640]{1,0:T(8,128)(2,1)S(1)}, u32[]{:S(2)}, u32[]{:S(2)}) collective-permute-start(bf16[64,640]{1,0:T(8,128)(2,1)S(1)} %get-tuple-element.61), channel_id=1, source_target_pairs={{0,16},{8,24},{16,0},{24,8},{32,48},{40,56},{48,32},{56,40},{1,17}... | collective-permute-start | bytes 245768 | tf_op jit(solution)/shard_map/ppermute | solution.py:28
  57.2 9.2 %collective-permute-start.15 = (bf16[64,640]{1,0:T(8,128)(2,1)S(1)}, bf16[64,640]{1,0:T(8,128)(2,1)S(1)}, u32[]{:S(2)}, u32[]{:S(2)}) collective-permute-start(bf16[64,640]{1,0:T(8,128)(2,1)S(1)} %get-tuple-element.62), channel_id=1, source_target_pairs={{0,32},{8,40},{16,48},{24,56},{32,0},{40,8},{48,16},{56,24},{1,33}... | collective-permute-start | bytes 245768 | tf_op jit(solution)/shard_map/ppermute | solution.py:28
  59.7 9.2 %collective-permute-start.16 = (bf16[64,640]{1,0:T(8,128)(2,1)S(1)}, bf16[64,640]{1,0:T(8,128)(2,1)S(1)}, u32[]{:S(2)}, u32[]{:S(2)}) collective-permute-start(bf16[64,640]{1,0:T(8,128)(2,1)S(1)} %get-tuple-element.63), channel_id=1, source_target_pairs={{0,48},{8,56},{16,32},{24,40},{32,16},{40,24},{48,0},{56,8},{1,49}... | collective-permute-start | bytes 245768 | tf_op jit(solution)/shard_map/ppermute | solution.py:28
  64.5 11.9 %copy-start.5 = (f32[256,640]{1,0:T(8,128)}, f32[256,640]{1,0:T(8,128)S(1)}, u32[]{:S(2)}) copy-start(f32[256,640]{1,0:T(8,128)S(1)} %get-tuple-element.58.near_ref) | copy-start | bytes 1966084
  68.9 6.7 %collective-permute-start.23 = (bf16[64,640]{1,0:T(8,128)(2,1)S(1)}, bf16[64,640]{1,0:T(8,128)(2,1)S(1)}, u32[]{:S(2)}, u32[]{:S(2)}) collective-permute-start(bf16[64,640]{1,0:T(8,128)(2,1)S(1)} %add_convert_fusion.1.dq_ref.y_ref), channel_id=1, source_target_pairs={{0,4},{4,0},{1,5},{5,1},{2,6},{6,2},{3,7},{7,3},{8,12},{12,8},{9,1... | collective-permute-start | bytes 245768 | tf_op jit(solution)/shard_map/ppermute | solution.py:28
  69.0 10.4 %collective-permute-start.20 = (bf16[160,640]{1,0:T(8,128)(2,1)S(1)}, bf16[160,640]{1,0:T(8,128)(2,1)S(1)}, u32[]{:S(2)}, u32[]{:S(2)}) collective-permute-start(bf16[160,640]{1,0:T(8,128)(2,1)S(1)} %get-tuple-element.73), channel_id=1, source_target_pairs={{0,128},{64,192},{128,0},{192,64},{1,129},{65,193},{129,1},{193,65... | collective-permute-start | bytes 614408 | tf_op jit(solution)/shard_map/ppermute | solution.py:28
  72.2 10.9 %collective-permute-start.21 = (bf16[160,640]{1,0:T(8,128)(2,1)S(1)}, bf16[160,640]{1,0:T(8,128)(2,1)S(1)}, u32[]{:S(2)}, u32[]{:S(2)}) collective-permute-start(bf16[160,640]{1,0:T(8,128)(2,1)S(1)} %get-tuple-element.74), channel_id=1, source_target_pairs={{0,64},{64,0},{128,192},{192,128},{1,65},{65,1},{129,193},{193,129... | collective-permute-start | bytes 614408 | tf_op jit(solution)/shard_map/ppermute | solution.py:28
  72.7 10.7 %collective-permute-start.22 = (bf16[160,640]{1,0:T(8,128)(2,1)S(1)}, bf16[160,640]{1,0:T(8,128)(2,1)S(1)}, u32[]{:S(2)}, u32[]{:S(2)}) collective-permute-start(bf16[160,640]{1,0:T(8,128)(2,1)S(1)} %get-tuple-element.75), channel_id=1, source_target_pairs={{0,192},{64,128},{128,64},{192,0},{1,193},{65,129},{129,65},{193,1... | collective-permute-start | bytes 614408 | tf_op jit(solution)/shard_map/ppermute | solution.py:28
  73.3 21.3 %collective-permute-start.13 = (bf16[256,640]{1,0:T(8,128)(2,1)S(1)}, bf16[256,640]{1,0:T(8,128)(2,1)S(1)}, u32[]{:S(2)}, u32[]{:S(2)}) collective-permute-start(bf16[256,640]{1,0:T(8,128)(2,1)S(1)} %get-tuple-element.59), channel_id=1, source_target_pairs={{0,8},{8,0},{16,24},{24,16},{32,40},{40,32},{48,56},{56,48},{1,9},... | collective-permute-start | bytes 983048 | tf_op jit(solution)/shard_map/ppermute | solution.py:28
  76.4 10.9 %collective-permute-start.24 = (bf16[160,640]{1,0:T(8,128)(2,1)S(1)}, bf16[160,640]{1,0:T(8,128)(2,1)S(1)}, u32[]{:S(2)}, u32[]{:S(2)}) collective-permute-start(bf16[160,640]{1,0:T(8,128)(2,1)S(1)} %get-tuple-element.77), channel_id=1, source_target_pairs={{0,128},{64,192},{128,0},{192,64},{1,129},{65,193},{129,1},{193,65... | collective-permute-start | bytes 614408 | tf_op jit(solution)/shard_map/ppermute | solution.py:28
  79.4 12.0 %collective-permute-start.25 = (bf16[160,640]{1,0:T(8,128)(2,1)S(1)}, bf16[160,640]{1,0:T(8,128)(2,1)S(1)}, u32[]{:S(2)}, u32[]{:S(2)}) collective-permute-start(bf16[160,640]{1,0:T(8,128)(2,1)S(1)} %get-tuple-element.78), channel_id=1, source_target_pairs={{0,64},{64,0},{128,192},{192,128},{1,65},{65,1},{129,193},{193,129... | collective-permute-start | bytes 614408 | tf_op jit(solution)/shard_map/ppermute | solution.py:28
  83.0 8.4 %collective-permute-start.26 = (bf16[160,640]{1,0:T(8,128)(2,1)S(1)}, bf16[160,640]{1,0:T(8,128)(2,1)S(1)}, u32[]{:S(2)}, u32[]{:S(2)}) collective-permute-start(bf16[160,640]{1,0:T(8,128)(2,1)S(1)} %get-tuple-element.79), channel_id=1, source_target_pairs={{0,192},{64,128},{128,64},{192,0},{1,193},{65,129},{129,65},{193,1... | collective-permute-start | bytes 614408 | tf_op jit(solution)/shard_map/ppermute | solution.py:28
  83.6 7.9 %copy-start.7 = (f32[160,640]{1,0:T(8,128)}, f32[160,640]{1,0:T(8,128)S(1)}, u32[]{:S(2)}) copy-start(f32[160,640]{1,0:T(8,128)S(1)} %add_add_fusion.1) | copy-start | bytes 1228804
  83.6 11.1 %copy-start = (bf16[1280,320]{0,1:T(8,128)(2,1)S(1)}, bf16[1280,320]{0,1:T(8,128)(2,1)}, u32[]{:S(2)}) copy-start(bf16[1280,320]{0,1:T(8,128)(2,1)} %param.12) | copy-start | bytes 2457604
  83.6 11.0 %copy-start.1 = (bf16[1280,320]{0,1:T(8,128)(2,1)S(1)}, bf16[1280,320]{0,1:T(8,128)(2,1)}, u32[]{:S(2)}) copy-start(bf16[1280,320]{0,1:T(8,128)(2,1)} %param.13) | copy-start | bytes 2457604
  83.6 11.0 %copy-start.2 = (bf16[1280,320]{0,1:T(8,128)(2,1)S(1)}, bf16[1280,320]{0,1:T(8,128)(2,1)}, u32[]{:S(2)}) copy-start(bf16[1280,320]{0,1:T(8,128)(2,1)} %param.14) | copy-start | bytes 2457604
  91.5 0.8 copy-start.9
  92.3 9.0 %collective-permute-start.27 = (bf16[80,1280]{1,0:T(8,128)(2,1)}, bf16[80,1280]{1,0:T(8,128)(2,1)S(1)}, u32[]{:S(2)}, u32[]{:S(2)}) collective-permute-start(bf16[80,1280]{1,0:T(8,128)(2,1)} %fusion.21), channel_id=1, source_target_pairs={{0,8},{8,0},{16,24},{24,16},{32,40},{40,32},{48,56},{56,48},{1,9},... | collective-permute-start | bytes 614408 | tf_op jit(solution)/shard_map/ppermute | solution.py:28
  94.6 1.1 copy-start.6
  95.7 5.6 %copy-start.8 = (f32[160,640]{1,0:T(8,128)S(1)}, f32[160,640]{1,0:T(8,128)}, u32[]{:S(2)}) copy-start(f32[160,640]{1,0:T(8,128)} %copy-done.7) | copy-start | bytes 1228804
  95.7 5.6 %copy-start.10 = (f32[160,640]{1,0:T(8,128)S(1)}, f32[160,640]{1,0:T(8,128)}, u32[]{:S(2)}) copy-start(f32[160,640]{1,0:T(8,128)} %copy-done.9) | copy-start | bytes 1228804
  97.2 10.5 %collective-permute-start.17 = (bf16[320,320]{1,0:T(8,128)(2,1)S(1)}, bf16[320,320]{1,0:T(8,128)(2,1)S(1)}, u32[]{:S(2)}, u32[]{:S(2)}) collective-permute-start(bf16[320,320]{1,0:T(8,128)(2,1)S(1)} %get-tuple-element.69), channel_id=1, source_target_pairs={{0,2},{1,3},{2,0},{3,1},{4,6},{5,7},{6,4},{7,5},{8,10},{9,11},{10,... | collective-permute-start | bytes 614408 | tf_op jit(solution)/shard_map/ppermute | solution.py:28
  99.5 11.9 %collective-permute-start.18 = (bf16[320,320]{1,0:T(8,128)(2,1)S(1)}, bf16[320,320]{1,0:T(8,128)(2,1)S(1)}, u32[]{:S(2)}, u32[]{:S(2)}) collective-permute-start(bf16[320,320]{1,0:T(8,128)(2,1)S(1)} %get-tuple-element.70), channel_id=1, source_target_pairs={{0,1},{1,0},{2,3},{3,2},{4,5},{5,4},{6,7},{7,6},{8,9},{9,8},{10,11... | collective-permute-start | bytes 614408 | tf_op jit(solution)/shard_map/ppermute | solution.py:28
  100.9 10.5 %collective-permute-start.19 = (bf16[320,320]{1,0:T(8,128)(2,1)S(1)}, bf16[320,320]{1,0:T(8,128)(2,1)S(1)}, u32[]{:S(2)}, u32[]{:S(2)}) collective-permute-start(bf16[320,320]{1,0:T(8,128)(2,1)S(1)} %get-tuple-element.71), channel_id=1, source_target_pairs={{0,3},{1,2},{2,1},{3,0},{4,7},{5,6},{6,5},{7,4},{8,11},{9,10},{10,... | collective-permute-start | bytes 614408 | tf_op jit(solution)/shard_map/ppermute | solution.py:28
  101.5 11.5 %collective-permute-start.28 = (bf16[20,1280]{1,0:T(8,128)(2,1)S(1)}, bf16[20,1280]{1,0:T(8,128)(2,1)S(1)}, u32[]{:S(2)}, u32[]{:S(2)}) collective-permute-start(bf16[20,1280]{1,0:T(8,128)(2,1)S(1)} %get-tuple-element.92), channel_id=1, source_target_pairs={{0,32},{8,40},{16,48},{24,56},{32,0},{40,8},{48,16},{56,24},{1,33}... | collective-permute-start | bytes 153608 | tf_op jit(solution)/shard_map/ppermute | solution.py:28
  104.4 8.6 %collective-permute-start.30 = (bf16[20,1280]{1,0:T(8,128)(2,1)S(1)}, bf16[20,1280]{1,0:T(8,128)(2,1)S(1)}, u32[]{:S(2)}, u32[]{:S(2)}) collective-permute-start(bf16[20,1280]{1,0:T(8,128)(2,1)S(1)} %get-tuple-element.93), channel_id=1, source_target_pairs={{0,48},{8,56},{16,32},{24,40},{32,16},{40,24},{48,0},{56,8},{1,49}... | collective-permute-start | bytes 153608 | tf_op jit(solution)/shard_map/ppermute | solution.py:28
  107.7 5.5 %collective-permute-start.29 = (bf16[20,1280]{1,0:T(8,128)(2,1)S(1)}, bf16[20,1280]{1,0:T(8,128)(2,1)S(1)}, u32[]{:S(2)}, u32[]{:S(2)}) collective-permute-start(bf16[20,1280]{1,0:T(8,128)(2,1)S(1)} %get-tuple-element.94), channel_id=1, source_target_pairs={{0,16},{8,24},{16,0},{24,8},{32,48},{40,56},{48,32},{56,40},{1,17}... | collective-permute-start | bytes 153608 | tf_op jit(solution)/shard_map/ppermute | solution.py:28
where the time goes:
time: 114 us
  starting transfers between devices  47.7 us (42%)
  waiting for transfers between devices  38.4 us (34%)
  Pallas kernels  16.7 us (15%)
  local copies, waits for them, and re-layouts  4.33 us (4%)
  matrix products  3.87 us (3%)
  between operations  1.58 us (1%)
  other arithmetic  1.33 us (1%)
    ppermute x31, starting transfers between devices, flip(): return lax.ppermute(x, axis, [(i, i ^ bits) for i in range(size)])  47.7 us
    ppermute x31, waiting for transfers between devices, flip(): return lax.ppermute(x, axis, [(i, i ^ bits) for i in range(size)])  38.4 us
    pallas_call x5, Pallas kernels, call(): pl.pallas_call(kernel, out_shape=shapes, in_specs=specs, out_specs=[VMEM]...  12.3 us
    pallas_call x1, Pallas kernels, per_device(): pl.pallas_call(project_kernel, out_shape=[jax.ShapeDtypeStruct((own, 2 *...  4.35 us
    dot_general x2, matrix products, mm(): return lax.dot_general(left, right, dims, preferred_element_type=F32)  3.87 us
  transfers between devices with their start and end apart: 31, of which 13 were waited for; matrix products, arithmetic and copies ran while one was open for 7% of the time, Pallas kernels for 5%

commit v1 on v0

--- a/solution.py
+++ b/solution.py
@@ -37,11 +37,16 @@
     return jnp.where(positions < valid_ref[block], 0.0, LOW)
 
 
+def frame_blocks(refs):
+    part = refs[0].shape[0] // 2
+    return [r[db * part : (db + 1) * part, :] for db in (0, 1) for r in refs]
+
+
 def stats_kernel(heads, valid_ref, *refs):
-    rows_refs, frame_refs, out_ref = refs[:4], refs[4:8], refs[8]
+    rows_refs, frame_refs, out_ref = refs[:4], refs[4:6], refs[6]
     width = heads * HD
     rows = jnp.concatenate([r[...] for r in rows_refs], axis=0)
-    blocks = [r[...] for r in frame_refs]
+    blocks = frame_blocks(frame_refs)
     biases = [frame_bias(valid_ref, j, b.shape[0]) for j, b in enumerate(blocks)]
     out_ref[...] = jnp.zeros_like(out_ref)
     for h in range(heads):
@@ -79,11 +84,11 @@
 
 
 def grads_kernel(heads, valid_ref, *refs):
-    rows_refs, frame_refs, stat_refs = refs[:4], refs[4:8], refs[8:12]
-    dkv_ref, dq_refs = refs[12], refs[13:17]
+    rows_refs, frame_refs, stat_refs = refs[:4], refs[4:6], refs[6:10]
+    dkv_ref, dq_refs = refs[10], refs[11:15]
     width = heads * HD
     rows = jnp.concatenate([r[...] for r in rows_refs], axis=0)
-    blocks = [r[...] for r in frame_refs]
+    blocks = frame_blocks(frame_refs)
     part = blocks[0].shape[0]
     own = rows_refs[0].shape[0]
     stats = [in_own_order(stat_refs[k][...], k, own) for k in range(4)]
@@ -135,8 +140,8 @@
 
 
 def project_kernel(
-    left_ref, right_ref, frames_ref, wq_ref, wo_ref, wk_ref, wv_ref, rows_ref, kv_ref,
-    left, right, frames, wq, wo, wk, wv, sems,
+    where_ref, left_ref, right_ref, frames_ref, wq_ref, wo_ref, wk_ref, wv_ref,
+    rows_ref, kv_ref, quarter_ref, left, right, frames, wq, wo, wk, wv, sems,
 ):
     width = wq.shape[0]
     half = width // 2
@@ -151,60 +156,70 @@
         if source is wo_ref:
             pairs.append((frames_ref, frames))
     copies = fetch(pairs, sems)
+    part = quarter_ref.shape[0]
     for i, (x, w, out, side) in enumerate(
         ((left, wq, rows_ref, 0), (right, wo, rows_ref, 1), (frames, wk, kv_ref, 0), (frames, wv, kv_ref, 1))
     ):
         for copy in copies[3 * i : 3 * i + 3]:
             copy.wait()
+        if i == 2:
+            start = pl.multiple_of(where_ref[0] * part, part)
+            quarter_ref[...] = frames[pl.ds(start, part), :]
         out[:, side * width : (side + 1) * width] = mm(x[...], w[...], NT).astype(BF)
 
 
-def kv_weights_kernel(xt_ref, xt2_ref, xp_ref, xp2_ref, y_ref, y2_ref, *out_refs):
-    part = y_ref.shape[0] // 4
-    step = out_refs[0].shape[0]
-    sums = []
-    for j in range(4):
-        near = slice(j * part, (j + 1) * part)
-        far = slice((j ^ 1) * part, ((j ^ 1) + 1) * part)
-        total = y_ref[near].astype(F32) + y2_ref[far].astype(F32)
-        if j == 0:
-            out_refs[4][...] = total
-        sums.append(total.astype(BF))
-    out_refs[5][...] = sums[2]
+def pair_kernel(
+    where_ref, e0_ref, e1_ref, e2_ref, e3_ref, w1_ref, w2_ref, kv_ref, both_ref, pair_ref
+):
+    part, width, slab = e0_ref.shape[0], w1_ref.shape[0], kv_ref.shape[0]
+    for k, e_ref in enumerate((e0_ref, e1_ref, e2_ref, e3_ref)):
+        start = pl.multiple_of((where_ref[0] ^ k) * part, part)
+        pair_ref[pl.ds(start, part), :] = e_ref[...]
+    both_ref[:slab, :] = kv_ref[...]
+    both_ref[slab:, :width] = mm(pair_ref[...], w1_ref[...], NT).astype(BF)
+    both_ref[slab:, width:] = mm(pair_ref[...], w2_ref[...], NT).astype(BF)
+
+
+def chip_sum(own_ref, other_ref, block, rows):
+    near = slice(block * rows, (block + 1) * rows)
+    far = slice((block ^ 1) * rows, ((block ^ 1) + 1) * rows)
+    return (own_ref[near].astype(F32) + other_ref[far].astype(F32)).astype(BF)
+
+
+def weights_kernel(xt_ref, xt2_ref, dkv_ref, dkv2_ref, dqo_ref, dqo2_ref, *out_refs):
+    kv_refs, keep_ref, send_ref = out_refs[:4], out_refs[4], out_refs[5]
+    slab, own = dkv_ref.shape[0] // 4, dqo_ref.shape[0]
+    half = dqo_ref.shape[1] // 2
+    step = kv_refs[0].shape[0]
+    sums = [chip_sum(dkv_ref, dkv2_ref, j, slab) for j in range(4)]
+    near = jnp.concatenate([sums[0], sums[2]], axis=0)
+    far = jnp.concatenate([sums[1], sums[3]], axis=0)
     for k in (2, 3, 1, 0):
         span = slice(k * step, (k + 1) * step)
-        total = mm(xt_ref[span, :part], sums[0]) + mm(xt2_ref[span, :part], sums[1])
-        total += mm(xp_ref[span], sums[2]) + mm(xp2_ref[span], sums[3])
-        out_refs[k][...] = total.astype(out_refs[k].dtype)
-
-
-def qo_weights_kernel(xt_ref, xt2_ref, y_ref, y2_ref, *out_refs):
-    own = y_ref.shape[0]
-    half = y_ref.shape[1] // 2
-    step = out_refs[0].shape[0]
-    first = xt_ref.shape[1] - 2 * own
-    for k in (2, 3, 1, 0):
-        span = slice(k * step, (k + 1) * step)
+        total = mm(xt_ref[span, : 2 * slab], near) + mm(xt2_ref[span, : 2 * slab], far)
+        kv_refs[k][...] = total.astype(kv_refs[k].dtype)
+        close = slice(k * step // 2, (k + 1) * step // 2)
         for side in (0, 1):
             cols = slice(side * half, (side + 1) * half)
-            at = slice(first + side * own, first + (side + 1) * own)
-            total = mm(xt_ref[span, at], y_ref[:, cols]) + mm(xt2_ref[span, at], y2_ref[:, cols])
-            out_refs[k][:, cols] = total.astype(out_refs[k].dtype)
-
-
-def inputs_kernel(where_ref, near_ref, pair_ref, dq_ref, wk_ref, wv_ref, wq_ref, own_ref, *refs):
-    send_refs, scratch = refs[:3], refs[3]
+            at = slice(2 * slab + side * own, 2 * slab + (side + 1) * own)
+            total = mm(xt_ref[span, at], dqo_ref[:, cols])
+            total += mm(xt2_ref[span, at], dqo2_ref[:, cols])
+            keep_ref[close, cols] = total[: step // 2]
+            send_ref[close, cols] = total[step // 2 :].astype(send_ref.dtype)
+
+
+def inputs_kernel(dkv_ref, dkv2_ref, pair_ref, dq_ref, wk_ref, wv_ref, wq_ref, out_ref):
     width = wk_ref.shape[0]
-    part = near_ref.shape[0]
-    dkv = (near_ref[...] + pair_ref[...].astype(F32)).astype(BF)
-    dkey, dvalue, dquery = dkv[:, :width], dkv[:, width:], dq_ref[:, :width]
+    part = pair_ref.shape[0]
+    dkv = dkv_ref[:part].astype(F32) + dkv2_ref[part : 2 * part].astype(F32)
+    dkv = (dkv + pair_ref[...].astype(F32)).astype(BF)
+    rows = out_ref.shape[0] // 4
     for t in range(4):
         span = slice(t * width, (t + 1) * width)
-        scratch[t, :part] = mm(dkey, wk_ref[:, span]) + mm(dvalue, wv_ref[:, span])
-        scratch[t, part:] = mm(dquery, wq_ref[:, span])
-    own_ref[...] = scratch[where_ref[0]]
-    for k in (1, 2, 3):
-        send_refs[k - 1][...] = scratch[where_ref[0] ^ k].astype(BF)
+        term = mm(dkv[:, :width], wk_ref[:, span]) + mm(dkv[:, width:], wv_ref[:, span])
+        out_ref[t * rows : t * rows + part] = term.astype(BF)
+        term = mm(dq_ref[:, :width], wq_ref[:, span])
+        out_ref[t * rows + part : (t + 1) * rows] = term.astype(BF)
 
 
 VMEM = pl.BlockSpec(memory_space=pltpu.VMEM)
@@ -234,34 +249,45 @@
             scratch_shapes=scratch,
             compiler_params=pltpu.CompilerParams(vmem_limit_bytes=24 * 1024 * 1024),
             cost_estimate=pl.CostEstimate(
-                flops=int(work * 1e9), bytes_accessed=0, transcendentals=0
+                flops=work, bytes_accessed=0, transcendentals=0
             ),
         )(*ins)
 
     hbm = pl.BlockSpec(memory_space=pl.ANY)
     weights = [pltpu.VMEM((width, model), BF)] * 4
-    rows0, kv = pl.pallas_call(
+    rows0, kv, e_part = pl.pallas_call(
         project_kernel,
         out_shape=[
             jax.ShapeDtypeStruct((own, 2 * width), BF),
             jax.ShapeDtypeStruct((slab, 2 * width), BF),
+            jax.ShapeDtypeStruct((quarter, model), BF),
         ],
-        in_specs=[hbm] * 7,
-        out_specs=[VMEM] * 2,
+        in_specs=[SMEM] + [hbm] * 7,
+        out_specs=[VMEM] * 3,
         scratch_shapes=[pltpu.VMEM((rows, model), BF) for rows in (own, own, slab)]
         + weights
         + [pltpu.SemaphoreType.DMA((12,))],
         compiler_params=pltpu.CompilerParams(vmem_limit_bytes=56 * 1024 * 1024),
-    )(rows_in, rows_grad, frames, wq_t, w_out, wk_t, wv_t)
-
-    kv_pair = flip(kv, "z", 8, 1)
-    kv_core = swap(kv, "core")
+    )(where, rows_in, rows_grad, frames, wq_t, w_out, wk_t, wv_t)
+
+    e_part = flip(e_part, "z", 8, 1)
+    e_parts = [e_part] + [flip(e_part, "head", 4, k) for k in (1, 2, 3)]
+
     row_blocks = [rows0] + [flip(rows0, "z", 8, 2 * j) for j in (1, 2, 3)]
 
-    def turn(stacked, other):
+    e_parts[1:], row_blocks[1:] = lax.optimization_barrier((e_parts[1:], row_blocks[1:]))
+    kv, e_pair = call(
+        pair_kernel,
+        [((2 * slab, 2 * width), BF), ((slab, model), BF)],
+        (where, *e_parts, wk_t, wv_t, kv),
+        True,
+    )
+    both = (kv, swap(kv, "core"))
+
+    def turn(stacked):
         place = jnp.arange(model, dtype=jnp.int32)
         unit, rest = place % inner, place // inner
-        a_rel, b_rel = rest % 4, ((rest // 4) % 2) ^ other
+        a_rel, b_rel = rest % 4, (rest // 4) % 2
         x_rel, c_rel = (rest // 8) % 4, rest // 32
         target = (
             (x_rel ^ xi) * 16 + ((2 * a_rel + b_rel) ^ zi) * 2 + (c_rel ^ ci)
@@ -269,14 +295,6 @@
         pick = (place[:, None] == target[None, :]).astype(BF)
         return mm(pick, stacked, (((0,), (1,)), ((), ()))).astype(BF)
 
-    turned = turn(jnp.concatenate([frames, rows_in, rows_grad], axis=0), 0)
-    for_pair = turn(frames, 1)
-    row_blocks[1:], kv_pair, kv_core, for_pair, turned = lax.optimization_barrier(
-        (row_blocks[1:], kv_pair, kv_core, for_pair, turned)
-    )
-    xt, xt_other = turned[: model // 2], swap(turned[model // 2 :], "core")
-    frame_blocks = [kv, kv_core, kv_pair, swap(kv_pair, "core")]
-    from_pair = flip(for_pair, "z", 8, 1)
     starts = [
         slab * (2 * (zi ^ db) + (ci ^ dc)) for db in (0, 1) for dc in (0, 1)
     ]
@@ -285,66 +303,61 @@
     (stats,) = call(
         functools.partial(stats_kernel, heads),
         [((16, 4 * own), F32)],
-        (valid, *row_blocks, *frame_blocks),
+        (valid, *row_blocks, *both),
         True,
-        work=3,
-    )
+    )
+    stats, e_pair = lax.optimization_barrier((stats, e_pair))
     all_stats = [stats] + [flip(stats, "z", 8, 2 * j) for j in (1, 2, 3)]
 
-    all_stats[1:], from_pair, xt_other = lax.optimization_barrier(
-        (all_stats[1:], from_pair, xt_other)
-    )
-    xp, xp_other = from_pair[: model // 2], swap(from_pair[model // 2 :], "core")
+    turned = turn(jnp.concatenate([frames, e_pair, rows_in, rows_grad], axis=0))
+    xt, xt_other = turned[: model // 2], swap(turned[model // 2 :], "core")
+    all_stats[1:], xt, xt_other = lax.optimization_barrier((all_stats[1:], xt, xt_other))
 
     dkv, dq0, *dq_sends = call(
         functools.partial(grads_kernel, heads),
         [((4 * slab, 2 * width), BF), ((own, 2 * width), F32)]
         + [((own, 2 * width), BF)] * 3,
-        (valid, *row_blocks, *frame_blocks, *all_stats),
+        (valid, *row_blocks, *both, *all_stats),
         True,
-        work=8,
     )
 
     dkv_other = swap(dkv, "core")
     dq_recv = [flip(d, "z", 8, 2 * k) for k, d in zip((1, 2, 3), dq_sends)]
 
+    pair = chip_sum(dkv, dkv_other, 2, slab)
+    dq_recv, pair = lax.optimization_barrier((dq_recv, pair))
+    pair_recv = flip(pair, "z", 8, 1)
+    dqo = (dq0 + sum(d.astype(F32) for d in dq_recv)).astype(BF)
+    dqo_other, pair_recv = lax.optimization_barrier((swap(dqo, "core"), pair_recv))
+
     part = model // 8
-    kv_own, *kv_sends, near, pair = call(
-        kv_weights_kernel,
+    kv_own, *kv_sends, qo_keep, qo_send = call(
+        weights_kernel,
         [((part, 2 * width), F32)]
         + [((part, 2 * width), BF)] * 3
-        + [((slab, 2 * width), F32), ((slab, 2 * width), BF)],
-        (xt, xt_other, xp, xp_other, dkv, dkv_other),
+        + [((2 * part, 2 * width), F32), ((2 * part, 2 * width), BF)],
+        (xt, xt_other, dkv, dkv_other, dqo, dqo_other),
     )
     kv_x = [flip(kv_sends[k - 1], "dp", 4, k) for k in (2, 1, 3)]
-    pair_recv = flip(pair, "z", 8, 1)
-
-    dq_recv, kv_own = lax.optimization_barrier((dq_recv, kv_own))
-    dqo = (dq0 + sum(d.astype(F32) for d in dq_recv)).astype(BF)
-    dqo_other = swap(dqo, "core")
-    qo_own, *qo_sends = call(
-        qo_weights_kernel,
-        [((part, 2 * width), F32)] + [((part, 2 * width), BF)] * 3,
-        (xt, xt_other, dqo, dqo_other),
-    )
-    qo_x = [flip(qo_sends[k - 1], "dp", 4, k) for k in (2, 1, 3)]
-
-    own_part, *sends = call(
+    qo_b = flip(qo_send, "z", 8, 1)
+
+    dqo, kv_own = lax.optimization_barrier((dqo, kv_own))
+    (inputs,) = call(
         inputs_kernel,
-        [((slab + own, width), F32)] + [((slab + own, width), BF)] * 3,
-        (where, near, pair_recv, dqo, wk_t, wv_t, wq_t),
-        True,
-        [pltpu.VMEM((4, slab + own, width), F32)],
-    )
-    arrived = [flip(sends[k - 1], "head", 4, k) for k in (2, 1, 3)]
-    inputs = (own_part + sum(p.astype(F32) for p in arrived)).astype(BF)
+        [((4 * (slab + own), width), BF)],
+        (dkv, dkv_other, pair_recv, dqo, wk_t, wv_t, wq_t),
+    )
+    inputs = lax.psum_scatter(inputs, "head", scatter_dimension=0, tiled=True)
     dframes, dinput = inputs[:slab], inputs[slab:]
 
+    cut = part // 2
     kv_sum = kv_own + sum(k.astype(F32) for k in kv_x)
-    qo_sum = qo_own + sum(k.astype(F32) for k in qo_x)
+    kv_b = flip(kv_sum[cut:].astype(BF), "z", 8, 1)
+    qo_sum = qo_keep + qo_b.astype(F32)
+    qo_x = [flip(qo_sum[k * cut : (k + 1) * cut].astype(BF), "dp", 4, k) for k in (2, 1, 3)]
+    kv_sum = kv_sum[:cut] + kv_b.astype(F32)
+    qo_sum = qo_sum[:cut] + sum(q.astype(F32) for q in qo_x)
     total = jnp.concatenate([kv_sum, qo_sum], axis=1)
-    cut = part // 2
-    total = total[:cut] + flip(total[cut:].astype(BF), "z", 8, 1).astype(F32)
     low = total.astype(BF)
     over = [flip(low[k * inner : (k + 1) * inner], "z", 8, 2 * k) for k in (2, 1, 3)]
     total = total[:inner] + sum(p.astype(F32) for p in over)

time: 114 us -> 137 us (1.20)
  between operations: 1.58 us -> 15 us
  starting transfers between devices: 47.7 us -> 53.8 us
  Pallas kernels: 16.7 us -> 18.7 us
  local copies, waits for them, and re-layouts: 4.33 us -> 5.96 us
    ppermute x31 -> x29, starting transfers between devices: 47.7 us -> 53.7 us  [flip(): return lax.ppermute(x, axis, [(i, i ^ bits) for i in range(size)])]
    pallas_call x5, Pallas kernels: 12.3 us -> 14.3 us  [call(): pl.pallas_call(kernel, out_shape=shapes, in_specs=specs, out_specs=[VMEM]...]
    dot_general x2 -> x1, matrix products: 3.87 us -> 2.77 us  [mm(): return lax.dot_general(left, right, dims, preferred_element_type=F32)]
    ppermute x31 -> x29, waiting for transfers between devices: 38.4 us -> 38 us  [flip(): return lax.ppermute(x, axis, [(i, i ^ bits) for i in range(size)])]
  transfers between devices with their start and end apart: 31 -> 30, of which waited for: 13 -> 16; matrix products, arithmetic and copies ran while one was open for 7% -> 3% of each run, Pallas kernels for 5% -> 2%
where the time goes in v1:
time: 137 us
  starting transfers between devices  53.8 us (39%)
  waiting for transfers between devices  38 us (28%)
  Pallas kernels  18.7 us (14%)
  between operations  15 us (11%)
  local copies, waits for them, and re-layouts  5.96 us (4%)
  matrix products  2.77 us (2%)
  other arithmetic  2.68 us (2%)
    ppermute x29, starting transfers between devices, flip(): return lax.ppermute(x, axis, [(i, i ^ bits) for i in range(size)])  53.7 us
    ppermute x29, waiting for transfers between devices, flip(): return lax.ppermute(x, axis, [(i, i ^ bits) for i in range(size)])  38 us
    pallas_call x5, Pallas kernels, call(): pl.pallas_call(kernel, out_shape=shapes, in_specs=specs, out_specs=[VMEM]...  14.3 us
    pallas_call x1, Pallas kernels, per_device(): pl.pallas_call(project_kernel, out_shape=[jax.ShapeDtypeStruct((own, 2 *...  4.41 us
    dot_general x1, matrix products, mm(): return lax.dot_general(left, right, dims, preferred_element_type=F32)  2.77 us
  transfers between devices with their start and end apart: 30, of which 16 were waited for; matrix products, arithmetic and copies ran while one was open for 3% of the time, Pallas kernels for 2%

profile of v1, /device:TPU:8, one launch (start us, length us, event | category | flops | bytes accessed | tf_op | source)
XLA Modules:
  0.0 136.9 jit_solution(6069957554463772361)
XLA Ops:
  7.2 4.4 %shard_map.127 = (bf16[64,640]{1,0:T(8,128)(2,1)}, bf16[256,640]{1,0:T(8,128)(2,1)}, bf16[64,1280]{1,0:T(8,128)(2,1)}) custom-call(s32[1]{0:T(128)} %bitcast.5.where_ref, bf16[64,1280]{1,0:T(8,128)(2,1)} %bitcast.32, bf16[64,1280]{1,0:T(8,128)(2,1)} %bitcast.34, bf16[256,1280]{1,0:T(8,128)(2,1)} %bitcast.30, bf16[320,1280]{1,0:T(8,128)(2,1)} %bitcast.28, ...), custom_call_target="tpu_custom_call" | custom-call | tf_op jit(solution)/shard_map/pallas_call | solution.py:258
  11.7 2.0 %collective-permute-start = (bf16[64,1280]{1,0:T(8,128)(2,1)}, bf16[64,1280]{1,0:T(8,128)(2,1)S(1)}, u32[]{:S(2)}, u32[]{:S(2)}) collective-permute-start(bf16[64,1280]{1,0:T(8,128)(2,1)} %get-tuple-element.44), channel_id=1, source_target_pairs={{0,8},{8,0},{16,24},{24,16},{32,40},{40,32},{48,56},{56,48},{1,9},... | collective-permute-start | bytes 491528 | tf_op jit(solution)/shard_map/ppermute | solution.py:28
  13.7 5.4 %collective-permute-start.6 = (bf16[64,640]{1,0:T(8,128)(2,1)}, bf16[64,640]{1,0:T(8,128)(2,1)S(1)}, u32[]{:S(2)}, u32[]{:S(2)}) collective-permute-start(bf16[64,640]{1,0:T(8,128)(2,1)} %get-tuple-element.43.refs_0_), channel_id=1, source_target_pairs={{0,48},{8,56},{16,32},{24,40},{32,16},{40,24},{48,0},{56,8},{1,49}... | collective-permute-start | bytes 245768 | tf_op jit(solution)/shard_map/ppermute | solution.py:28
  19.1 1.6 %collective-permute-start.3 = (bf16[64,1280]{1,0:T(8,128)(2,1)S(1)}, bf16[64,1280]{1,0:T(8,128)(2,1)S(1)}, u32[]{:S(2)}, u32[]{:S(2)}) collective-permute-start(bf16[64,1280]{1,0:T(8,128)(2,1)S(1)} %collective-permute-done.e0_ref), channel_id=1, source_target_pairs={{0,3},{1,2},{2,1},{3,0},{4,7},{5,6},{6,5},{7,4},{8,11},{9,10},{10,... | collective-permute-start | bytes 491528 | tf_op jit(solution)/shard_map/ppermute | solution.py:28
  20.6 0.9 collective-permute-start.2
  21.6 1.6 %collective-permute-start.1 = (bf16[64,1280]{1,0:T(8,128)(2,1)S(1)}, bf16[64,1280]{1,0:T(8,128)(2,1)S(1)}, u32[]{:S(2)}, u32[]{:S(2)}) collective-permute-start(bf16[64,1280]{1,0:T(8,128)(2,1)S(1)} %collective-permute-done.e0_ref), channel_id=1, source_target_pairs={{0,1},{1,0},{2,3},{3,2},{4,5},{5,4},{6,7},{7,6},{8,9},{9,8},{10,11... | collective-permute-start | bytes 491528 | tf_op jit(solution)/shard_map/ppermute | solution.py:28
  23.2 6.9 %collective-permute-start.5 = (bf16[64,640]{1,0:T(8,128)(2,1)}, bf16[64,640]{1,0:T(8,128)(2,1)S(1)}, u32[]{:S(2)}, u32[]{:S(2)}) collective-permute-start(bf16[64,640]{1,0:T(8,128)(2,1)} %get-tuple-element.43.refs_0_), channel_id=1, source_target_pairs={{0,32},{8,40},{16,48},{24,56},{32,0},{40,8},{48,16},{56,24},{1,33}... | collective-permute-start | bytes 245768 | tf_op jit(solution)/shard_map/ppermute | solution.py:28
  30.1 1.1 collective-permute-start.4
  31.2 2.5 %collective-permute-done.5.refs_2_ = bf16[64,640]{1,0:T(8,128)(2,1)S(1)} collective-permute-done((bf16[64,640]{1,0:T(8,128)(2,1)}, bf16[64,640]{1,0:T(8,128)(2,1)S(1)}, u32[]{:S(2)}, u32[]{:S(2)}) %collective-permute-start.5) | collective-permute-done | bytes 81952 | tf_op jit(solution)/shard_map/ppermute | solution.py:28
  33.7 2.8 %collective-permute-done.4.refs_1_ = bf16[64,640]{1,0:T(8,128)(2,1)S(1)} collective-permute-done((bf16[64,640]{1,0:T(8,128)(2,1)}, bf16[64,640]{1,0:T(8,128)(2,1)S(1)}, u32[]{:S(2)}, u32[]{:S(2)}) %collective-permute-start.4) | collective-permute-done | bytes 81952 | tf_op jit(solution)/shard_map/ppermute | solution.py:28
  36.5 1.0 copy-done.4
  37.5 0.9 shard_map.128
  38.4 0.8 copy-done.5
  40.1 1.3 collective-permute-done.7.refs_5_
  41.4 2.5 %shard_map.129.refs_6_ = f32[16,256]{1,0:T(8,128)S(1)} custom-call(s32[4]{0:T(128)S(1)} %pad_add_fusion.valid_ref, bf16[64,640]{1,0:T(8,128)(2,1)S(1)} %copy-done.3, bf16[64,640]{1,0:T(8,128)(2,1)S(1)} %collective-permute-done.4.refs_1_, bf16[64,640]{1,0:T(8,128)(2,1)S(1)} %collective-permute-done.5.refs_2_, ...), custom_call_target="tpu_custom_call" | custom-call | flops 2 | tf_op jit(solution)/shard_map/pallas_call | solution.py:244
  43.9 2.8 %fusion.4 = bf16[1280,640]{1,0:T(8,128)(2,1)S(1)} fusion(s32[1280]{0:T(1024)S(1)} %fusion.30, bf16[64,1280]{1,0:T(8,128)(2,1)S(1)} %bitcast.35, bf16[64,1280]{1,0:T(8,128)(2,1)S(1)} %bitcast.33, bf16[256,1280]{1,0:T(8,128)(2,1)S(1)} %copy-done.6, bf16[256,1280]{1,0:T(8,128)(2,1)S(1)} %bitcast.31), kind=kOutput, calls=%fused_computation.4 | convolution fusion | flops 2107801600 | bytes 3281920 | tf_op jit(solution)/shard_map/dot_general | solution.py:24
  47.1 2.7 %collective-permute-start.10 = (f32[16,256]{1,0:T(8,128)S(1)}, f32[16,256]{1,0:T(8,128)S(1)}, u32[]{:S(2)}, u32[]{:S(2)}) collective-permute-start(f32[16,256]{1,0:T(8,128)S(1)} %shard_map.129.refs_6_), channel_id=1, source_target_pairs={{0,48},{8,56},{16,32},{24,40},{32,16},{40,24},{48,0},{56,8},{1,49}... | collective-permute-start | bytes 49160 | tf_op jit(solution)/shard_map/ppermute | solution.py:28
  49.8 1.5 %collective-permute-start.9 = (f32[16,256]{1,0:T(8,128)S(1)}, f32[16,256]{1,0:T(8,128)S(1)}, u32[]{:S(2)}, u32[]{:S(2)}) collective-permute-start(f32[16,256]{1,0:T(8,128)S(1)} %shard_map.129.refs_6_), channel_id=1, source_target_pairs={{0,32},{8,40},{16,48},{24,56},{32,0},{40,8},{48,16},{56,24},{1,33}... | collective-permute-start | bytes 49160 | tf_op jit(solution)/shard_map/ppermute | solution.py:28
  51.3 2.4 %collective-permute-start.8 = (f32[16,256]{1,0:T(8,128)S(1)}, f32[16,256]{1,0:T(8,128)S(1)}, u32[]{:S(2)}, u32[]{:S(2)}) collective-permute-start(f32[16,256]{1,0:T(8,128)S(1)} %shard_map.129.refs_6_), channel_id=1, source_target_pairs={{0,16},{8,24},{16,0},{24,8},{32,48},{40,56},{48,32},{56,40},{1,17}... | collective-permute-start | bytes 49160 | tf_op jit(solution)/shard_map/ppermute | solution.py:28
  53.7 3.8 %collective-permute-done.9.refs_8_ = f32[16,256]{1,0:T(8,128)S(1)} collective-permute-done((f32[16,256]{1,0:T(8,128)S(1)}, f32[16,256]{1,0:T(8,128)S(1)}, u32[]{:S(2)}, u32[]{:S(2)}) %collective-permute-start.9) | collective-permute-done | bytes 16416 | tf_op jit(solution)/shard_map/ppermute | solution.py:28
  57.6 6.3 %shard_map.130 = (bf16[1024,640]{1,0:T(8,128)(2,1)S(1)}, f32[64,640]{1,0:T(8,128)S(1)}, bf16[64,640]{1,0:T(8,128)(2,1)S(1)}, bf16[64,640]{1,0:T(8,128)(2,1)S(1)}, bf16[64,640]{1,0:T(8,128)(2,1)S(1)}) custom-call(s32[4]{0:T(128)S(1)} %pad_add_fusion.valid_ref, bf16[64,640]{1,0:T(8,128)(2,1)S(1)} %copy-done.3, ...), custom_call_target="tpu_custom_call" | custom-call | flops 2 | tf_op jit(solution)/shard_map/pallas_call | solution.py:244
  64.0 0.9 collective-permute-start.13
  64.9 3.1 %collective-permute-start.14 = (bf16[64,640]{1,0:T(8,128)(2,1)S(1)}, bf16[64,640]{1,0:T(8,128)(2,1)S(1)}, u32[]{:S(2)}, u32[]{:S(2)}) collective-permute-start(bf16[64,640]{1,0:T(8,128)(2,1)S(1)} %get-tuple-element.62), channel_id=1, source_target_pairs={{0,32},{8,40},{16,48},{24,56},{32,0},{40,8},{48,16},{56,24},{1,33}... | collective-permute-start | bytes 245768 | tf_op jit(solution)/shard_map/ppermute | solution.py:28
  68.0 2.6 %collective-permute-start.15 = (bf16[64,640]{1,0:T(8,128)(2,1)S(1)}, bf16[64,640]{1,0:T(8,128)(2,1)S(1)}, u32[]{:S(2)}, u32[]{:S(2)}) collective-permute-start(bf16[64,640]{1,0:T(8,128)(2,1)S(1)} %get-tuple-element.63), channel_id=1, source_target_pairs={{0,48},{8,56},{16,32},{24,40},{32,16},{40,24},{48,0},{56,8},{1,49}... | collective-permute-start | bytes 245768 | tf_op jit(solution)/shard_map/ppermute | solution.py:28
  70.7 2.7 %collective-permute-done.13 = bf16[64,640]{1,0:T(8,128)(2,1)S(1)} collective-permute-done((bf16[64,640]{1,0:T(8,128)(2,1)S(1)}, bf16[64,640]{1,0:T(8,128)(2,1)S(1)}, u32[]{:S(2)}, u32[]{:S(2)}) %collective-permute-start.13) | collective-permute-done | bytes 81952 | tf_op jit(solution)/shard_map/ppermute | solution.py:28
  73.5 4.2 %collective-permute-done.15 = bf16[64,640]{1,0:T(8,128)(2,1)S(1)} collective-permute-done((bf16[64,640]{1,0:T(8,128)(2,1)S(1)}, bf16[64,640]{1,0:T(8,128)(2,1)S(1)}, u32[]{:S(2)}, u32[]{:S(2)}) %collective-permute-start.15) | collective-permute-done | bytes 81952 | tf_op jit(solution)/shard_map/ppermute | solution.py:28
  77.8 2.3 %collective-permute-start.17 = (bf16[256,640]{1,0:T(8,128)(2,1)S(1)}, bf16[256,640]{1,0:T(8,128)(2,1)S(1)}, u32[]{:S(2)}, u32[]{:S(2)}) collective-permute-start(bf16[256,640]{1,0:T(8,128)(2,1)S(1)} %add_convert_fusion), channel_id=1, source_target_pairs={{0,8},{8,0},{16,24},{24,16},{32,40},{40,32},{48,56},{56,48},{1,9},... | collective-permute-start | bytes 983048 | tf_op jit(solution)/shard_map/ppermute | solution.py:28
  80.3 1.3 collective-permute-done.16.dqo2_ref
  81.5 6.1 %collective-permute-done.17.pair_ref = bf16[256,640]{1,0:T(8,128)(2,1)S(1)} collective-permute-done((bf16[256,640]{1,0:T(8,128)(2,1)S(1)}, bf16[256,640]{1,0:T(8,128)(2,1)S(1)}, u32[]{:S(2)}, u32[]{:S(2)}) %collective-permute-start.17) | collective-permute-done | bytes 327712 | tf_op jit(solution)/shard_map/ppermute | solution.py:28
  87.6 2.3 %shard_map.131 = (f32[160,640]{1,0:T(8,128)S(1)}, bf16[160,640]{1,0:T(8,128)(2,1)}, bf16[160,640]{1,0:T(8,128)(2,1)}, bf16[160,640]{1,0:T(8,128)(2,1)S(1)}, f32[...) custom-call(bf16[640,640]{1,0:T(8,128)(2,1)S(1)} %get-tuple-element.69.xt_ref, ...), custom_call_target="tpu_custom_call" | custom-call | flops 2 | tf_op jit(solution)/shard_map/pallas_call | solution.py:244
  89.9 3.0 %collective-permute-start.18 = (bf16[160,640]{1,0:T(8,128)(2,1)}, bf16[160,640]{1,0:T(8,128)(2,1)}, u32[]{:S(2)}, u32[]{:S(2)}) collective-permute-start(bf16[160,640]{1,0:T(8,128)(2,1)} %get-tuple-element.75), channel_id=1, source_target_pairs={{0,128},{64,192},{128,0},{192,64},{1,129},{65,193},{129,1},{193,65... | collective-permute-start | bytes 614408 | tf_op jit(solution)/shard_map/ppermute | solution.py:28
  94.1 1.7 %collective-permute-start.22 = (bf16[320,640]{1,0:T(8,128)(2,1)S(1)}, bf16[320,640]{1,0:T(8,128)(2,1)}, u32[]{:S(2)}, u32[]{:S(2)}) collective-permute-start(bf16[320,640]{1,0:T(8,128)(2,1)S(1)} %get-tuple-element.79), channel_id=1, source_target_pairs={{0,8},{8,0},{16,24},{24,16},{32,40},{40,32},{48,56},{56,48},{1,9},... | collective-permute-start | bytes 1228808 | tf_op jit(solution)/shard_map/ppermute | solution.py:28
  95.8 2.3 %shard_map.132 = bf16[1280,320]{1,0:T(8,128)(2,1)} custom-call(bf16[1024,640]{1,0:T(8,128)(2,1)S(1)} %get-tuple-element.59.dkv_ref, bf16[1024,640]{1,0:T(8,128)(2,1)S(1)} %collective-permute-done.12.dkv2_ref, bf16[256,640]{1,0:T(8,128)(2,1)S(1)} %collective-permute-done.17.pair_ref, bf16[64,640]{1,0:T(8,128)(2,1)S(1)} %add_convert_fusion.1.dqo_ref.dq_ref, ...), custom_call_target="tpu_custom_call" | custom-call | flops 2 | tf_op jit(solution)/shard_map/pallas_call | solution.py:244
  98.1 1.6 %collective-permute-done.18 = bf16[160,640]{1,0:T(8,128)(2,1)} collective-permute-done((bf16[160,640]{1,0:T(8,128)(2,1)}, bf16[160,640]{1,0:T(8,128)(2,1)}, u32[]{:S(2)}, u32[]{:S(2)}) %collective-permute-start.18) | collective-permute-done | bytes 204832 | tf_op jit(solution)/shard_map/ppermute | solution.py:28
  99.7 2.5 %collective-permute-done.19 = bf16[160,640]{1,0:T(8,128)(2,1)} collective-permute-done((bf16[160,640]{1,0:T(8,128)(2,1)}, bf16[160,640]{1,0:T(8,128)(2,1)}, u32[]{:S(2)}, u32[]{:S(2)}) %collective-permute-start.19) | collective-permute-done | bytes 204832 | tf_op jit(solution)/shard_map/ppermute | solution.py:28
  102.3 1.2 add_add_fusion
  103.5 1.6 %collective-permute-start.21 = (bf16[80,640]{1,0:T(8,128)(2,1)S(1)}, bf16[80,640]{1,0:T(8,128)(2,1)S(1)}, u32[]{:S(2)}, u32[]{:S(2)}) collective-permute-start(bf16[80,640]{1,0:T(8,128)(2,1)S(1)} %slice.120), channel_id=1, source_target_pairs={{0,8},{8,0},{16,24},{24,16},{32,40},{40,32},{48,56},{56,48},{1,9},... | collective-permute-start | bytes 307208 | tf_op jit(solution)/shard_map/ppermute | solution.py:28
  105.1 1.1 fusion.45
  106.3 2.9 %collective-permute-start.23 = (bf16[80,640]{1,0:T(8,128)(2,1)S(1)}, bf16[80,640]{1,0:T(8,128)(2,1)S(1)}, u32[]{:S(2)}, u32[]{:S(2)}) collective-permute-start(bf16[80,640]{1,0:T(8,128)(2,1)S(1)} %get-tuple-element.90), channel_id=1, source_target_pairs={{0,128},{64,192},{128,0},{192,64},{1,129},{65,193},{129,1},{193,65... | collective-permute-start | bytes 307208 | tf_op jit(solution)/shard_map/ppermute | solution.py:28
  109.2 1.2 collective-permute-start.25
  110.4 2.1 %collective-permute-done.23 = bf16[80,640]{1,0:T(8,128)(2,1)S(1)} collective-permute-done((bf16[80,640]{1,0:T(8,128)(2,1)S(1)}, bf16[80,640]{1,0:T(8,128)(2,1)S(1)}, u32[]{:S(2)}, u32[]{:S(2)}) %collective-permute-start.23) | collective-permute-done | bytes 102432 | tf_op jit(solution)/shard_map/ppermute | solution.py:28
  112.6 2.5 %collective-permute-done.25 = bf16[80,640]{1,0:T(8,128)(2,1)S(1)} collective-permute-done((bf16[80,640]{1,0:T(8,128)(2,1)S(1)}, bf16[80,640]{1,0:T(8,128)(2,1)S(1)}, u32[]{:S(2)}, u32[]{:S(2)}) %collective-permute-start.25) | collective-permute-done | bytes 102432 | tf_op jit(solution)/shard_map/ppermute | solution.py:28
  115.2 3.3 %collective-permute-start.26 = (bf16[20,1280]{1,0:T(8,128)(2,1)S(1)}, bf16[20,1280]{1,0:T(8,128)(2,1)S(1)}, u32[]{:S(2)}, u32[]{:S(2)}) collective-permute-start(bf16[20,1280]{1,0:T(8,128)(2,1)S(1)} %get-tuple-element.93), channel_id=1, source_target_pairs={{0,32},{8,40},{16,48},{24,56},{32,0},{40,8},{48,16},{56,24},{1,33}... | collective-permute-start | bytes 153608 | tf_op jit(solution)/shard_map/ppermute | solution.py:28
  118.5 2.5 %collective-permute-start.28 = (bf16[20,1280]{1,0:T(8,128)(2,1)S(1)}, bf16[20,1280]{1,0:T(8,128)(2,1)S(1)}, u32[]{:S(2)}, u32[]{:S(2)}) collective-permute-start(bf16[20,1280]{1,0:T(8,128)(2,1)S(1)} %get-tuple-element.94), channel_id=1, source_target_pairs={{0,48},{8,56},{16,32},{24,40},{32,16},{40,24},{48,0},{56,8},{1,49}... | collective-permute-start | bytes 153608 | tf_op jit(solution)/shard_map/ppermute | solution.py:28
  121.8 2.6 %collective-permute-done.26 = bf16[20,1280]{1,0:T(8,128)(2,1)S(1)} collective-permute-done((bf16[20,1280]{1,0:T(8,128)(2,1)S(1)}, bf16[20,1280]{1,0:T(8,128)(2,1)S(1)}, u32[]{:S(2)}, u32[]{:S(2)}) %collective-permute-start.26) | collective-permute-done | bytes 51232 | tf_op jit(solution)/shard_map/ppermute | solution.py:28
  125.2 0.9 collective-permute-done.27
  126.8 0.9 slice_bitcast_fusion
  128.6 1.4 %slice_bitcast_fusion.1 = bf16[1,64,320]{2,1,0:T(8,128)(2,1)} fusion(bf16[320,320]{1,0:T(8,128)(2,1)} %reduce-scatter.2.cloned.1.call-done), kind=kLoop, calls=%fused_computation.26 | loop fusion | bytes 81920 | tf_op jit(solution)/shard_map/broadcast_in_dim | solution.py:365
  (58 shorter events, 5.6 us)
Async XLA Ops:
  7.2 119.7 %reduce-scatter.2.cloned.1.call-start = ((), (), s32[]{:S(2)}) async-start(), calls=%async_computation.1 | async-start | bytes 1228800 | tf_op jit(solution)/shard_map/reduce_scatter | solution.py:350
  7.2 29.3 %copy-start = (bf16[1280,320]{0,1:T(8,128)(2,1)S(1)}, bf16[1280,320]{0,1:T(8,128)(2,1)}, u32[]{:S(2)}) copy-start(bf16[1280,320]{0,1:T(8,128)(2,1)} %param.13) | copy-start | bytes 2457604
  7.2 29.3 %copy-start.1 = (bf16[1280,320]{0,1:T(8,128)(2,1)S(1)}, bf16[1280,320]{0,1:T(8,128)(2,1)}, u32[]{:S(2)}) copy-start(bf16[1280,320]{0,1:T(8,128)(2,1)} %param.14) | copy-start | bytes 2457604
  11.7 29.7 %copy-start.3 = (bf16[64,640]{1,0:T(8,128)(2,1)S(1)}, bf16[64,640]{1,0:T(8,128)(2,1)}, u32[]{:S(2)}) copy-start(bf16[64,640]{1,0:T(8,128)(2,1)} %get-tuple-element.43.refs_0_) | copy-start | bytes 245764
  11.7 7.4 %collective-permute-start = (bf16[64,1280]{1,0:T(8,128)(2,1)}, bf16[64,1280]{1,0:T(8,128)(2,1)S(1)}, u32[]{:S(2)}, u32[]{:S(2)}) collective-permute-start(bf16[64,1280]{1,0:T(8,128)(2,1)} %get-tuple-element.44), channel_id=1, source_target_pairs={{0,8},{8,0},{16,24},{24,16},{32,40},{40,32},{48,56},{56,48},{1,9},... | collective-permute-start | bytes 491528 | tf_op jit(solution)/shard_map/ppermute | solution.py:28
  13.7 16.4 %collective-permute-start.6 = (bf16[64,640]{1,0:T(8,128)(2,1)}, bf16[64,640]{1,0:T(8,128)(2,1)S(1)}, u32[]{:S(2)}, u32[]{:S(2)}) collective-permute-start(bf16[64,640]{1,0:T(8,128)(2,1)} %get-tuple-element.43.refs_0_), channel_id=1, source_target_pairs={{0,48},{8,56},{16,32},{24,40},{32,16},{40,24},{48,0},{56,8},{1,49}... | collective-permute-start | bytes 245768 | tf_op jit(solution)/shard_map/ppermute | solution.py:28
  19.1 17.4 %collective-permute-start.3 = (bf16[64,1280]{1,0:T(8,128)(2,1)S(1)}, bf16[64,1280]{1,0:T(8,128)(2,1)S(1)}, u32[]{:S(2)}, u32[]{:S(2)}) collective-permute-start(bf16[64,1280]{1,0:T(8,128)(2,1)S(1)} %collective-permute-done.e0_ref), channel_id=1, source_target_pairs={{0,3},{1,2},{2,1},{3,0},{4,7},{5,6},{6,5},{7,4},{8,11},{9,10},{10,... | collective-permute-start | bytes 491528 | tf_op jit(solution)/shard_map/ppermute | solution.py:28
  20.6 15.8 %collective-permute-start.2 = (bf16[64,1280]{1,0:T(8,128)(2,1)S(1)}, bf16[64,1280]{1,0:T(8,128)(2,1)S(1)}, u32[]{:S(2)}, u32[]{:S(2)}) collective-permute-start(bf16[64,1280]{1,0:T(8,128)(2,1)S(1)} %collective-permute-done.e0_ref), channel_id=1, source_target_pairs={{0,2},{1,3},{2,0},{3,1},{4,6},{5,7},{6,4},{7,5},{8,10},{9,11},{10,... | collective-permute-start | bytes 491528 | tf_op jit(solution)/shard_map/ppermute | solution.py:28
  21.6 14.9 %collective-permute-start.1 = (bf16[64,1280]{1,0:T(8,128)(2,1)S(1)}, bf16[64,1280]{1,0:T(8,128)(2,1)S(1)}, u32[]{:S(2)}, u32[]{:S(2)}) collective-permute-start(bf16[64,1280]{1,0:T(8,128)(2,1)S(1)} %collective-permute-done.e0_ref), channel_id=1, source_target_pairs={{0,1},{1,0},{2,3},{3,2},{4,5},{5,4},{6,7},{7,6},{8,9},{9,8},{10,11... | collective-permute-start | bytes 491528 | tf_op jit(solution)/shard_map/ppermute | solution.py:28
  23.2 10.5 %collective-permute-start.5 = (bf16[64,640]{1,0:T(8,128)(2,1)}, bf16[64,640]{1,0:T(8,128)(2,1)S(1)}, u32[]{:S(2)}, u32[]{:S(2)}) collective-permute-start(bf16[64,640]{1,0:T(8,128)(2,1)} %get-tuple-element.43.refs_0_), channel_id=1, source_target_pairs={{0,32},{8,40},{16,48},{24,56},{32,0},{40,8},{48,16},{56,24},{1,33}... | collective-permute-start | bytes 245768 | tf_op jit(solution)/shard_map/ppermute | solution.py:28
  30.1 6.4 %collective-permute-start.4 = (bf16[64,640]{1,0:T(8,128)(2,1)}, bf16[64,640]{1,0:T(8,128)(2,1)S(1)}, u32[]{:S(2)}, u32[]{:S(2)}) collective-permute-start(bf16[64,640]{1,0:T(8,128)(2,1)} %get-tuple-element.43.refs_0_), channel_id=1, source_target_pairs={{0,16},{8,24},{16,0},{24,8},{32,48},{40,56},{48,32},{56,40},{1,17}... | collective-permute-start | bytes 245768 | tf_op jit(solution)/shard_map/ppermute | solution.py:28
  36.5 1.0 copy-start.4
  37.5 6.4 %copy-start.8 = (bf16[1,64,1280]{2,1,0:T(8,128)(2,1)S(1)}, bf16[1,64,1280]{2,1,0:T(8,128)(2,1)}, u32[]{:S(2)}) copy-start(bf16[1,64,1280]{2,1,0:T(8,128)(2,1)} %param.8) | copy-start | bytes 491524
  38.4 0.8 copy-start.5
  39.3 2.1 %collective-permute-start.7 = (bf16[512,640]{1,0:T(8,128)(2,1)S(1)}, bf16[512,640]{1,0:T(8,128)(2,1)S(1)}, u32[]{:S(2)}, u32[]{:S(2)}) collective-permute-start(bf16[512,640]{1,0:T(8,128)(2,1)S(1)} %get-tuple-element.52.refs_4_), channel_id=1, source_target_pairs={{0,4},{4,0},{1,5},{5,1},{2,6},{6,2},{3,7},{7,3},{8,12},{12,8},{9,1... | collective-permute-start | bytes 1966088 | tf_op jit(solution)/shard_map/ppermute | solution.py:28
  39.9 4.0 %copy-start.6 = (bf16[256,1280]{1,0:T(8,128)(2,1)S(1)}, bf16[256,1280]{1,0:T(8,128)(2,1)}, u32[]{:S(2)}) copy-start(bf16[256,1280]{1,0:T(8,128)(2,1)} %copy-done.5) | copy-start | bytes 1966084
  40.0 4.0 %copy-start.7 = (bf16[1,256,1280]{2,1,0:T(8,128)(2,1)S(1)}, bf16[1,256,1280]{2,1,0:T(8,128)(2,1)}, u32[]{:S(2)}) copy-start(bf16[1,256,1280]{2,1,0:T(8,128)(2,1)} %param.10) | copy-start | bytes 1966084
  40.0 4.0 %copy-start.9 = (bf16[1,64,1280]{2,1,0:T(8,128)(2,1)S(1)}, bf16[1,64,1280]{2,1,0:T(8,128)(2,1)}, u32[]{:S(2)}) copy-start(bf16[1,64,1280]{2,1,0:T(8,128)(2,1)} %param.9) | copy-start | bytes 491524
  46.9 10.7 %collective-permute-start.11 = (bf16[640,640]{1,0:T(8,128)(2,1)S(1)}, bf16[640,640]{1,0:T(8,128)(2,1)S(1)}, u32[]{:S(2)}, u32[]{:S(2)}) collective-permute-start(bf16[640,640]{1,0:T(8,128)(2,1)S(1)} %get-tuple-element.88), channel_id=1, source_target_pairs={{0,4},{4,0},{1,5},{5,1},{2,6},{6,2},{3,7},{7,3},{8,12},{12,8},{9,1... | collective-permute-start | bytes 2457608 | tf_op jit(solution)/shard_map/ppermute | solution.py:28
  47.1 6.6 %collective-permute-start.10 = (f32[16,256]{1,0:T(8,128)S(1)}, f32[16,256]{1,0:T(8,128)S(1)}, u32[]{:S(2)}, u32[]{:S(2)}) collective-permute-start(f32[16,256]{1,0:T(8,128)S(1)} %shard_map.129.refs_6_), channel_id=1, source_target_pairs={{0,48},{8,56},{16,32},{24,40},{32,16},{40,24},{48,0},{56,8},{1,49}... | collective-permute-start | bytes 49160 | tf_op jit(solution)/shard_map/ppermute | solution.py:28
  49.8 7.7 %collective-permute-start.9 = (f32[16,256]{1,0:T(8,128)S(1)}, f32[16,256]{1,0:T(8,128)S(1)}, u32[]{:S(2)}, u32[]{:S(2)}) collective-permute-start(f32[16,256]{1,0:T(8,128)S(1)} %shard_map.129.refs_6_), channel_id=1, source_target_pairs={{0,32},{8,40},{16,48},{24,56},{32,0},{40,8},{48,16},{56,24},{1,33}... | collective-permute-start | bytes 49160 | tf_op jit(solution)/shard_map/ppermute | solution.py:28
  51.3 6.2 %collective-permute-start.8 = (f32[16,256]{1,0:T(8,128)S(1)}, f32[16,256]{1,0:T(8,128)S(1)}, u32[]{:S(2)}, u32[]{:S(2)}) collective-permute-start(f32[16,256]{1,0:T(8,128)S(1)} %shard_map.129.refs_6_), channel_id=1, source_target_pairs={{0,16},{8,24},{16,0},{24,8},{32,48},{40,56},{48,32},{56,40},{1,17}... | collective-permute-start | bytes 49160 | tf_op jit(solution)/shard_map/ppermute | solution.py:28
  63.9 6.7 %collective-permute-start.12 = (bf16[1024,640]{1,0:T(8,128)(2,1)S(1)}, bf16[1024,640]{1,0:T(8,128)(2,1)S(1)}, u32[]{:S(2)}, u32[]{:S(2)}) collective-permute-start(bf16[1024,640]{1,0:T(8,128)(2,1)S(1)} %get-tuple-element.59.dkv_ref), channel_id=1, source_target_pairs={{0,4},{4,0},{1,5},{5,1},{2,6},{6,2},{3,7},{7,3},{8,12},{12,8},{9,1... | collective-permute-start | bytes 3932168 | tf_op jit(solution)/shard_map/ppermute | solution.py:28
  64.0 9.4 %collective-permute-start.13 = (bf16[64,640]{1,0:T(8,128)(2,1)S(1)}, bf16[64,640]{1,0:T(8,128)(2,1)S(1)}, u32[]{:S(2)}, u32[]{:S(2)}) collective-permute-start(bf16[64,640]{1,0:T(8,128)(2,1)S(1)} %get-tuple-element.61), channel_id=1, source_target_pairs={{0,16},{8,24},{16,0},{24,8},{32,48},{40,56},{48,32},{56,40},{1,17}... | collective-permute-start | bytes 245768 | tf_op jit(solution)/shard_map/ppermute | solution.py:28
  64.9 8.7 %collective-permute-start.14 = (bf16[64,640]{1,0:T(8,128)(2,1)S(1)}, bf16[64,640]{1,0:T(8,128)(2,1)S(1)}, u32[]{:S(2)}, u32[]{:S(2)}) collective-permute-start(bf16[64,640]{1,0:T(8,128)(2,1)S(1)} %get-tuple-element.62), channel_id=1, source_target_pairs={{0,32},{8,40},{16,48},{24,56},{32,0},{40,8},{48,16},{56,24},{1,33}... | collective-permute-start | bytes 245768 | tf_op jit(solution)/shard_map/ppermute | solution.py:28
  68.0 9.8 %collective-permute-start.15 = (bf16[64,640]{1,0:T(8,128)(2,1)S(1)}, bf16[64,640]{1,0:T(8,128)(2,1)S(1)}, u32[]{:S(2)}, u32[]{:S(2)}) collective-permute-start(bf16[64,640]{1,0:T(8,128)(2,1)S(1)} %get-tuple-element.63), channel_id=1, source_target_pairs={{0,48},{8,56},{16,32},{24,40},{32,16},{40,24},{48,0},{56,8},{1,49}... | collective-permute-start | bytes 245768 | tf_op jit(solution)/shard_map/ppermute | solution.py:28
  77.8 9.8 %collective-permute-start.17 = (bf16[256,640]{1,0:T(8,128)(2,1)S(1)}, bf16[256,640]{1,0:T(8,128)(2,1)S(1)}, u32[]{:S(2)}, u32[]{:S(2)}) collective-permute-start(bf16[256,640]{1,0:T(8,128)(2,1)S(1)} %add_convert_fusion), channel_id=1, source_target_pairs={{0,8},{8,0},{16,24},{24,16},{32,40},{40,32},{48,56},{56,48},{1,9},... | collective-permute-start | bytes 983048 | tf_op jit(solution)/shard_map/ppermute | solution.py:28
  80.2 15.7 %copy-start.2 = (bf16[1280,320]{0,1:T(8,128)(2,1)S(1)}, bf16[1280,320]{0,1:T(8,128)(2,1)}, u32[]{:S(2)}) copy-start(bf16[1280,320]{0,1:T(8,128)(2,1)} %param.12) | copy-start | bytes 2457604
  80.2 1.4 collective-permute-start.16
  89.9 9.8 %collective-permute-start.18 = (bf16[160,640]{1,0:T(8,128)(2,1)}, bf16[160,640]{1,0:T(8,128)(2,1)}, u32[]{:S(2)}, u32[]{:S(2)}) collective-permute-start(bf16[160,640]{1,0:T(8,128)(2,1)} %get-tuple-element.75), channel_id=1, source_target_pairs={{0,128},{64,192},{128,0},{192,64},{1,129},{65,193},{129,1},{193,65... | collective-permute-start | bytes 614408 | tf_op jit(solution)/shard_map/ppermute | solution.py:28
  92.9 9.3 %collective-permute-start.19 = (bf16[160,640]{1,0:T(8,128)(2,1)}, bf16[160,640]{1,0:T(8,128)(2,1)}, u32[]{:S(2)}, u32[]{:S(2)}) collective-permute-start(bf16[160,640]{1,0:T(8,128)(2,1)} %get-tuple-element.76), channel_id=1, source_target_pairs={{0,64},{64,0},{128,192},{192,128},{1,65},{65,1},{129,193},{193,129... | collective-permute-start | bytes 614408 | tf_op jit(solution)/shard_map/ppermute | solution.py:28
  93.5 8.8 %collective-permute-start.20 = (bf16[160,640]{1,0:T(8,128)(2,1)S(1)}, bf16[160,640]{1,0:T(8,128)(2,1)}, u32[]{:S(2)}, u32[]{:S(2)}) collective-permute-start(bf16[160,640]{1,0:T(8,128)(2,1)S(1)} %get-tuple-element.77), channel_id=1, source_target_pairs={{0,192},{64,128},{128,64},{192,0},{1,193},{65,129},{129,65},{193,1... | collective-permute-start | bytes 614408 | tf_op jit(solution)/shard_map/ppermute | solution.py:28
  94.1 11.1 %collective-permute-start.22 = (bf16[320,640]{1,0:T(8,128)(2,1)S(1)}, bf16[320,640]{1,0:T(8,128)(2,1)}, u32[]{:S(2)}, u32[]{:S(2)}) collective-permute-start(bf16[320,640]{1,0:T(8,128)(2,1)S(1)} %get-tuple-element.79), channel_id=1, source_target_pairs={{0,8},{8,0},{16,24},{24,16},{32,40},{40,32},{48,56},{56,48},{1,9},... | collective-permute-start | bytes 1228808 | tf_op jit(solution)/shard_map/ppermute | solution.py:28
  103.5 6.9 %collective-permute-start.21 = (bf16[80,640]{1,0:T(8,128)(2,1)S(1)}, bf16[80,640]{1,0:T(8,128)(2,1)S(1)}, u32[]{:S(2)}, u32[]{:S(2)}) collective-permute-start(bf16[80,640]{1,0:T(8,128)(2,1)S(1)} %slice.120), channel_id=1, source_target_pairs={{0,8},{8,0},{16,24},{24,16},{32,40},{40,32},{48,56},{56,48},{1,9},... | collective-permute-start | bytes 307208 | tf_op jit(solution)/shard_map/ppermute | solution.py:28
  106.3 6.3 %collective-permute-start.23 = (bf16[80,640]{1,0:T(8,128)(2,1)S(1)}, bf16[80,640]{1,0:T(8,128)(2,1)S(1)}, u32[]{:S(2)}, u32[]{:S(2)}) collective-permute-start(bf16[80,640]{1,0:T(8,128)(2,1)S(1)} %get-tuple-element.90), channel_id=1, source_target_pairs={{0,128},{64,192},{128,0},{192,64},{1,129},{65,193},{129,1},{193,65... | collective-permute-start | bytes 307208 | tf_op jit(solution)/shard_map/ppermute | solution.py:28
  109.2 5.9 %collective-permute-start.25 = (bf16[80,640]{1,0:T(8,128)(2,1)S(1)}, bf16[80,640]{1,0:T(8,128)(2,1)S(1)}, u32[]{:S(2)}, u32[]{:S(2)}) collective-permute-start(bf16[80,640]{1,0:T(8,128)(2,1)S(1)} %get-tuple-element.91), channel_id=1, source_target_pairs={{0,192},{64,128},{128,64},{192,0},{1,193},{65,129},{129,65},{193,1... | collective-permute-start | bytes 307208 | tf_op jit(solution)/shard_map/ppermute | solution.py:28
  110.4 4.7 %collective-permute-start.24 = (bf16[80,640]{1,0:T(8,128)(2,1)S(1)}, bf16[80,640]{1,0:T(8,128)(2,1)S(1)}, u32[]{:S(2)}, u32[]{:S(2)}) collective-permute-start(bf16[80,640]{1,0:T(8,128)(2,1)S(1)} %get-tuple-element.92), channel_id=1, source_target_pairs={{0,64},{64,0},{128,192},{192,128},{1,65},{65,1},{129,193},{193,129... | collective-permute-start | bytes 307208 | tf_op jit(solution)/shard_map/ppermute | solution.py:28
  115.2 9.2 %collective-permute-start.26 = (bf16[20,1280]{1,0:T(8,128)(2,1)S(1)}, bf16[20,1280]{1,0:T(8,128)(2,1)S(1)}, u32[]{:S(2)}, u32[]{:S(2)}) collective-permute-start(bf16[20,1280]{1,0:T(8,128)(2,1)S(1)} %get-tuple-element.93), channel_id=1, source_target_pairs={{0,32},{8,40},{16,48},{24,56},{32,0},{40,8},{48,16},{56,24},{1,33}... | collective-permute-start | bytes 153608 | tf_op jit(solution)/shard_map/ppermute | solution.py:28
  118.5 6.7 %collective-permute-start.28 = (bf16[20,1280]{1,0:T(8,128)(2,1)S(1)}, bf16[20,1280]{1,0:T(8,128)(2,1)S(1)}, u32[]{:S(2)}, u32[]{:S(2)}) collective-permute-start(bf16[20,1280]{1,0:T(8,128)(2,1)S(1)} %get-tuple-element.94), channel_id=1, source_target_pairs={{0,48},{8,56},{16,32},{24,40},{32,16},{40,24},{48,0},{56,8},{1,49}... | collective-permute-start | bytes 153608 | tf_op jit(solution)/shard_map/ppermute | solution.py:28
  121.0 5.1 %collective-permute-start.27 = (bf16[20,1280]{1,0:T(8,128)(2,1)S(1)}, bf16[20,1280]{1,0:T(8,128)(2,1)S(1)}, u32[]{:S(2)}, u32[]{:S(2)}) collective-permute-start(bf16[20,1280]{1,0:T(8,128)(2,1)S(1)} %get-tuple-element.95), channel_id=1, source_target_pairs={{0,16},{8,24},{16,0},{24,8},{32,48},{40,56},{48,32},{56,40},{1,17}... | collective-permute-start | bytes 153608 | tf_op jit(solution)/shard_map/ppermute | solution.py:28
Sparse Core Ops, SparseCore 0:
  98.2 22.2 reduce-scatter.1

commit v2 on v0

--- a/solution.py
+++ b/solution.py
@@ -80,7 +80,8 @@
 
 def grads_kernel(heads, valid_ref, *refs):
     rows_refs, frame_refs, stat_refs = refs[:4], refs[4:8], refs[8:12]
-    dkv_ref, dq_refs = refs[12], refs[13:17]
+    keep_refs, send_ref = refs[12:14], refs[14]
+    dq_refs = refs[15:19]
     width = heads * HD
     rows = jnp.concatenate([r[...] for r in rows_refs], axis=0)
     blocks = [r[...] for r in frame_refs]
@@ -112,9 +113,10 @@
             probs = probs.astype(BF)
             dkey = mm(dscores, query) * SCALE
             dvalue = mm(probs, dout)
-            span = slice(j * part, (j + 1) * part)
-            dkv_ref[span, cut] = dkey.astype(dkv_ref.dtype)
-            dkv_ref[span, cut2] = dvalue.astype(dkv_ref.dtype)
+            out_ref = send_ref if j % 2 else keep_refs[j // 2]
+            span = slice((j // 2) * part, (j // 2 + 1) * part) if j % 2 else slice(0, part)
+            out_ref[span, cut] = dkey.astype(out_ref.dtype)
+            out_ref[span, cut2] = dvalue.astype(out_ref.dtype)
             dq_sum += mm(key, dscores, TN)
             att_sum += mm(value, probs, TN)
         dq_t.append(dq_sum * SCALE)
@@ -122,6 +124,9 @@
     joined = jnp.concatenate(dq_t + att_t, axis=0).T
     for k in range(4):
         dq_refs[k][...] = joined[k * own : (k + 1) * own].astype(dq_refs[k].dtype)
+
+
+QUAD = (0, 2, 5, 7)
 
 
 def fetch(pairs, sems):
@@ -159,49 +164,55 @@
         out[:, side * width : (side + 1) * width] = mm(x[...], w[...], NT).astype(BF)
 
 
-def kv_weights_kernel(xt_ref, xt2_ref, xp_ref, xp2_ref, y_ref, y2_ref, *out_refs):
-    part = y_ref.shape[0] // 4
-    step = out_refs[0].shape[0]
-    sums = []
-    for j in range(4):
-        near = slice(j * part, (j + 1) * part)
-        far = slice((j ^ 1) * part, ((j ^ 1) + 1) * part)
-        total = y_ref[near].astype(F32) + y2_ref[far].astype(F32)
-        if j == 0:
-            out_refs[4][...] = total
-        sums.append(total.astype(BF))
-    out_refs[5][...] = sums[2]
-    for k in (2, 3, 1, 0):
+def collect_kernel(keep_ref, core_ref, pair_ref, dq_ref, a_ref, b_ref, c_ref, out_ref):
+    slab = keep_ref.shape[0]
+    total = keep_ref[...] + core_ref[:slab].astype(F32) + pair_ref[...].astype(F32)
+    out_ref[:slab] = total.astype(out_ref.dtype)
+    total = dq_ref[...] + a_ref[...].astype(F32) + b_ref[...].astype(F32)
+    out_ref[slab:] = (total + c_ref[...].astype(F32)).astype(out_ref.dtype)
+
+
+def weights_kernel(part, xt_ref, xt2_ref, y_ref, y2_ref, *out_refs):
+    kv_refs, keep_ref, send_ref = out_refs[:4], out_refs[4], out_refs[5]
+    frames = y_ref.shape[0] - part
+    half = y_ref.shape[1] // 2
+    step = kv_refs[0].shape[0]
+    pairs = ((xt_ref, y_ref), (xt2_ref, y2_ref))
+    for k in (3, 1, 2, 0):
         span = slice(k * step, (k + 1) * step)
-        total = mm(xt_ref[span, :part], sums[0]) + mm(xt2_ref[span, :part], sums[1])
-        total += mm(xp_ref[span], sums[2]) + mm(xp2_ref[span], sums[3])
-        out_refs[k][...] = total.astype(out_refs[k].dtype)
-
-
-def qo_weights_kernel(xt_ref, xt2_ref, y_ref, y2_ref, *out_refs):
-    own = y_ref.shape[0]
-    half = y_ref.shape[1] // 2
-    step = out_refs[0].shape[0]
-    first = xt_ref.shape[1] - 2 * own
-    for k in (2, 3, 1, 0):
-        span = slice(k * step, (k + 1) * step)
-        for side in (0, 1):
-            cols = slice(side * half, (side + 1) * half)
-            at = slice(first + side * own, first + (side + 1) * own)
-            total = mm(xt_ref[span, at], y_ref[:, cols]) + mm(xt2_ref[span, at], y2_ref[:, cols])
-            out_refs[k][:, cols] = total.astype(out_refs[k].dtype)
-
-
-def inputs_kernel(where_ref, near_ref, pair_ref, dq_ref, wk_ref, wv_ref, wq_ref, own_ref, *refs):
-    send_refs, scratch = refs[:3], refs[3]
-    width = wk_ref.shape[0]
-    part = near_ref.shape[0]
-    dkv = (near_ref[...] + pair_ref[...].astype(F32)).astype(BF)
-    dkey, dvalue, dquery = dkv[:, :width], dkv[:, width:], dq_ref[:, :width]
+        kv = sum(mm(x[span, :frames], y[:frames, :]) for x, y in pairs)
+        kv_refs[k][...] = kv.astype(kv_refs[k].dtype)
+        q = sum(
+            mm(x[span, frames : frames + part], y[frames:, :half]) for x, y in pairs
+        )
+        o = sum(mm(x[span, frames + part :], y[frames:, half:]) for x, y in pairs)
+        near = slice(k * step // 2, (k + 1) * step // 2)
+        keep_ref[near, :half] = q[: step // 2]
+        keep_ref[near, half:] = o[: step // 2]
+        send_ref[near, :half] = q[step // 2 :].astype(send_ref.dtype)
+        send_ref[near, half:] = o[step // 2 :].astype(send_ref.dtype)
+
+
+def inputs_kernel(where_ref, y_ref, wk_ref, wv_ref, wq_ref, own_ref, *refs):
+    send_refs, (scratch, wk, wv, wq, sems) = refs[:3], refs[3:]
+    width = wk.shape[0]
+    half = width // 2
+    pairs = []
+    for source, target in ((wk_ref, wk), (wv_ref, wv), (wq_ref, wq)):
+        pairs += [
+            (source.at[:half], target.at[:half]),
+            (source.at[half:], target.at[half:]),
+        ]
+    copies = fetch(pairs, sems)
+    part = y_ref.shape[0] // 5 * 4
+    dkey, dvalue = y_ref[:part, :width], y_ref[:part, width:]
+    dquery = y_ref[part:, :width]
+    for copy in copies:
+        copy.wait()
     for t in range(4):
         span = slice(t * width, (t + 1) * width)
-        scratch[t, :part] = mm(dkey, wk_ref[:, span]) + mm(dvalue, wv_ref[:, span])
-        scratch[t, part:] = mm(dquery, wq_ref[:, span])
+        scratch[t, :part] = mm(dkey, wk[:, span]) + mm(dvalue, wv[:, span])
+        scratch[t, part:] = mm(dquery, wq[:, span])
     own_ref[...] = scratch[where_ref[0]]
     for k in (1, 2, 3):
         send_refs[k - 1][...] = scratch[where_ref[0] ^ k].astype(BF)
@@ -234,7 +245,7 @@
             scratch_shapes=scratch,
             compiler_params=pltpu.CompilerParams(vmem_limit_bytes=24 * 1024 * 1024),
             cost_estimate=pl.CostEstimate(
-                flops=int(work * 1e9), bytes_accessed=0, transcendentals=0
+                flops=work, bytes_accessed=0, transcendentals=0
             ),
         )(*ins)
 
@@ -256,27 +267,27 @@
 
     kv_pair = flip(kv, "z", 8, 1)
     kv_core = swap(kv, "core")
-    row_blocks = [rows0] + [flip(rows0, "z", 8, 2 * j) for j in (1, 2, 3)]
-
-    def turn(stacked, other):
-        place = jnp.arange(model, dtype=jnp.int32)
+    rows0, kv_core = lax.optimization_barrier((rows0, kv_core))
+    row_blocks = [rows0] + [flip(rows0, "z", 8, QUAD[j]) for j in (1, 2, 3)]
+
+    def turn(stacked, c_rel):
+        place = jnp.arange(model // 2, dtype=jnp.int32)
         unit, rest = place % inner, place // inner
-        a_rel, b_rel = rest % 4, ((rest // 4) % 2) ^ other
-        x_rel, c_rel = (rest // 8) % 4, rest // 32
+        a_rel, b_rel = rest % 4, (rest // 4) % 2
+        x_rel = rest // 8
         target = (
-            (x_rel ^ xi) * 16 + ((2 * a_rel + b_rel) ^ zi) * 2 + (c_rel ^ ci)
+            (x_rel ^ xi) * 16 + ((2 * (a_rel % 2)) ^ (5 * (a_rel // 2)) ^ b_rel ^ zi) * 2 + (c_rel ^ ci)
         ) * inner + unit
-        pick = (place[:, None] == target[None, :]).astype(BF)
-        return mm(pick, stacked, (((0,), (1,)), ((), ()))).astype(BF)
-
-    turned = turn(jnp.concatenate([frames, rows_in, rows_grad], axis=0), 0)
-    for_pair = turn(frames, 1)
-    row_blocks[1:], kv_pair, kv_core, for_pair, turned = lax.optimization_barrier(
-        (row_blocks[1:], kv_pair, kv_core, for_pair, turned)
-    )
-    xt, xt_other = turned[: model // 2], swap(turned[model // 2 :], "core")
+        pick = (jnp.arange(model, dtype=jnp.int32)[None, :] == target[:, None]).astype(BF)
+        return mm(pick, stacked, NT).astype(BF)
+
+    stacked = jnp.concatenate([frames, rows_in, rows_grad], axis=0)
+    xt, xt_send = turn(stacked, 0), turn(stacked, 1)
+    row_blocks[1:], kv_pair, kv_core, xt, xt_send = lax.optimization_barrier(
+        (row_blocks[1:], kv_pair, kv_core, xt, xt_send)
+    )
+    xt_other = swap(xt_send, "core")
     frame_blocks = [kv, kv_core, kv_pair, swap(kv_pair, "core")]
-    from_pair = flip(for_pair, "z", 8, 1)
     starts = [
         slab * (2 * (zi ^ db) + (ci ^ dc)) for db in (0, 1) for dc in (0, 1)
     ]
@@ -287,66 +298,72 @@
         [((16, 4 * own), F32)],
         (valid, *row_blocks, *frame_blocks),
         True,
-        work=3,
-    )
-    all_stats = [stats] + [flip(stats, "z", 8, 2 * j) for j in (1, 2, 3)]
-
-    all_stats[1:], from_pair, xt_other = lax.optimization_barrier(
-        (all_stats[1:], from_pair, xt_other)
-    )
-    xp, xp_other = from_pair[: model // 2], swap(from_pair[model // 2 :], "core")
-
-    dkv, dq0, *dq_sends = call(
+    )
+    all_stats = [stats] + [flip(stats, "z", 8, QUAD[j]) for j in (1, 2, 3)]
+
+    all_stats[1:], xt_other = lax.optimization_barrier((all_stats[1:], xt_other))
+
+    keep0, keep1, send, dq0, *dq_sends = call(
         functools.partial(grads_kernel, heads),
-        [((4 * slab, 2 * width), BF), ((own, 2 * width), F32)]
+        [((slab, 2 * width), F32)] * 2
+        + [((2 * slab, 2 * width), BF), ((own, 2 * width), F32)]
         + [((own, 2 * width), BF)] * 3,
         (valid, *row_blocks, *frame_blocks, *all_stats),
         True,
-        work=8,
-    )
-
-    dkv_other = swap(dkv, "core")
-    dq_recv = [flip(d, "z", 8, 2 * k) for k, d in zip((1, 2, 3), dq_sends)]
+    )
+
+    recv = swap(send, "core")
+    pair = (keep1 + recv[slab:].astype(F32)).astype(BF)
+    dq_sends, pair = lax.optimization_barrier((dq_sends, pair))
+    pair_recv = flip(pair, "z", 8, 1)
+    dq_recv = [flip(d, "z", 8, QUAD[k]) for k, d in zip((1, 2, 3), dq_sends)]
+    (grads,) = call(
+        collect_kernel,
+        [((slab + own, 2 * width), BF)],
+        (keep0, recv, pair_recv, dq0, *dq_recv),
+    )
+    grads_other = swap(grads, "core")
 
     part = model // 8
-    kv_own, *kv_sends, near, pair = call(
-        kv_weights_kernel,
+    kv_own, *kv_sends, qo_keep, qo_send = call(
+        functools.partial(weights_kernel, own),
         [((part, 2 * width), F32)]
         + [((part, 2 * width), BF)] * 3
-        + [((slab, 2 * width), F32), ((slab, 2 * width), BF)],
-        (xt, xt_other, xp, xp_other, dkv, dkv_other),
+        + [((2 * part, 2 * width), F32), ((2 * part, 2 * width), BF)],
+        (xt, xt_other, grads, grads_other),
     )
     kv_x = [flip(kv_sends[k - 1], "dp", 4, k) for k in (2, 1, 3)]
-    pair_recv = flip(pair, "z", 8, 1)
-
-    dq_recv, kv_own = lax.optimization_barrier((dq_recv, kv_own))
-    dqo = (dq0 + sum(d.astype(F32) for d in dq_recv)).astype(BF)
-    dqo_other = swap(dqo, "core")
-    qo_own, *qo_sends = call(
-        qo_weights_kernel,
-        [((part, 2 * width), F32)] + [((part, 2 * width), BF)] * 3,
-        (xt, xt_other, dqo, dqo_other),
-    )
-    qo_x = [flip(qo_sends[k - 1], "dp", 4, k) for k in (2, 1, 3)]
-
-    own_part, *sends = call(
+    qo_b = flip(qo_send, "z", 8, 1)
+
+    held, kv_own = lax.optimization_barrier((grads, kv_own))
+    own_part, *sends = pl.pallas_call(
         inputs_kernel,
-        [((slab + own, width), F32)] + [((slab + own, width), BF)] * 3,
-        (where, near, pair_recv, dqo, wk_t, wv_t, wq_t),
-        True,
-        [pltpu.VMEM((4, slab + own, width), F32)],
-    )
+        out_shape=[jax.ShapeDtypeStruct((slab + own, width), F32)]
+        + [jax.ShapeDtypeStruct((slab + own, width), BF)] * 3,
+        in_specs=[SMEM, VMEM] + [pl.BlockSpec(memory_space=pltpu.HBM)] * 3,
+        out_specs=[VMEM] * 4,
+        scratch_shapes=[pltpu.VMEM((4, slab + own, width), F32)]
+        + weights[:3]
+        + [pltpu.SemaphoreType.DMA((6,))],
+        compiler_params=pltpu.CompilerParams(vmem_limit_bytes=24 * 1024 * 1024),
+        cost_estimate=pl.CostEstimate(
+            flops=12_000_000_000, bytes_accessed=0, transcendentals=0
+        ),
+    )(where, held, wk_t, wv_t, wq_t)
     arrived = [flip(sends[k - 1], "head", 4, k) for k in (2, 1, 3)]
     inputs = (own_part + sum(p.astype(F32) for p in arrived)).astype(BF)
     dframes, dinput = inputs[:slab], inputs[slab:]
 
+    cut = part // 2
     kv_sum = kv_own + sum(k.astype(F32) for k in kv_x)
-    qo_sum = qo_own + sum(k.astype(F32) for k in qo_x)
+    kv_b = flip(kv_sum[cut:].astype(BF), "z", 8, 1)
+    qo_sum = qo_keep + qo_b.astype(F32)
+    qo_x = [flip(qo_sum[k * cut : (k + 1) * cut].astype(BF), "dp", 4, k) for k in (2, 1, 3)]
+    kv_sum = kv_sum[:cut] + kv_b.astype(F32)
+    qo_sum = qo_sum[:cut] + sum(q.astype(F32) for q in qo_x)
     total = jnp.concatenate([kv_sum, qo_sum], axis=1)
-    cut = part // 2
-    total = total[:cut] + flip(total[cut:].astype(BF), "z", 8, 1).astype(F32)
     low = total.astype(BF)
-    over = [flip(low[k * inner : (k + 1) * inner], "z", 8, 2 * k) for k in (2, 1, 3)]
+    over = [flip(low[k * inner : (k + 1) * inner], "z", 8, QUAD[k]) for k in (2, 1, 3)]
     total = total[:inner] + sum(p.astype(F32) for p in over)
     return (
         dinput[None],

time: 114 us -> 110 us (0.965)
  waiting for transfers between devices: 38.4 us -> 34.8 us
  local copies, waits for them, and re-layouts: 4.33 us -> 2.29 us
  starting transfers between devices: 47.7 us -> 49.3 us
    ppermute x31 -> x30, waiting for transfers between devices: 38.4 us -> 34.8 us  [flip(): return lax.ppermute(x, axis, [(i, i ^ bits) for i in range(size)])]
    pallas_call x0 -> x1, Pallas kernels: none -> 2.76 us  [per_device(): pl.pallas_call(inputs_kernel, out_shape=[jax.ShapeDtypeStruct((slab + own...]
    pallas_call x5 -> x4, Pallas kernels: 12.3 us -> 10.3 us  [call(): pl.pallas_call(kernel, out_shape=shapes, in_specs=specs, out_specs=[VMEM]...]
    ppermute x31 -> x30, starting transfers between devices: 47.7 us -> 49.3 us  [flip(): return lax.ppermute(x, axis, [(i, i ^ bits) for i in range(size)])]
    unnamed x29 -> x17, local copies, waits for them, and re-layouts: 1.99 us -> 0.84 us
  transfers between devices with their start and end apart: 31 -> 30, of which waited for: 13 -> 17; matrix products, arithmetic and copies ran while one was open for 7% -> 4% of each run, Pallas kernels for 5% -> 5%
where the time goes in v2:
time: 110 us; the launch traced here: 109 us
  starting transfers between devices  49.3 us (45%)
  waiting for transfers between devices  34.8 us (32%)
  Pallas kernels  17.4 us (16%)
  matrix products  2.91 us (3%)
  local copies, waits for them, and re-layouts  2.29 us (2%)
  between operations  1.53 us (1%)
    ppermute x30, starting transfers between devices, flip(): return lax.ppermute(x, axis, [(i, i ^ bits) for i in range(size)])  49.3 us
    ppermute x30, waiting for transfers between devices, flip(): return lax.ppermute(x, axis, [(i, i ^ bits) for i in range(size)])  34.8 us
    pallas_call x4, Pallas kernels, call(): pl.pallas_call(kernel, out_shape=shapes, in_specs=specs, out_specs=[VMEM]...  10.3 us
    pallas_call x1, Pallas kernels, per_device(): pl.pallas_call(project_kernel, out_shape=[jax.ShapeDtypeStruct((own, 2 *...  4.34 us
    dot_general x2, matrix products, mm(): return lax.dot_general(left, right, dims, preferred_element_type=F32)  2.91 us
    pallas_call x1, Pallas kernels, per_device(): pl.pallas_call(inputs_kernel, out_shape=[jax.ShapeDtypeStruct((slab + own...  2.76 us
  transfers between devices with their start and end apart: 30, of which 17 were waited for; matrix products, arithmetic and copies ran while one was open for 4% of the time, Pallas kernels for 5%

profile of v2, /device:TPU:8, one launch (start us, length us, event | category | flops | bytes accessed | tf_op | source)
XLA Modules:
  0.0 108.9 jit_solution(847491136343418244)
XLA Ops:
  0.7 4.3 %shard_map.127 = (bf16[64,640]{1,0:T(8,128)(2,1)}, bf16[256,640]{1,0:T(8,128)(2,1)}) custom-call(bf16[64,1280]{1,0:T(8,128)(2,1)} %bitcast.31, bf16[64,1280]{1,0:T(8,128)(2,1)} %bitcast.34, bf16[256,1280]{1,0:T(8,128)(2,1)} %bitcast.28, bf16[320,1280]{1,0:T(8,128)(2,1)} %bitcast.22, bf16[320,1280]{1,0:T(8,128)(2,1)} %wo_ref.1, bf16[320,1280]{1,0:T(8,128)(2,1)} %bitcast.24, ...), custom_call_target="tpu_custom_call" | custom-call | tf_op jit(solution)/shard_map/pallas_call | solution.py:254
  5.0 2.0 %collective-permute-start.4 = (bf16[256,640]{1,0:T(8,128)(2,1)}, bf16[256,640]{1,0:T(8,128)(2,1)S(1)}, u32[]{:S(2)}, u32[]{:S(2)}) collective-permute-start(bf16[256,640]{1,0:T(8,128)(2,1)} %get-tuple-element.45.refs_4_), channel_id=1, source_target_pairs={{0,8},{8,0},{16,24},{24,16},{32,40},{40,32},{48,56},{56,48},{1,9},... | collective-permute-start | bytes 983048 | tf_op jit(solution)/shard_map/ppermute | solution.py:28
  7.1 1.1 fusion.5.xt_ref
  8.2 0.7 collective-permute-done.refs_5_
  8.9 4.9 %collective-permute-start.3 = (bf16[64,640]{1,0:T(8,128)(2,1)S(1)}, bf16[64,640]{1,0:T(8,128)(2,1)S(1)}, u32[]{:S(2)}, u32[]{:S(2)}) collective-permute-start(bf16[64,640]{1,0:T(8,128)(2,1)S(1)} %copy-done.4), channel_id=1, source_target_pairs={{0,56},{8,48},{16,40},{24,32},{32,24},{40,16},{48,8},{56,0},{1,57}... | collective-permute-start | bytes 245768 | tf_op jit(solution)/shard_map/ppermute | solution.py:28
  13.8 1.9 %collective-permute-start.2 = (bf16[64,640]{1,0:T(8,128)(2,1)S(1)}, bf16[64,640]{1,0:T(8,128)(2,1)S(1)}, u32[]{:S(2)}, u32[]{:S(2)}) collective-permute-start(bf16[64,640]{1,0:T(8,128)(2,1)S(1)} %copy-done.4), channel_id=1, source_target_pairs={{0,40},{8,32},{16,56},{24,48},{32,8},{40,0},{48,24},{56,16},{1,41}... | collective-permute-start | bytes 245768 | tf_op jit(solution)/shard_map/ppermute | solution.py:28
  16.2 1.8 %fusion.4 = bf16[640,384]{1,0:T(8,128)(2,1)} fusion(s32[640]{0:T(1024)S(1)} %get-tuple-element.100, bf16[64,1280]{1,0:T(8,128)(2,1)S(1)} %bitcast.36, bf16[64,1280]{1,0:T(8,128)(2,1)S(1)} %bitcast.33, bf16[256,1280]{1,0:T(8,128)(2,1)S(1)} %bitcast.30), kind=kOutput, calls=%fused_computation.6 | convolution fusion | flops 633159680 | bytes 1477120 | tf_op jit(solution)/shard_map/dot_general | solution.py:24
  18.0 1.5 %collective-permute-done.3.refs_3_ = bf16[64,640]{1,0:T(8,128)(2,1)S(1)} collective-permute-done((bf16[64,640]{1,0:T(8,128)(2,1)S(1)}, bf16[64,640]{1,0:T(8,128)(2,1)S(1)}, u32[]{:S(2)}, u32[]{:S(2)}) %collective-permute-start.3) | collective-permute-done | bytes 81952 | tf_op jit(solution)/shard_map/ppermute | solution.py:28
  19.5 2.9 %collective-permute-done.2.refs_2_ = bf16[64,640]{1,0:T(8,128)(2,1)S(1)} collective-permute-done((bf16[64,640]{1,0:T(8,128)(2,1)S(1)}, bf16[64,640]{1,0:T(8,128)(2,1)S(1)}, u32[]{:S(2)}, u32[]{:S(2)}) %collective-permute-start.2) | collective-permute-done | bytes 81952 | tf_op jit(solution)/shard_map/ppermute | solution.py:28
  22.4 0.5 collective-permute-start.5
  23.6 0.9 collective-permute-done.5.refs_7_
  24.5 2.5 %shard_map.128.refs_8_ = f32[16,256]{1,0:T(8,128)S(1)} custom-call(s32[4]{0:T(128)S(1)} %pad_add_fusion.valid_ref, bf16[64,640]{1,0:T(8,128)(2,1)S(1)} %copy-done.4, bf16[64,640]{1,0:T(8,128)(2,1)S(1)} %collective-permute-done.1.refs_1_, bf16[64,640]{1,0:T(8,128)(2,1)S(1)} %collective-permute-done.2.refs_2_, ...), custom_call_target="tpu_custom_call" | custom-call | flops 2 | tf_op jit(solution)/shard_map/pallas_call | solution.py:240
  27.0 4.6 %collective-permute-start.8 = (f32[16,256]{1,0:T(8,128)S(1)}, f32[16,256]{1,0:T(8,128)S(1)}, u32[]{:S(2)}, u32[]{:S(2)}) collective-permute-start(f32[16,256]{1,0:T(8,128)S(1)} %shard_map.128.refs_8_), channel_id=1, source_target_pairs={{0,56},{8,48},{16,40},{24,32},{32,24},{40,16},{48,8},{56,0},{1,57}... | collective-permute-start | bytes 49160 | tf_op jit(solution)/shard_map/ppermute | solution.py:28
  31.6 3.8 %collective-permute-start.7 = (f32[16,256]{1,0:T(8,128)S(1)}, f32[16,256]{1,0:T(8,128)S(1)}, u32[]{:S(2)}, u32[]{:S(2)}) collective-permute-start(f32[16,256]{1,0:T(8,128)S(1)} %shard_map.128.refs_8_), channel_id=1, source_target_pairs={{0,40},{8,32},{16,56},{24,48},{32,8},{40,0},{48,24},{56,16},{1,41}... | collective-permute-start | bytes 49160 | tf_op jit(solution)/shard_map/ppermute | solution.py:28
  35.4 2.9 %collective-permute-done.7.refs_10_ = f32[16,256]{1,0:T(8,128)S(1)} collective-permute-done((f32[16,256]{1,0:T(8,128)S(1)}, f32[16,256]{1,0:T(8,128)S(1)}, u32[]{:S(2)}, u32[]{:S(2)}) %collective-permute-start.7) | collective-permute-done | bytes 16416 | tf_op jit(solution)/shard_map/ppermute | solution.py:28
  38.3 1.7 %collective-permute-done.6.refs_9_ = f32[16,256]{1,0:T(8,128)S(1)} collective-permute-done((f32[16,256]{1,0:T(8,128)S(1)}, f32[16,256]{1,0:T(8,128)S(1)}, u32[]{:S(2)}, u32[]{:S(2)}) %collective-permute-start.6) | collective-permute-done | bytes 16416 | tf_op jit(solution)/shard_map/ppermute | solution.py:28
  40.1 6.4 %shard_map.129 = (f32[256,640]{1,0:T(8,128)S(1)}, f32[256,640]{1,0:T(8,128)S(1)}, bf16[512,640]{1,0:T(8,128)(2,1)S(1)}, f32[64,640]{1,0:T(8,128)S(1)}, bf16[64,6...) custom-call(s32[4]{0:T(128)S(1)} %pad_add_fusion.valid_ref, ...), custom_call_target="tpu_custom_call" | custom-call | flops 2 | tf_op jit(solution)/shard_map/pallas_call | solution.py:240
  46.5 2.1 %collective-permute-done.10.core_ref = bf16[512,640]{1,0:T(8,128)(2,1)S(1)} collective-permute-done((bf16[512,640]{1,0:T(8,128)(2,1)S(1)}, bf16[512,640]{1,0:T(8,128)(2,1)S(1)}, u32[]{:S(2)}, u32[]{:S(2)}) %collective-permute-start.10) | collective-permute-done | bytes 655392 | tf_op jit(solution)/shard_map/ppermute | solution.py:28
  48.8 2.4 %collective-permute-start.12 = (bf16[64,640]{1,0:T(8,128)(2,1)S(1)}, bf16[64,640]{1,0:T(8,128)(2,1)S(1)}, u32[]{:S(2)}, u32[]{:S(2)}) collective-permute-start(bf16[64,640]{1,0:T(8,128)(2,1)S(1)} %get-tuple-element.65), channel_id=1, source_target_pairs={{0,16},{8,24},{16,0},{24,8},{32,48},{40,56},{48,32},{56,40},{1,17}... | collective-permute-start | bytes 245768 | tf_op jit(solution)/shard_map/ppermute | solution.py:28
  51.2 2.1 %collective-permute-start.13 = (bf16[64,640]{1,0:T(8,128)(2,1)S(1)}, bf16[64,640]{1,0:T(8,128)(2,1)S(1)}, u32[]{:S(2)}, u32[]{:S(2)}) collective-permute-start(bf16[64,640]{1,0:T(8,128)(2,1)S(1)} %get-tuple-element.66), channel_id=1, source_target_pairs={{0,40},{8,32},{16,56},{24,48},{32,8},{40,0},{48,24},{56,16},{1,41}... | collective-permute-start | bytes 245768 | tf_op jit(solution)/shard_map/ppermute | solution.py:28
  53.3 1.2 %collective-permute-start.14 = (bf16[64,640]{1,0:T(8,128)(2,1)S(1)}, bf16[64,640]{1,0:T(8,128)(2,1)S(1)}, u32[]{:S(2)}, u32[]{:S(2)}) collective-permute-start(bf16[64,640]{1,0:T(8,128)(2,1)S(1)} %get-tuple-element.67), channel_id=1, source_target_pairs={{0,56},{8,48},{16,40},{24,32},{32,24},{40,16},{48,8},{56,0},{1,57}... | collective-permute-start | bytes 245768 | tf_op jit(solution)/shard_map/ppermute | solution.py:28
  54.5 5.4 %collective-permute-done.12.a_ref = bf16[64,640]{1,0:T(8,128)(2,1)S(1)} collective-permute-done((bf16[64,640]{1,0:T(8,128)(2,1)S(1)}, bf16[64,640]{1,0:T(8,128)(2,1)S(1)}, u32[]{:S(2)}, u32[]{:S(2)}) %collective-permute-start.12) | collective-permute-done | bytes 81952 | tf_op jit(solution)/shard_map/ppermute | solution.py:28
  59.9 0.6 collective-permute-done.14.c_ref
  60.4 2.4 %collective-permute-done.11.pair_ref = bf16[256,640]{1,0:T(8,128)(2,1)S(1)} collective-permute-done((bf16[256,640]{1,0:T(8,128)(2,1)S(1)}, bf16[256,640]{1,0:T(8,128)(2,1)S(1)}, u32[]{:S(2)}, u32[]{:S(2)}) %collective-permute-start.11) | collective-permute-done | bytes 327712 | tf_op jit(solution)/shard_map/ppermute | solution.py:28
  63.1 1.7 %collective-permute-done.15.y2_ref = bf16[320,640]{1,0:T(8,128)(2,1)S(1)} collective-permute-done((bf16[320,640]{1,0:T(8,128)(2,1)S(1)}, bf16[320,640]{1,0:T(8,128)(2,1)S(1)}, u32[]{:S(2)}, u32[]{:S(2)}) %collective-permute-start.15) | collective-permute-done | bytes 409632 | tf_op jit(solution)/shard_map/ppermute | solution.py:28
  64.9 1.3 %shard_map.131 = (f32[160,640]{1,0:T(8,128)S(1)}, bf16[160,640]{1,0:T(8,128)(2,1)S(1)}, bf16[160,640]{1,0:T(8,128)(2,1)S(1)}, bf16[160,640]{1,0:T(8,128)(2,1)S(1...) custom-call(bf16[640,384]{1,0:T(8,128)(2,1)S(1)} %fusion.5.xt_ref, ...), custom_call_target="tpu_custom_call" | custom-call | flops 2 | tf_op jit(solution)/shard_map/pallas_call | solution.py:240
  66.2 3.1 %collective-permute-start.19 = (bf16[160,640]{1,0:T(8,128)(2,1)S(1)}, bf16[160,640]{1,0:T(8,128)(2,1)S(1)}, u32[]{:S(2)}, u32[]{:S(2)}) collective-permute-start(bf16[160,640]{1,0:T(8,128)(2,1)S(1)} %get-tuple-element.77), channel_id=1, source_target_pairs={{0,128},{64,192},{128,0},{192,64},{1,129},{65,193},{129,1},{193,65... | collective-permute-start | bytes 614408 | tf_op jit(solution)/shard_map/ppermute | solution.py:28
  69.3 0.6 collective-permute-start.20
  69.9 0.5 collective-permute-start.21
  70.4 2.5 %collective-permute-start.23 = (bf16[320,640]{1,0:T(8,128)(2,1)S(1)}, bf16[320,640]{1,0:T(8,128)(2,1)S(1)}, u32[]{:S(2)}, u32[]{:S(2)}) collective-permute-start(bf16[320,640]{1,0:T(8,128)(2,1)S(1)} %get-tuple-element.81), channel_id=1, source_target_pairs={{0,8},{8,0},{16,24},{24,16},{32,40},{40,32},{48,56},{56,48},{1,9},... | collective-permute-start | bytes 1228808 | tf_op jit(solution)/shard_map/ppermute | solution.py:28
  73.0 2.8 %shard_map.132 = (f32[320,320]{1,0:T(8,128)S(1)}, bf16[320,320]{1,0:T(8,128)(2,1)S(1)}, bf16[320,320]{1,0:T(8,128)(2,1)S(1)}, bf16[320,320]{1,0:T(8,128)(2,1)S(1)}) custom-call(s32[1]{0:T(128)} %bitcast.where_ref, bf16[320,640]{1,0:T(8,128)(2,1)S(1)} %shard_map.130.y_ref, bf16[320,1280]{1,0:T(8,128)(2,1)S(1)} %bitcast.25, bf16[320,1280]{1,0:T(8,128)(2,1)S(1)} %bitcast.27, ...), custom_call_target="tpu_custom_call" | custom-call | flops 12000000000 | tf_op jit(solution)/shard_map/pallas_call | solution.py:339
  75.7 2.4 %collective-permute-start.16 = (bf16[320,320]{1,0:T(8,128)(2,1)S(1)}, bf16[320,320]{1,0:T(8,128)(2,1)S(1)}, u32[]{:S(2)}, u32[]{:S(2)}) collective-permute-start(bf16[320,320]{1,0:T(8,128)(2,1)S(1)} %get-tuple-element.73), channel_id=1, source_target_pairs={{0,2},{1,3},{2,0},{3,1},{4,6},{5,7},{6,4},{7,5},{8,10},{9,11},{10,... | collective-permute-start | bytes 614408 | tf_op jit(solution)/shard_map/ppermute | solution.py:28
  78.1 1.3 %collective-permute-start.17 = (bf16[320,320]{1,0:T(8,128)(2,1)S(1)}, bf16[320,320]{1,0:T(8,128)(2,1)S(1)}, u32[]{:S(2)}, u32[]{:S(2)}) collective-permute-start(bf16[320,320]{1,0:T(8,128)(2,1)S(1)} %get-tuple-element.74), channel_id=1, source_target_pairs={{0,1},{1,0},{2,3},{3,2},{4,5},{5,4},{6,7},{7,6},{8,9},{9,8},{10,11... | collective-permute-start | bytes 614408 | tf_op jit(solution)/shard_map/ppermute | solution.py:28
  79.5 1.5 %collective-permute-start.18 = (bf16[320,320]{1,0:T(8,128)(2,1)S(1)}, bf16[320,320]{1,0:T(8,128)(2,1)S(1)}, u32[]{:S(2)}, u32[]{:S(2)}) collective-permute-start(bf16[320,320]{1,0:T(8,128)(2,1)S(1)} %get-tuple-element.75), channel_id=1, source_target_pairs={{0,3},{1,2},{2,1},{3,0},{4,7},{5,6},{6,5},{7,4},{8,11},{9,10},{10,... | collective-permute-start | bytes 614408 | tf_op jit(solution)/shard_map/ppermute | solution.py:28
  81.1 2.6 %collective-permute-start.22 = (bf16[80,640]{1,0:T(8,128)(2,1)S(1)}, bf16[80,640]{1,0:T(8,128)(2,1)S(1)}, u32[]{:S(2)}, u32[]{:S(2)}) collective-permute-start(bf16[80,640]{1,0:T(8,128)(2,1)S(1)} %slice.105), channel_id=1, source_target_pairs={{0,8},{8,0},{16,24},{24,16},{32,40},{40,32},{48,56},{56,48},{1,9},... | collective-permute-start | bytes 307208 | tf_op jit(solution)/shard_map/ppermute | solution.py:28
  83.7 2.5 %collective-permute-done.16 = bf16[320,320]{1,0:T(8,128)(2,1)S(1)} collective-permute-done((bf16[320,320]{1,0:T(8,128)(2,1)S(1)}, bf16[320,320]{1,0:T(8,128)(2,1)S(1)}, u32[]{:S(2)}, u32[]{:S(2)}) %collective-permute-start.16) | collective-permute-done | bytes 204832 | tf_op jit(solution)/shard_map/ppermute | solution.py:28
  86.2 3.6 %collective-permute-done.17 = bf16[320,320]{1,0:T(8,128)(2,1)S(1)} collective-permute-done((bf16[320,320]{1,0:T(8,128)(2,1)S(1)}, bf16[320,320]{1,0:T(8,128)(2,1)S(1)}, u32[]{:S(2)}, u32[]{:S(2)}) %collective-permute-start.17) | collective-permute-done | bytes 204832 | tf_op jit(solution)/shard_map/ppermute | solution.py:28
  90.2 2.8 %collective-permute-start.24 = (bf16[80,640]{1,0:T(8,128)(2,1)S(1)}, bf16[80,640]{1,0:T(8,128)(2,1)S(1)}, u32[]{:S(2)}, u32[]{:S(2)}) collective-permute-start(bf16[80,640]{1,0:T(8,128)(2,1)S(1)} %get-tuple-element.90), channel_id=1, source_target_pairs={{0,128},{64,192},{128,0},{192,64},{1,129},{65,193},{129,1},{193,65... | collective-permute-start | bytes 307208 | tf_op jit(solution)/shard_map/ppermute | solution.py:28
  93.0 1.1 %collective-permute-start.26 = (bf16[80,640]{1,0:T(8,128)(2,1)S(1)}, bf16[80,640]{1,0:T(8,128)(2,1)S(1)}, u32[]{:S(2)}, u32[]{:S(2)}) collective-permute-start(bf16[80,640]{1,0:T(8,128)(2,1)S(1)} %get-tuple-element.91), channel_id=1, source_target_pairs={{0,192},{64,128},{128,64},{192,0},{1,193},{65,129},{129,65},{193,1... | collective-permute-start | bytes 307208 | tf_op jit(solution)/shard_map/ppermute | solution.py:28
  94.1 2.4 %collective-permute-done.24 = bf16[80,640]{1,0:T(8,128)(2,1)S(1)} collective-permute-done((bf16[80,640]{1,0:T(8,128)(2,1)S(1)}, bf16[80,640]{1,0:T(8,128)(2,1)S(1)}, u32[]{:S(2)}, u32[]{:S(2)}) %collective-permute-start.24) | collective-permute-done | bytes 102432 | tf_op jit(solution)/shard_map/ppermute | solution.py:28
  96.5 2.4 %collective-permute-done.26 = bf16[80,640]{1,0:T(8,128)(2,1)S(1)} collective-permute-done((bf16[80,640]{1,0:T(8,128)(2,1)S(1)}, bf16[80,640]{1,0:T(8,128)(2,1)S(1)}, u32[]{:S(2)}, u32[]{:S(2)}) %collective-permute-start.26) | collective-permute-done | bytes 102432 | tf_op jit(solution)/shard_map/ppermute | solution.py:28
  99.0 3.0 %collective-permute-start.27 = (bf16[20,1280]{1,0:T(8,128)(2,1)S(1)}, bf16[20,1280]{1,0:T(8,128)(2,1)S(1)}, u32[]{:S(2)}, u32[]{:S(2)}) collective-permute-start(bf16[20,1280]{1,0:T(8,128)(2,1)S(1)} %get-tuple-element.93), channel_id=1, source_target_pairs={{0,40},{8,32},{16,56},{24,48},{32,8},{40,0},{48,24},{56,16},{1,41}... | collective-permute-start | bytes 153608 | tf_op jit(solution)/shard_map/ppermute | solution.py:28
  102.0 0.6 collective-permute-start.29
  102.6 3.0 %collective-permute-start.28 = (bf16[20,1280]{1,0:T(8,128)(2,1)S(1)}, bf16[20,1280]{1,0:T(8,128)(2,1)S(1)}, u32[]{:S(2)}, u32[]{:S(2)}) collective-permute-start(bf16[20,1280]{1,0:T(8,128)(2,1)S(1)} %get-tuple-element.95), channel_id=1, source_target_pairs={{0,16},{8,24},{16,0},{24,8},{32,48},{40,56},{48,32},{56,40},{1,17}... | collective-permute-start | bytes 153608 | tf_op jit(solution)/shard_map/ppermute | solution.py:28
  105.6 0.6 slice_bitcast_fusion.1
  106.2 0.8 copy.14
  107.0 1.0 collective-permute-done.29
  108.2 0.7 slice_bitcast_fusion.2
  (53 shorter events, 1.9 us)
Async XLA Ops:
  0.6 6.4 %copy-start.5 = (bf16[1,256,1280]{2,1,0:T(8,128)(2,1)S(1)}, bf16[1,256,1280]{2,1,0:T(8,128)(2,1)}, u32[]{:S(2)}) copy-start(bf16[1,256,1280]{2,1,0:T(8,128)(2,1)} %param.10) | copy-start | bytes 1966084
  0.6 6.4 %copy-start.6 = (bf16[1,64,1280]{2,1,0:T(8,128)(2,1)S(1)}, bf16[1,64,1280]{2,1,0:T(8,128)(2,1)}, u32[]{:S(2)}) copy-start(bf16[1,64,1280]{2,1,0:T(8,128)(2,1)} %param.8) | copy-start | bytes 491524
  0.7 6.4 %copy-start.7 = (bf16[1,64,1280]{2,1,0:T(8,128)(2,1)S(1)}, bf16[1,64,1280]{2,1,0:T(8,128)(2,1)}, u32[]{:S(2)}) copy-start(bf16[1,64,1280]{2,1,0:T(8,128)(2,1)} %param.9) | copy-start | bytes 491524
  5.0 13.0 %collective-permute-start.4 = (bf16[256,640]{1,0:T(8,128)(2,1)}, bf16[256,640]{1,0:T(8,128)(2,1)S(1)}, u32[]{:S(2)}, u32[]{:S(2)}) collective-permute-start(bf16[256,640]{1,0:T(8,128)(2,1)} %get-tuple-element.45.refs_4_), channel_id=1, source_target_pairs={{0,8},{8,0},{16,24},{24,16},{32,40},{40,32},{48,56},{56,48},{1,9},... | collective-permute-start | bytes 983048 | tf_op jit(solution)/shard_map/ppermute | solution.py:28
  7.0 1.8 %collective-permute-start = (bf16[256,640]{1,0:T(8,128)(2,1)}, bf16[256,640]{1,0:T(8,128)(2,1)S(1)}, u32[]{:S(2)}, u32[]{:S(2)}) collective-permute-start(bf16[256,640]{1,0:T(8,128)(2,1)} %get-tuple-element.45.refs_4_), channel_id=1, source_target_pairs={{0,4},{4,0},{1,5},{5,1},{2,6},{6,2},{3,7},{7,3},{8,12},{12,8},{9,1... | collective-permute-start | bytes 983048 | tf_op jit(solution)/shard_map/ppermute | solution.py:28
  7.1 1.8 %copy-start.4 = (bf16[64,640]{1,0:T(8,128)(2,1)S(1)}, bf16[64,640]{1,0:T(8,128)(2,1)}, u32[]{:S(2)}) copy-start(bf16[64,640]{1,0:T(8,128)(2,1)} %get-tuple-element.46.refs_0_) | copy-start | bytes 245764
  8.9 10.6 %collective-permute-start.3 = (bf16[64,640]{1,0:T(8,128)(2,1)S(1)}, bf16[64,640]{1,0:T(8,128)(2,1)S(1)}, u32[]{:S(2)}, u32[]{:S(2)}) collective-permute-start(bf16[64,640]{1,0:T(8,128)(2,1)S(1)} %copy-done.4), channel_id=1, source_target_pairs={{0,56},{8,48},{16,40},{24,32},{32,24},{40,16},{48,8},{56,0},{1,57}... | collective-permute-start | bytes 245768 | tf_op jit(solution)/shard_map/ppermute | solution.py:28
  13.8 8.6 %collective-permute-start.2 = (bf16[64,640]{1,0:T(8,128)(2,1)S(1)}, bf16[64,640]{1,0:T(8,128)(2,1)S(1)}, u32[]{:S(2)}, u32[]{:S(2)}) collective-permute-start(bf16[64,640]{1,0:T(8,128)(2,1)S(1)} %copy-done.4), channel_id=1, source_target_pairs={{0,40},{8,32},{16,56},{24,48},{32,8},{40,0},{48,24},{56,16},{1,41}... | collective-permute-start | bytes 245768 | tf_op jit(solution)/shard_map/ppermute | solution.py:28
  15.7 6.7 %collective-permute-start.1 = (bf16[64,640]{1,0:T(8,128)(2,1)S(1)}, bf16[64,640]{1,0:T(8,128)(2,1)S(1)}, u32[]{:S(2)}, u32[]{:S(2)}) collective-permute-start(bf16[64,640]{1,0:T(8,128)(2,1)S(1)} %copy-done.4), channel_id=1, source_target_pairs={{0,16},{8,24},{16,0},{24,8},{32,48},{40,56},{48,32},{56,40},{1,17}... | collective-permute-start | bytes 245768 | tf_op jit(solution)/shard_map/ppermute | solution.py:28
  16.2 8.4 %copy-start = (bf16[256,640]{1,0:T(8,128)(2,1)S(1)}, bf16[256,640]{1,0:T(8,128)(2,1)}, u32[]{:S(2)}) copy-start(bf16[256,640]{1,0:T(8,128)(2,1)} %get-tuple-element.45.refs_4_) | copy-start | bytes 983044
  22.4 17.7 %collective-permute-start.9 = (bf16[640,384]{1,0:T(8,128)(2,1)}, bf16[640,384]{1,0:T(8,128)(2,1)S(1)}, u32[]{:S(2)}, u32[]{:S(2)}) collective-permute-start(bf16[640,384]{1,0:T(8,128)(2,1)} %fusion.4), channel_id=1, source_target_pairs={{0,4},{4,0},{1,5},{5,1},{2,6},{6,2},{3,7},{7,3},{8,12},{12,8},{9,1... | collective-permute-start | bytes 1474568 | tf_op jit(solution)/shard_map/ppermute | solution.py:28
  22.4 2.1 %collective-permute-start.5 = (bf16[256,640]{1,0:T(8,128)(2,1)S(1)}, bf16[256,640]{1,0:T(8,128)(2,1)S(1)}, u32[]{:S(2)}, u32[]{:S(2)}) collective-permute-start(bf16[256,640]{1,0:T(8,128)(2,1)S(1)} %collective-permute-done.4.refs_6_), channel_id=1, source_target_pairs={{0,4},{4,0},{1,5},{5,1},{2,6},{6,2},{3,7},{7,3},{8,12},{12,8},{9,1... | collective-permute-start | bytes 983048 | tf_op jit(solution)/shard_map/ppermute | solution.py:28
  27.0 8.4 %collective-permute-start.8 = (f32[16,256]{1,0:T(8,128)S(1)}, f32[16,256]{1,0:T(8,128)S(1)}, u32[]{:S(2)}, u32[]{:S(2)}) collective-permute-start(f32[16,256]{1,0:T(8,128)S(1)} %shard_map.128.refs_8_), channel_id=1, source_target_pairs={{0,56},{8,48},{16,40},{24,32},{32,24},{40,16},{48,8},{56,0},{1,57}... | collective-permute-start | bytes 49160 | tf_op jit(solution)/shard_map/ppermute | solution.py:28
  31.6 6.7 %collective-permute-start.7 = (f32[16,256]{1,0:T(8,128)S(1)}, f32[16,256]{1,0:T(8,128)S(1)}, u32[]{:S(2)}, u32[]{:S(2)}) collective-permute-start(f32[16,256]{1,0:T(8,128)S(1)} %shard_map.128.refs_8_), channel_id=1, source_target_pairs={{0,40},{8,32},{16,56},{24,48},{32,8},{40,0},{48,24},{56,16},{1,41}... | collective-permute-start | bytes 49160 | tf_op jit(solution)/shard_map/ppermute | solution.py:28
  35.4 4.6 %collective-permute-start.6 = (f32[16,256]{1,0:T(8,128)S(1)}, f32[16,256]{1,0:T(8,128)S(1)}, u32[]{:S(2)}, u32[]{:S(2)}) collective-permute-start(f32[16,256]{1,0:T(8,128)S(1)} %shard_map.128.refs_8_), channel_id=1, source_target_pairs={{0,16},{8,24},{16,0},{24,8},{32,48},{40,56},{48,32},{56,40},{1,17}... | collective-permute-start | bytes 49160 | tf_op jit(solution)/shard_map/ppermute | solution.py:28
  46.4 2.2 %collective-permute-start.10 = (bf16[512,640]{1,0:T(8,128)(2,1)S(1)}, bf16[512,640]{1,0:T(8,128)(2,1)S(1)}, u32[]{:S(2)}, u32[]{:S(2)}) collective-permute-start(bf16[512,640]{1,0:T(8,128)(2,1)S(1)} %get-tuple-element.58), channel_id=1, source_target_pairs={{0,4},{4,0},{1,5},{5,1},{2,6},{6,2},{3,7},{7,3},{8,12},{12,8},{9,1... | collective-permute-start | bytes 1966088 | tf_op jit(solution)/shard_map/ppermute | solution.py:28
  48.7 14.2 %collective-permute-start.11 = (bf16[256,640]{1,0:T(8,128)(2,1)S(1)}, bf16[256,640]{1,0:T(8,128)(2,1)S(1)}, u32[]{:S(2)}, u32[]{:S(2)}) collective-permute-start(bf16[256,640]{1,0:T(8,128)(2,1)S(1)} %add_convert_fusion), channel_id=1, source_target_pairs={{0,8},{8,0},{16,24},{24,16},{32,40},{40,32},{48,56},{56,48},{1,9},... | collective-permute-start | bytes 983048 | tf_op jit(solution)/shard_map/ppermute | solution.py:28
  48.8 11.1 %collective-permute-start.12 = (bf16[64,640]{1,0:T(8,128)(2,1)S(1)}, bf16[64,640]{1,0:T(8,128)(2,1)S(1)}, u32[]{:S(2)}, u32[]{:S(2)}) collective-permute-start(bf16[64,640]{1,0:T(8,128)(2,1)S(1)} %get-tuple-element.65), channel_id=1, source_target_pairs={{0,16},{8,24},{16,0},{24,8},{32,48},{40,56},{48,32},{56,40},{1,17}... | collective-permute-start | bytes 245768 | tf_op jit(solution)/shard_map/ppermute | solution.py:28
  51.2 8.7 %collective-permute-start.13 = (bf16[64,640]{1,0:T(8,128)(2,1)S(1)}, bf16[64,640]{1,0:T(8,128)(2,1)S(1)}, u32[]{:S(2)}, u32[]{:S(2)}) collective-permute-start(bf16[64,640]{1,0:T(8,128)(2,1)S(1)} %get-tuple-element.66), channel_id=1, source_target_pairs={{0,40},{8,32},{16,56},{24,48},{32,8},{40,0},{48,24},{56,16},{1,41}... | collective-permute-start | bytes 245768 | tf_op jit(solution)/shard_map/ppermute | solution.py:28
  53.3 7.1 %collective-permute-start.14 = (bf16[64,640]{1,0:T(8,128)(2,1)S(1)}, bf16[64,640]{1,0:T(8,128)(2,1)S(1)}, u32[]{:S(2)}, u32[]{:S(2)}) collective-permute-start(bf16[64,640]{1,0:T(8,128)(2,1)S(1)} %get-tuple-element.67), channel_id=1, source_target_pairs={{0,56},{8,48},{16,40},{24,32},{32,24},{40,16},{48,8},{56,0},{1,57}... | collective-permute-start | bytes 245768 | tf_op jit(solution)/shard_map/ppermute | solution.py:28
  62.9 10.1 %copy-start.3 = (bf16[1280,320]{0,1:T(8,128)(2,1)S(1)}, bf16[1280,320]{0,1:T(8,128)(2,1)}, u32[]{:S(2)}) copy-start(bf16[1280,320]{0,1:T(8,128)(2,1)} %param.14) | copy-start | bytes 2457604
  63.0 1.8 %collective-permute-start.15 = (bf16[320,640]{1,0:T(8,128)(2,1)S(1)}, bf16[320,640]{1,0:T(8,128)(2,1)S(1)}, u32[]{:S(2)}, u32[]{:S(2)}) collective-permute-start(bf16[320,640]{1,0:T(8,128)(2,1)S(1)} %shard_map.130.y_ref), channel_id=1, source_target_pairs={{0,4},{4,0},{1,5},{5,1},{2,6},{6,2},{3,7},{7,3},{8,12},{12,8},{9,1... | collective-permute-start | bytes 1228808 | tf_op jit(solution)/shard_map/ppermute | solution.py:28
  63.1 9.8 %copy-start.1 = (bf16[1280,320]{0,1:T(8,128)(2,1)S(1)}, bf16[1280,320]{0,1:T(8,128)(2,1)}, u32[]{:S(2)}) copy-start(bf16[1280,320]{0,1:T(8,128)(2,1)} %param.12) | copy-start | bytes 2457604
  63.1 9.8 %copy-start.2 = (bf16[1280,320]{0,1:T(8,128)(2,1)S(1)}, bf16[1280,320]{0,1:T(8,128)(2,1)}, u32[]{:S(2)}) copy-start(bf16[1280,320]{0,1:T(8,128)(2,1)} %param.13) | copy-start | bytes 2457604
  66.2 11.9 %collective-permute-start.19 = (bf16[160,640]{1,0:T(8,128)(2,1)S(1)}, bf16[160,640]{1,0:T(8,128)(2,1)S(1)}, u32[]{:S(2)}, u32[]{:S(2)}) collective-permute-start(bf16[160,640]{1,0:T(8,128)(2,1)S(1)} %get-tuple-element.77), channel_id=1, source_target_pairs={{0,128},{64,192},{128,0},{192,64},{1,129},{65,193},{129,1},{193,65... | collective-permute-start | bytes 614408 | tf_op jit(solution)/shard_map/ppermute | solution.py:28
  69.3 10.2 %collective-permute-start.20 = (bf16[160,640]{1,0:T(8,128)(2,1)S(1)}, bf16[160,640]{1,0:T(8,128)(2,1)S(1)}, u32[]{:S(2)}, u32[]{:S(2)}) collective-permute-start(bf16[160,640]{1,0:T(8,128)(2,1)S(1)} %get-tuple-element.78), channel_id=1, source_target_pairs={{0,64},{64,0},{128,192},{192,128},{1,65},{65,1},{129,193},{193,129... | collective-permute-start | bytes 614408 | tf_op jit(solution)/shard_map/ppermute | solution.py:28
  69.9 11.1 %collective-permute-start.21 = (bf16[160,640]{1,0:T(8,128)(2,1)S(1)}, bf16[160,640]{1,0:T(8,128)(2,1)S(1)}, u32[]{:S(2)}, u32[]{:S(2)}) collective-permute-start(bf16[160,640]{1,0:T(8,128)(2,1)S(1)} %get-tuple-element.79), channel_id=1, source_target_pairs={{0,192},{64,128},{128,64},{192,0},{1,193},{65,129},{129,65},{193,1... | collective-permute-start | bytes 614408 | tf_op jit(solution)/shard_map/ppermute | solution.py:28
  70.4 19.6 %collective-permute-start.23 = (bf16[320,640]{1,0:T(8,128)(2,1)S(1)}, bf16[320,640]{1,0:T(8,128)(2,1)S(1)}, u32[]{:S(2)}, u32[]{:S(2)}) collective-permute-start(bf16[320,640]{1,0:T(8,128)(2,1)S(1)} %get-tuple-element.81), channel_id=1, source_target_pairs={{0,8},{8,0},{16,24},{24,16},{32,40},{40,32},{48,56},{56,48},{1,9},... | collective-permute-start | bytes 1228808 | tf_op jit(solution)/shard_map/ppermute | solution.py:28
  75.7 10.5 %collective-permute-start.16 = (bf16[320,320]{1,0:T(8,128)(2,1)S(1)}, bf16[320,320]{1,0:T(8,128)(2,1)S(1)}, u32[]{:S(2)}, u32[]{:S(2)}) collective-permute-start(bf16[320,320]{1,0:T(8,128)(2,1)S(1)} %get-tuple-element.73), channel_id=1, source_target_pairs={{0,2},{1,3},{2,0},{3,1},{4,6},{5,7},{6,4},{7,5},{8,10},{9,11},{10,... | collective-permute-start | bytes 614408 | tf_op jit(solution)/shard_map/ppermute | solution.py:28
  78.1 11.7 %collective-permute-start.17 = (bf16[320,320]{1,0:T(8,128)(2,1)S(1)}, bf16[320,320]{1,0:T(8,128)(2,1)S(1)}, u32[]{:S(2)}, u32[]{:S(2)}) collective-permute-start(bf16[320,320]{1,0:T(8,128)(2,1)S(1)} %get-tuple-element.74), channel_id=1, source_target_pairs={{0,1},{1,0},{2,3},{3,2},{4,5},{5,4},{6,7},{7,6},{8,9},{9,8},{10,11... | collective-permute-start | bytes 614408 | tf_op jit(solution)/shard_map/ppermute | solution.py:28
  79.5 10.4 %collective-permute-start.18 = (bf16[320,320]{1,0:T(8,128)(2,1)S(1)}, bf16[320,320]{1,0:T(8,128)(2,1)S(1)}, u32[]{:S(2)}, u32[]{:S(2)}) collective-permute-start(bf16[320,320]{1,0:T(8,128)(2,1)S(1)} %get-tuple-element.75), channel_id=1, source_target_pairs={{0,3},{1,2},{2,1},{3,0},{4,7},{5,6},{6,5},{7,4},{8,11},{9,10},{10,... | collective-permute-start | bytes 614408 | tf_op jit(solution)/shard_map/ppermute | solution.py:28
  81.1 13.0 %collective-permute-start.22 = (bf16[80,640]{1,0:T(8,128)(2,1)S(1)}, bf16[80,640]{1,0:T(8,128)(2,1)S(1)}, u32[]{:S(2)}, u32[]{:S(2)}) collective-permute-start(bf16[80,640]{1,0:T(8,128)(2,1)S(1)} %slice.105), channel_id=1, source_target_pairs={{0,8},{8,0},{16,24},{24,16},{32,40},{40,32},{48,56},{56,48},{1,9},... | collective-permute-start | bytes 307208 | tf_op jit(solution)/shard_map/ppermute | solution.py:28
  90.2 6.3 %collective-permute-start.24 = (bf16[80,640]{1,0:T(8,128)(2,1)S(1)}, bf16[80,640]{1,0:T(8,128)(2,1)S(1)}, u32[]{:S(2)}, u32[]{:S(2)}) collective-permute-start(bf16[80,640]{1,0:T(8,128)(2,1)S(1)} %get-tuple-element.90), channel_id=1, source_target_pairs={{0,128},{64,192},{128,0},{192,64},{1,129},{65,193},{129,1},{193,65... | collective-permute-start | bytes 307208 | tf_op jit(solution)/shard_map/ppermute | solution.py:28
  93.0 5.9 %collective-permute-start.26 = (bf16[80,640]{1,0:T(8,128)(2,1)S(1)}, bf16[80,640]{1,0:T(8,128)(2,1)S(1)}, u32[]{:S(2)}, u32[]{:S(2)}) collective-permute-start(bf16[80,640]{1,0:T(8,128)(2,1)S(1)} %get-tuple-element.91), channel_id=1, source_target_pairs={{0,192},{64,128},{128,64},{192,0},{1,193},{65,129},{129,65},{193,1... | collective-permute-start | bytes 307208 | tf_op jit(solution)/shard_map/ppermute | solution.py:28
  94.1 4.8 %collective-permute-start.25 = (bf16[80,640]{1,0:T(8,128)(2,1)S(1)}, bf16[80,640]{1,0:T(8,128)(2,1)S(1)}, u32[]{:S(2)}, u32[]{:S(2)}) collective-permute-start(bf16[80,640]{1,0:T(8,128)(2,1)S(1)} %get-tuple-element.92), channel_id=1, source_target_pairs={{0,64},{64,0},{128,192},{192,128},{1,65},{65,1},{129,193},{193,129... | collective-permute-start | bytes 307208 | tf_op jit(solution)/shard_map/ppermute | solution.py:28
  99.0 8.0 %collective-permute-start.27 = (bf16[20,1280]{1,0:T(8,128)(2,1)S(1)}, bf16[20,1280]{1,0:T(8,128)(2,1)S(1)}, u32[]{:S(2)}, u32[]{:S(2)}) collective-permute-start(bf16[20,1280]{1,0:T(8,128)(2,1)S(1)} %get-tuple-element.93), channel_id=1, source_target_pairs={{0,40},{8,32},{16,56},{24,48},{32,8},{40,0},{48,24},{56,16},{1,41}... | collective-permute-start | bytes 153608 | tf_op jit(solution)/shard_map/ppermute | solution.py:28
  102.0 6.0 %collective-permute-start.29 = (bf16[20,1280]{1,0:T(8,128)(2,1)S(1)}, bf16[20,1280]{1,0:T(8,128)(2,1)S(1)}, u32[]{:S(2)}, u32[]{:S(2)}) collective-permute-start(bf16[20,1280]{1,0:T(8,128)(2,1)S(1)} %get-tuple-element.94), channel_id=1, source_target_pairs={{0,56},{8,48},{16,40},{24,32},{32,24},{40,16},{48,8},{56,0},{1,57}... | collective-permute-start | bytes 153608 | tf_op jit(solution)/shard_map/ppermute | solution.py:28
  102.6 5.6 %collective-permute-start.28 = (bf16[20,1280]{1,0:T(8,128)(2,1)S(1)}, bf16[20,1280]{1,0:T(8,128)(2,1)S(1)}, u32[]{:S(2)}, u32[]{:S(2)}) collective-permute-start(bf16[20,1280]{1,0:T(8,128)(2,1)S(1)} %get-tuple-element.95), channel_id=1, source_target_pairs={{0,16},{8,24},{16,0},{24,8},{32,48},{40,56},{48,32},{56,40},{1,17}... | collective-permute-start | bytes 153608 | tf_op jit(solution)/shard_map/ppermute | solution.py:28

commit v3 on v2

--- a/solution.py
+++ b/solution.py
@@ -37,12 +37,25 @@
     return jnp.where(positions < valid_ref[block], 0.0, LOW)
 
 
+SPAN = 2
+
+
+def joined_blocks(valid_ref, refs, span):
+    blocks, biases = [], []
+    for first in range(0, len(refs), span):
+        some = range(first, first + span)
+        blocks.append(jnp.concatenate([refs[j][...] for j in some], axis=0))
+        biases.append(
+            jnp.concatenate([frame_bias(valid_ref, j, refs[j].shape[0]) for j in some], axis=0)
+        )
+    return blocks, biases
+
+
 def stats_kernel(heads, valid_ref, *refs):
     rows_refs, frame_refs, out_ref = refs[:4], refs[4:8], refs[8]
     width = heads * HD
     rows = jnp.concatenate([r[...] for r in rows_refs], axis=0)
-    blocks = [r[...] for r in frame_refs]
-    biases = [frame_bias(valid_ref, j, b.shape[0]) for j, b in enumerate(blocks)]
+    blocks, biases = joined_blocks(valid_ref, frame_refs, 1)
     out_ref[...] = jnp.zeros_like(out_ref)
     for h in range(heads):
         cut = slice(h * HD, (h + 1) * HD)
@@ -84,8 +97,8 @@
     dq_refs = refs[15:19]
     width = heads * HD
     rows = jnp.concatenate([r[...] for r in rows_refs], axis=0)
-    blocks = [r[...] for r in frame_refs]
-    part = blocks[0].shape[0]
+    blocks, biases = joined_blocks(valid_ref, frame_refs, SPAN)
+    part = frame_refs[0].shape[0]
     own = rows_refs[0].shape[0]
     stats = [in_own_order(stat_refs[k][...], k, own) for k in range(4)]
     tops = [s[:8] for s in stats]
@@ -96,7 +109,6 @@
     delta = functools.reduce(
         jnp.add, [w * s[8:] for w, s in zip(shares, stats)]
     ) / total
-    biases = [frame_bias(valid_ref, j, part) for j in range(4)]
     dq_t, att_t = [], []
     for h in range(heads):
         cut = slice(h * HD, (h + 1) * HD)
@@ -113,10 +125,12 @@
             probs = probs.astype(BF)
             dkey = mm(dscores, query) * SCALE
             dvalue = mm(probs, dout)
-            out_ref = send_ref if j % 2 else keep_refs[j // 2]
-            span = slice((j // 2) * part, (j // 2 + 1) * part) if j % 2 else slice(0, part)
-            out_ref[span, cut] = dkey.astype(out_ref.dtype)
-            out_ref[span, cut2] = dvalue.astype(out_ref.dtype)
+            for i in range(SPAN):
+                owner, at = j * SPAN + i, slice(i * part, (i + 1) * part)
+                out_ref = send_ref if owner % 2 else keep_refs[owner // 2]
+                low = (owner // 2) * part if owner % 2 else 0
+                out_ref[low : low + part, cut] = dkey[at].astype(out_ref.dtype)
+                out_ref[low : low + part, cut2] = dvalue[at].astype(out_ref.dtype)
             dq_sum += mm(key, dscores, TN)
             att_sum += mm(value, probs, TN)
         dq_t.append(dq_sum * SCALE)
@@ -350,9 +364,7 @@
             flops=12_000_000_000, bytes_accessed=0, transcendentals=0
         ),
     )(where, held, wk_t, wv_t, wq_t)
-    arrived = [flip(sends[k - 1], "head", 4, k) for k in (2, 1, 3)]
-    inputs = (own_part + sum(p.astype(F32) for p in arrived)).astype(BF)
-    dframes, dinput = inputs[:slab], inputs[slab:]
+    arrived = [flip(sends[k - 1], "head", 4, k) for k in (2, 1)]
 
     cut = part // 2
     kv_sum = kv_own + sum(k.astype(F32) for k in kv_x)
@@ -362,9 +374,13 @@
     kv_sum = kv_sum[:cut] + kv_b.astype(F32)
     qo_sum = qo_sum[:cut] + sum(q.astype(F32) for q in qo_x)
     total = jnp.concatenate([kv_sum, qo_sum], axis=1)
+    total, sends[2], arrived = lax.optimization_barrier((total, sends[2], arrived))
+    arrived.append(flip(sends[2], "head", 4, 3))
     low = total.astype(BF)
     over = [flip(low[k * inner : (k + 1) * inner], "z", 8, QUAD[k]) for k in (2, 1, 3)]
     total = total[:inner] + sum(p.astype(F32) for p in over)
+    inputs = (own_part + sum(p.astype(F32) for p in arrived)).astype(BF)
+    dframes, dinput = inputs[:slab], inputs[slab:]
     return (
         dinput[None],
         dframes[None],

time: 110 us -> 105 us (0.955)
  waiting for transfers between devices: 34.8 us -> 31.2 us
  Pallas kernels: 17.4 us -> 15.4 us
    ppermute x30, waiting for transfers between devices: 34.8 us -> 31.2 us  [flip(): return lax.ppermute(x, axis, [(i, i ^ bits) for i in range(size)])]
    pallas_call x4, Pallas kernels: 10.3 us -> 8.29 us  [call(): pl.pallas_call(kernel, out_shape=shapes, in_specs=specs, out_specs=[VMEM]...]
where the time goes in v3:
time: 105 us; the launch traced here: 104 us
  starting transfers between devices  49.7 us (47%)
  waiting for transfers between devices  31.2 us (30%)
  Pallas kernels  15.4 us (15%)
  matrix products  2.91 us (3%)
  local copies, waits for them, and re-layouts  2.29 us (2%)
  between operations  1.54 us (1%)
    ppermute x30, starting transfers between devices, flip(): return lax.ppermute(x, axis, [(i, i ^ bits) for i in range(size)])  49.7 us
    ppermute x30, waiting for transfers between devices, flip(): return lax.ppermute(x, axis, [(i, i ^ bits) for i in range(size)])  31.2 us
    pallas_call x4, Pallas kernels, call(): pl.pallas_call(kernel, out_shape=shapes, in_specs=specs, out_specs=[VMEM]...  8.29 us
    pallas_call x1, Pallas kernels, per_device(): pl.pallas_call(project_kernel, out_shape=[jax.ShapeDtypeStruct((own, 2 *...  4.34 us
    dot_general x2, matrix products, mm(): return lax.dot_general(left, right, dims, preferred_element_type=F32)  2.91 us
    pallas_call x1, Pallas kernels, per_device(): pl.pallas_call(inputs_kernel, out_shape=[jax.ShapeDtypeStruct((slab + own...  2.75 us
  transfers between devices with their start and end apart: 30, of which 17 were waited for; matrix products, arithmetic and copies ran while one was open for 4% of the time, Pallas kernels for 5%

profile of v3, /device:TPU:8, one launch (start us, length us, event | category | flops | bytes accessed | tf_op | source)
XLA Modules:
  0.0 103.7 jit_solution(4316665086103395110)
XLA Ops:
  0.7 4.3 %shard_map.127 = (bf16[64,640]{1,0:T(8,128)(2,1)}, bf16[256,640]{1,0:T(8,128)(2,1)}) custom-call(bf16[64,1280]{1,0:T(8,128)(2,1)} %bitcast.31, bf16[64,1280]{1,0:T(8,128)(2,1)} %bitcast.34, bf16[256,1280]{1,0:T(8,128)(2,1)} %bitcast.28, bf16[320,1280]{1,0:T(8,128)(2,1)} %bitcast.22, bf16[320,1280]{1,0:T(8,128)(2,1)} %wo_ref.1, bf16[320,1280]{1,0:T(8,128)(2,1)} %bitcast.24, ...), custom_call_target="tpu_custom_call" | custom-call | tf_op jit(solution)/shard_map/pallas_call | solution.py:268
  5.0 2.0 %collective-permute-start.4 = (bf16[256,640]{1,0:T(8,128)(2,1)}, bf16[256,640]{1,0:T(8,128)(2,1)S(1)}, u32[]{:S(2)}, u32[]{:S(2)}) collective-permute-start(bf16[256,640]{1,0:T(8,128)(2,1)} %get-tuple-element.49.refs_4_), channel_id=1, source_target_pairs={{0,8},{8,0},{16,24},{24,16},{32,40},{40,32},{48,56},{56,48},{1,9},... | collective-permute-start | bytes 983048 | tf_op jit(solution)/shard_map/ppermute | solution.py:28
  7.1 1.1 %fusion.5.xt_ref = bf16[640,384]{1,0:T(8,128)(2,1)S(1)} fusion(s32[640]{0:T(1024)S(1)} %get-tuple-element.109, bf16[64,1280]{1,0:T(8,128)(2,1)S(1)} %bitcast.35, bf16[64,1280]{1,0:T(8,128)(2,1)S(1)} %bitcast.32, bf16[256,1280]{1,0:T(8,128)(2,1)S(1)} %bitcast.29), kind=kOutput, calls=%fused_computation.7 | convolution fusion | flops 633159680 | bytes 1477120 | tf_op jit(solution)/shard_map/dot_general | solution.py:24
  8.2 0.7 collective-permute-done.refs_5_
  8.9 4.9 %collective-permute-start.3 = (bf16[64,640]{1,0:T(8,128)(2,1)S(1)}, bf16[64,640]{1,0:T(8,128)(2,1)S(1)}, u32[]{:S(2)}, u32[]{:S(2)}) collective-permute-start(bf16[64,640]{1,0:T(8,128)(2,1)S(1)} %copy-done.4), channel_id=1, source_target_pairs={{0,56},{8,48},{16,40},{24,32},{32,24},{40,16},{48,8},{56,0},{1,57}... | collective-permute-start | bytes 245768 | tf_op jit(solution)/shard_map/ppermute | solution.py:28
  13.8 1.9 %collective-permute-start.2 = (bf16[64,640]{1,0:T(8,128)(2,1)S(1)}, bf16[64,640]{1,0:T(8,128)(2,1)S(1)}, u32[]{:S(2)}, u32[]{:S(2)}) collective-permute-start(bf16[64,640]{1,0:T(8,128)(2,1)S(1)} %copy-done.4), channel_id=1, source_target_pairs={{0,40},{8,32},{16,56},{24,48},{32,8},{40,0},{48,24},{56,16},{1,41}... | collective-permute-start | bytes 245768 | tf_op jit(solution)/shard_map/ppermute | solution.py:28
  16.2 1.8 %fusion.4 = bf16[640,384]{1,0:T(8,128)(2,1)} fusion(s32[640]{0:T(1024)S(1)} %get-tuple-element.108, bf16[64,1280]{1,0:T(8,128)(2,1)S(1)} %bitcast.36, bf16[64,1280]{1,0:T(8,128)(2,1)S(1)} %bitcast.33, bf16[256,1280]{1,0:T(8,128)(2,1)S(1)} %bitcast.30), kind=kOutput, calls=%fused_computation.6 | convolution fusion | flops 633159680 | bytes 1477120 | tf_op jit(solution)/shard_map/dot_general | solution.py:24
  18.0 1.5 %collective-permute-done.3.refs_3_ = bf16[64,640]{1,0:T(8,128)(2,1)S(1)} collective-permute-done((bf16[64,640]{1,0:T(8,128)(2,1)S(1)}, bf16[64,640]{1,0:T(8,128)(2,1)S(1)}, u32[]{:S(2)}, u32[]{:S(2)}) %collective-permute-start.3) | collective-permute-done | bytes 81952 | tf_op jit(solution)/shard_map/ppermute | solution.py:28
  19.5 2.9 %collective-permute-done.2.refs_2_ = bf16[64,640]{1,0:T(8,128)(2,1)S(1)} collective-permute-done((bf16[64,640]{1,0:T(8,128)(2,1)S(1)}, bf16[64,640]{1,0:T(8,128)(2,1)S(1)}, u32[]{:S(2)}, u32[]{:S(2)}) %collective-permute-start.2) | collective-permute-done | bytes 81952 | tf_op jit(solution)/shard_map/ppermute | solution.py:28
  22.4 0.5 collective-permute-start.5
  23.6 0.9 collective-permute-done.5.refs_7_
  24.5 2.5 %shard_map.128.refs_8_ = f32[16,256]{1,0:T(8,128)S(1)} custom-call(s32[4]{0:T(128)S(1)} %pad_add_fusion.valid_ref, bf16[64,640]{1,0:T(8,128)(2,1)S(1)} %copy-done.4, bf16[64,640]{1,0:T(8,128)(2,1)S(1)} %collective-permute-done.1.refs_1_, bf16[64,640]{1,0:T(8,128)(2,1)S(1)} %collective-permute-done.2.refs_2_, ...), custom_call_target="tpu_custom_call" | custom-call | flops 2 | tf_op jit(solution)/shard_map/pallas_call | solution.py:254
  27.0 4.6 %collective-permute-start.8 = (f32[16,256]{1,0:T(8,128)S(1)}, f32[16,256]{1,0:T(8,128)S(1)}, u32[]{:S(2)}, u32[]{:S(2)}) collective-permute-start(f32[16,256]{1,0:T(8,128)S(1)} %shard_map.128.refs_8_), channel_id=1, source_target_pairs={{0,56},{8,48},{16,40},{24,32},{32,24},{40,16},{48,8},{56,0},{1,57}... | collective-permute-start | bytes 49160 | tf_op jit(solution)/shard_map/ppermute | solution.py:28
  31.6 3.8 %collective-permute-start.7 = (f32[16,256]{1,0:T(8,128)S(1)}, f32[16,256]{1,0:T(8,128)S(1)}, u32[]{:S(2)}, u32[]{:S(2)}) collective-permute-start(f32[16,256]{1,0:T(8,128)S(1)} %shard_map.128.refs_8_), channel_id=1, source_target_pairs={{0,40},{8,32},{16,56},{24,48},{32,8},{40,0},{48,24},{56,16},{1,41}... | collective-permute-start | bytes 49160 | tf_op jit(solution)/shard_map/ppermute | solution.py:28
  35.4 2.9 %collective-permute-done.7.refs_10_ = f32[16,256]{1,0:T(8,128)S(1)} collective-permute-done((f32[16,256]{1,0:T(8,128)S(1)}, f32[16,256]{1,0:T(8,128)S(1)}, u32[]{:S(2)}, u32[]{:S(2)}) %collective-permute-start.7) | collective-permute-done | bytes 16416 | tf_op jit(solution)/shard_map/ppermute | solution.py:28
  38.3 1.7 %collective-permute-done.6.refs_9_ = f32[16,256]{1,0:T(8,128)S(1)} collective-permute-done((f32[16,256]{1,0:T(8,128)S(1)}, f32[16,256]{1,0:T(8,128)S(1)}, u32[]{:S(2)}, u32[]{:S(2)}) %collective-permute-start.6) | collective-permute-done | bytes 16416 | tf_op jit(solution)/shard_map/ppermute | solution.py:28
  40.1 4.3 %shard_map.129 = (f32[256,640]{1,0:T(8,128)S(1)}, f32[256,640]{1,0:T(8,128)S(1)}, bf16[512,640]{1,0:T(8,128)(2,1)S(1)}, f32[64,640]{1,0:T(8,128)S(1)}, bf16[64,6...) custom-call(s32[4]{0:T(128)S(1)} %pad_add_fusion.valid_ref, ...), custom_call_target="tpu_custom_call" | custom-call | flops 2 | tf_op jit(solution)/shard_map/pallas_call | solution.py:254
  44.5 2.1 %collective-permute-done.10.core_ref = bf16[512,640]{1,0:T(8,128)(2,1)S(1)} collective-permute-done((bf16[512,640]{1,0:T(8,128)(2,1)S(1)}, bf16[512,640]{1,0:T(8,128)(2,1)S(1)}, u32[]{:S(2)}, u32[]{:S(2)}) %collective-permute-start.10) | collective-permute-done | bytes 655392 | tf_op jit(solution)/shard_map/ppermute | solution.py:28
  46.8 2.4 %collective-permute-start.12 = (bf16[64,640]{1,0:T(8,128)(2,1)S(1)}, bf16[64,640]{1,0:T(8,128)(2,1)S(1)}, u32[]{:S(2)}, u32[]{:S(2)}) collective-permute-start(bf16[64,640]{1,0:T(8,128)(2,1)S(1)} %get-tuple-element.69), channel_id=1, source_target_pairs={{0,16},{8,24},{16,0},{24,8},{32,48},{40,56},{48,32},{56,40},{1,17}... | collective-permute-start | bytes 245768 | tf_op jit(solution)/shard_map/ppermute | solution.py:28
  49.1 2.1 %collective-permute-start.13 = (bf16[64,640]{1,0:T(8,128)(2,1)S(1)}, bf16[64,640]{1,0:T(8,128)(2,1)S(1)}, u32[]{:S(2)}, u32[]{:S(2)}) collective-permute-start(bf16[64,640]{1,0:T(8,128)(2,1)S(1)} %get-tuple-element.70), channel_id=1, source_target_pairs={{0,40},{8,32},{16,56},{24,48},{32,8},{40,0},{48,24},{56,16},{1,41}... | collective-permute-start | bytes 245768 | tf_op jit(solution)/shard_map/ppermute | solution.py:28
  51.2 1.2 %collective-permute-start.14 = (bf16[64,640]{1,0:T(8,128)(2,1)S(1)}, bf16[64,640]{1,0:T(8,128)(2,1)S(1)}, u32[]{:S(2)}, u32[]{:S(2)}) collective-permute-start(bf16[64,640]{1,0:T(8,128)(2,1)S(1)} %get-tuple-element.71), channel_id=1, source_target_pairs={{0,56},{8,48},{16,40},{24,32},{32,24},{40,16},{48,8},{56,0},{1,57}... | collective-permute-start | bytes 245768 | tf_op jit(solution)/shard_map/ppermute | solution.py:28
  52.4 5.4 %collective-permute-done.12.a_ref = bf16[64,640]{1,0:T(8,128)(2,1)S(1)} collective-permute-done((bf16[64,640]{1,0:T(8,128)(2,1)S(1)}, bf16[64,640]{1,0:T(8,128)(2,1)S(1)}, u32[]{:S(2)}, u32[]{:S(2)}) %collective-permute-start.12) | collective-permute-done | bytes 81952 | tf_op jit(solution)/shard_map/ppermute | solution.py:28
  57.8 0.6 collective-permute-done.14.c_ref
  58.4 2.4 %collective-permute-done.11.pair_ref = bf16[256,640]{1,0:T(8,128)(2,1)S(1)} collective-permute-done((bf16[256,640]{1,0:T(8,128)(2,1)S(1)}, bf16[256,640]{1,0:T(8,128)(2,1)S(1)}, u32[]{:S(2)}, u32[]{:S(2)}) %collective-permute-start.11) | collective-permute-done | bytes 327712 | tf_op jit(solution)/shard_map/ppermute | solution.py:28
  61.1 1.7 %collective-permute-done.15.y2_ref = bf16[320,640]{1,0:T(8,128)(2,1)S(1)} collective-permute-done((bf16[320,640]{1,0:T(8,128)(2,1)S(1)}, bf16[320,640]{1,0:T(8,128)(2,1)S(1)}, u32[]{:S(2)}, u32[]{:S(2)}) %collective-permute-start.15) | collective-permute-done | bytes 409632 | tf_op jit(solution)/shard_map/ppermute | solution.py:28
  62.8 1.3 %shard_map.131 = (f32[160,640]{1,0:T(8,128)S(1)}, bf16[160,640]{1,0:T(8,128)(2,1)S(1)}, bf16[160,640]{1,0:T(8,128)(2,1)S(1)}, bf16[160,640]{1,0:T(8,128)(2,1)S(1...) custom-call(bf16[640,384]{1,0:T(8,128)(2,1)S(1)} %fusion.5.xt_ref, ...), custom_call_target="tpu_custom_call" | custom-call | flops 2 | tf_op jit(solution)/shard_map/pallas_call | solution.py:254
  64.1 3.1 %collective-permute-start.16 = (bf16[160,640]{1,0:T(8,128)(2,1)S(1)}, bf16[160,640]{1,0:T(8,128)(2,1)S(1)}, u32[]{:S(2)}, u32[]{:S(2)}) collective-permute-start(bf16[160,640]{1,0:T(8,128)(2,1)S(1)} %get-tuple-element.78), channel_id=1, source_target_pairs={{0,128},{64,192},{128,0},{192,64},{1,129},{65,193},{129,1},{193,65... | collective-permute-start | bytes 614408 | tf_op jit(solution)/shard_map/ppermute | solution.py:28
  67.2 0.6 collective-permute-start.17
  67.8 0.5 collective-permute-start.18
  68.4 2.5 %collective-permute-start.20 = (bf16[320,640]{1,0:T(8,128)(2,1)S(1)}, bf16[320,640]{1,0:T(8,128)(2,1)S(1)}, u32[]{:S(2)}, u32[]{:S(2)}) collective-permute-start(bf16[320,640]{1,0:T(8,128)(2,1)S(1)} %get-tuple-element.82), channel_id=1, source_target_pairs={{0,8},{8,0},{16,24},{24,16},{32,40},{40,32},{48,56},{56,48},{1,9},... | collective-permute-start | bytes 1228808 | tf_op jit(solution)/shard_map/ppermute | solution.py:28
  70.9 2.8 %shard_map.132 = (f32[320,320]{1,0:T(8,128)S(1)}, bf16[320,320]{1,0:T(8,128)(2,1)S(1)}, bf16[320,320]{1,0:T(8,128)(2,1)S(1)}, bf16[320,320]{1,0:T(8,128)(2,1)S(1)}) custom-call(s32[1]{0:T(128)} %bitcast.where_ref, bf16[320,640]{1,0:T(8,128)(2,1)S(1)} %shard_map.130.y_ref, bf16[320,1280]{1,0:T(8,128)(2,1)S(1)} %bitcast.25, bf16[320,1280]{1,0:T(8,128)(2,1)S(1)} %bitcast.27, ...), custom_call_target="tpu_custom_call" | custom-call | flops 12000000000 | tf_op jit(solution)/shard_map/pallas_call | solution.py:353
  73.7 2.4 %collective-permute-start.24 = (bf16[320,320]{1,0:T(8,128)(2,1)S(1)}, bf16[320,320]{1,0:T(8,128)(2,1)S(1)}, u32[]{:S(2)}, u32[]{:S(2)}) collective-permute-start(bf16[320,320]{1,0:T(8,128)(2,1)S(1)} %get-tuple-element.84), channel_id=1, source_target_pairs={{0,2},{1,3},{2,0},{3,1},{4,6},{5,7},{6,4},{7,5},{8,10},{9,11},{10,... | collective-permute-start | bytes 614408 | tf_op jit(solution)/shard_map/ppermute | solution.py:28
  76.1 1.3 %collective-permute-start.25 = (bf16[320,320]{1,0:T(8,128)(2,1)S(1)}, bf16[320,320]{1,0:T(8,128)(2,1)S(1)}, u32[]{:S(2)}, u32[]{:S(2)}) collective-permute-start(bf16[320,320]{1,0:T(8,128)(2,1)S(1)} %get-tuple-element.85), channel_id=1, source_target_pairs={{0,1},{1,0},{2,3},{3,2},{4,5},{5,4},{6,7},{7,6},{8,9},{9,8},{10,11... | collective-permute-start | bytes 614408 | tf_op jit(solution)/shard_map/ppermute | solution.py:28
  77.5 2.6 %collective-permute-start.19 = (bf16[80,640]{1,0:T(8,128)(2,1)S(1)}, bf16[80,640]{1,0:T(8,128)(2,1)S(1)}, u32[]{:S(2)}, u32[]{:S(2)}) collective-permute-start(bf16[80,640]{1,0:T(8,128)(2,1)S(1)} %slice.96), channel_id=1, source_target_pairs={{0,8},{8,0},{16,24},{24,16},{32,40},{40,32},{48,56},{56,48},{1,9},... | collective-permute-start | bytes 307208 | tf_op jit(solution)/shard_map/ppermute | solution.py:28
  80.3 3.0 %collective-permute-start.21 = (bf16[80,640]{1,0:T(8,128)(2,1)S(1)}, bf16[80,640]{1,0:T(8,128)(2,1)S(1)}, u32[]{:S(2)}, u32[]{:S(2)}) collective-permute-start(bf16[80,640]{1,0:T(8,128)(2,1)S(1)} %get-tuple-element.98), channel_id=1, source_target_pairs={{0,128},{64,192},{128,0},{192,64},{1,129},{65,193},{129,1},{193,65... | collective-permute-start | bytes 307208 | tf_op jit(solution)/shard_map/ppermute | solution.py:28
  83.2 1.2 %collective-permute-start.23 = (bf16[80,640]{1,0:T(8,128)(2,1)S(1)}, bf16[80,640]{1,0:T(8,128)(2,1)S(1)}, u32[]{:S(2)}, u32[]{:S(2)}) collective-permute-start(bf16[80,640]{1,0:T(8,128)(2,1)S(1)} %get-tuple-element.99), channel_id=1, source_target_pairs={{0,192},{64,128},{128,64},{192,0},{1,193},{65,129},{129,65},{193,1... | collective-permute-start | bytes 307208 | tf_op jit(solution)/shard_map/ppermute | solution.py:28
  84.5 2.0 %collective-permute-done.21 = bf16[80,640]{1,0:T(8,128)(2,1)S(1)} collective-permute-done((bf16[80,640]{1,0:T(8,128)(2,1)S(1)}, bf16[80,640]{1,0:T(8,128)(2,1)S(1)}, u32[]{:S(2)}, u32[]{:S(2)}) %collective-permute-start.21) | collective-permute-done | bytes 102432 | tf_op jit(solution)/shard_map/ppermute | solution.py:28
  86.5 2.6 %collective-permute-done.23 = bf16[80,640]{1,0:T(8,128)(2,1)S(1)} collective-permute-done((bf16[80,640]{1,0:T(8,128)(2,1)S(1)}, bf16[80,640]{1,0:T(8,128)(2,1)S(1)}, u32[]{:S(2)}, u32[]{:S(2)}) %collective-permute-start.23) | collective-permute-done | bytes 102432 | tf_op jit(solution)/shard_map/ppermute | solution.py:28
  89.3 4.0 %collective-permute-start.27 = (bf16[20,1280]{1,0:T(8,128)(2,1)S(1)}, bf16[20,1280]{1,0:T(8,128)(2,1)S(1)}, u32[]{:S(2)}, u32[]{:S(2)}) collective-permute-start(bf16[20,1280]{1,0:T(8,128)(2,1)S(1)} %get-tuple-element.101), channel_id=1, source_target_pairs={{0,40},{8,32},{16,56},{24,48},{32,8},{40,0},{48,24},{56,16},{1,41}... | collective-permute-start | bytes 153608 | tf_op jit(solution)/shard_map/ppermute | solution.py:28
  93.3 0.6 collective-permute-start.29
  93.8 2.0 %collective-permute-start.28 = (bf16[20,1280]{1,0:T(8,128)(2,1)S(1)}, bf16[20,1280]{1,0:T(8,128)(2,1)S(1)}, u32[]{:S(2)}, u32[]{:S(2)}) collective-permute-start(bf16[20,1280]{1,0:T(8,128)(2,1)S(1)} %get-tuple-element.103), channel_id=1, source_target_pairs={{0,16},{8,24},{16,0},{24,8},{32,48},{40,56},{48,32},{56,40},{1,17}... | collective-permute-start | bytes 153608 | tf_op jit(solution)/shard_map/ppermute | solution.py:28
  95.9 1.6 %collective-permute-start.26 = (bf16[320,320]{1,0:T(8,128)(2,1)S(1)}, bf16[320,320]{1,0:T(8,128)(2,1)S(1)}, u32[]{:S(2)}, u32[]{:S(2)}) collective-permute-start(bf16[320,320]{1,0:T(8,128)(2,1)S(1)} %get-tuple-element.88), channel_id=1, source_target_pairs={{0,3},{1,2},{2,1},{3,0},{4,7},{5,6},{6,5},{7,4},{8,11},{9,10},{10,... | collective-permute-start | bytes 614408 | tf_op jit(solution)/shard_map/ppermute | solution.py:28
  97.5 1.2 %collective-permute-done.29 = bf16[20,1280]{1,0:T(8,128)(2,1)S(1)} collective-permute-done((bf16[20,1280]{1,0:T(8,128)(2,1)S(1)}, bf16[20,1280]{1,0:T(8,128)(2,1)S(1)}, u32[]{:S(2)}, u32[]{:S(2)}) %collective-permute-start.29) | collective-permute-done | bytes 51232 | tf_op jit(solution)/shard_map/ppermute | solution.py:28
  98.7 1.4 %collective-permute-done.28 = bf16[20,1280]{1,0:T(8,128)(2,1)S(1)} collective-permute-done((bf16[20,1280]{1,0:T(8,128)(2,1)S(1)}, bf16[20,1280]{1,0:T(8,128)(2,1)S(1)}, u32[]{:S(2)}, u32[]{:S(2)}) %collective-permute-start.28) | collective-permute-done | bytes 51232 | tf_op jit(solution)/shard_map/ppermute | solution.py:28
  100.1 0.7 slice_bitcast_fusion.2
  100.8 1.2 %collective-permute-done.26 = bf16[320,320]{1,0:T(8,128)(2,1)S(1)} collective-permute-done((bf16[320,320]{1,0:T(8,128)(2,1)S(1)}, bf16[320,320]{1,0:T(8,128)(2,1)S(1)}, u32[]{:S(2)}, u32[]{:S(2)}) %collective-permute-start.26) | collective-permute-done | bytes 204832 | tf_op jit(solution)/shard_map/ppermute | solution.py:28
  102.2 0.6 slice_bitcast_fusion.1
  102.9 0.8 copy.14
  (54 shorter events, 1.9 us)
Async XLA Ops:
  0.6 6.4 %copy-start.5 = (bf16[1,256,1280]{2,1,0:T(8,128)(2,1)S(1)}, bf16[1,256,1280]{2,1,0:T(8,128)(2,1)}, u32[]{:S(2)}) copy-start(bf16[1,256,1280]{2,1,0:T(8,128)(2,1)} %param.10) | copy-start | bytes 1966084
  0.6 6.4 %copy-start.6 = (bf16[1,64,1280]{2,1,0:T(8,128)(2,1)S(1)}, bf16[1,64,1280]{2,1,0:T(8,128)(2,1)}, u32[]{:S(2)}) copy-start(bf16[1,64,1280]{2,1,0:T(8,128)(2,1)} %param.8) | copy-start | bytes 491524
  0.7 6.4 %copy-start.7 = (bf16[1,64,1280]{2,1,0:T(8,128)(2,1)S(1)}, bf16[1,64,1280]{2,1,0:T(8,128)(2,1)}, u32[]{:S(2)}) copy-start(bf16[1,64,1280]{2,1,0:T(8,128)(2,1)} %param.9) | copy-start | bytes 491524
  5.0 13.0 %collective-permute-start.4 = (bf16[256,640]{1,0:T(8,128)(2,1)}, bf16[256,640]{1,0:T(8,128)(2,1)S(1)}, u32[]{:S(2)}, u32[]{:S(2)}) collective-permute-start(bf16[256,640]{1,0:T(8,128)(2,1)} %get-tuple-element.49.refs_4_), channel_id=1, source_target_pairs={{0,8},{8,0},{16,24},{24,16},{32,40},{40,32},{48,56},{56,48},{1,9},... | collective-permute-start | bytes 983048 | tf_op jit(solution)/shard_map/ppermute | solution.py:28
  7.0 1.8 %collective-permute-start = (bf16[256,640]{1,0:T(8,128)(2,1)}, bf16[256,640]{1,0:T(8,128)(2,1)S(1)}, u32[]{:S(2)}, u32[]{:S(2)}) collective-permute-start(bf16[256,640]{1,0:T(8,128)(2,1)} %get-tuple-element.49.refs_4_), channel_id=1, source_target_pairs={{0,4},{4,0},{1,5},{5,1},{2,6},{6,2},{3,7},{7,3},{8,12},{12,8},{9,1... | collective-permute-start | bytes 983048 | tf_op jit(solution)/shard_map/ppermute | solution.py:28
  7.1 1.8 %copy-start.4 = (bf16[64,640]{1,0:T(8,128)(2,1)S(1)}, bf16[64,640]{1,0:T(8,128)(2,1)}, u32[]{:S(2)}) copy-start(bf16[64,640]{1,0:T(8,128)(2,1)} %get-tuple-element.50.refs_0_) | copy-start | bytes 245764
  8.9 10.6 %collective-permute-start.3 = (bf16[64,640]{1,0:T(8,128)(2,1)S(1)}, bf16[64,640]{1,0:T(8,128)(2,1)S(1)}, u32[]{:S(2)}, u32[]{:S(2)}) collective-permute-start(bf16[64,640]{1,0:T(8,128)(2,1)S(1)} %copy-done.4), channel_id=1, source_target_pairs={{0,56},{8,48},{16,40},{24,32},{32,24},{40,16},{48,8},{56,0},{1,57}... | collective-permute-start | bytes 245768 | tf_op jit(solution)/shard_map/ppermute | solution.py:28
  13.8 8.6 %collective-permute-start.2 = (bf16[64,640]{1,0:T(8,128)(2,1)S(1)}, bf16[64,640]{1,0:T(8,128)(2,1)S(1)}, u32[]{:S(2)}, u32[]{:S(2)}) collective-permute-start(bf16[64,640]{1,0:T(8,128)(2,1)S(1)} %copy-done.4), channel_id=1, source_target_pairs={{0,40},{8,32},{16,56},{24,48},{32,8},{40,0},{48,24},{56,16},{1,41}... | collective-permute-start | bytes 245768 | tf_op jit(solution)/shard_map/ppermute | solution.py:28
  15.7 6.7 %collective-permute-start.1 = (bf16[64,640]{1,0:T(8,128)(2,1)S(1)}, bf16[64,640]{1,0:T(8,128)(2,1)S(1)}, u32[]{:S(2)}, u32[]{:S(2)}) collective-permute-start(bf16[64,640]{1,0:T(8,128)(2,1)S(1)} %copy-done.4), channel_id=1, source_target_pairs={{0,16},{8,24},{16,0},{24,8},{32,48},{40,56},{48,32},{56,40},{1,17}... | collective-permute-start | bytes 245768 | tf_op jit(solution)/shard_map/ppermute | solution.py:28
  16.2 8.4 %copy-start = (bf16[256,640]{1,0:T(8,128)(2,1)S(1)}, bf16[256,640]{1,0:T(8,128)(2,1)}, u32[]{:S(2)}) copy-start(bf16[256,640]{1,0:T(8,128)(2,1)} %get-tuple-element.49.refs_4_) | copy-start | bytes 983044
  22.4 17.7 %collective-permute-start.9 = (bf16[640,384]{1,0:T(8,128)(2,1)}, bf16[640,384]{1,0:T(8,128)(2,1)S(1)}, u32[]{:S(2)}, u32[]{:S(2)}) collective-permute-start(bf16[640,384]{1,0:T(8,128)(2,1)} %fusion.4), channel_id=1, source_target_pairs={{0,4},{4,0},{1,5},{5,1},{2,6},{6,2},{3,7},{7,3},{8,12},{12,8},{9,1... | collective-permute-start | bytes 1474568 | tf_op jit(solution)/shard_map/ppermute | solution.py:28
  22.4 2.1 %collective-permute-start.5 = (bf16[256,640]{1,0:T(8,128)(2,1)S(1)}, bf16[256,640]{1,0:T(8,128)(2,1)S(1)}, u32[]{:S(2)}, u32[]{:S(2)}) collective-permute-start(bf16[256,640]{1,0:T(8,128)(2,1)S(1)} %collective-permute-done.4.refs_6_), channel_id=1, source_target_pairs={{0,4},{4,0},{1,5},{5,1},{2,6},{6,2},{3,7},{7,3},{8,12},{12,8},{9,1... | collective-permute-start | bytes 983048 | tf_op jit(solution)/shard_map/ppermute | solution.py:28
  27.0 8.4 %collective-permute-start.8 = (f32[16,256]{1,0:T(8,128)S(1)}, f32[16,256]{1,0:T(8,128)S(1)}, u32[]{:S(2)}, u32[]{:S(2)}) collective-permute-start(f32[16,256]{1,0:T(8,128)S(1)} %shard_map.128.refs_8_), channel_id=1, source_target_pairs={{0,56},{8,48},{16,40},{24,32},{32,24},{40,16},{48,8},{56,0},{1,57}... | collective-permute-start | bytes 49160 | tf_op jit(solution)/shard_map/ppermute | solution.py:28
  31.6 6.7 %collective-permute-start.7 = (f32[16,256]{1,0:T(8,128)S(1)}, f32[16,256]{1,0:T(8,128)S(1)}, u32[]{:S(2)}, u32[]{:S(2)}) collective-permute-start(f32[16,256]{1,0:T(8,128)S(1)} %shard_map.128.refs_8_), channel_id=1, source_target_pairs={{0,40},{8,32},{16,56},{24,48},{32,8},{40,0},{48,24},{56,16},{1,41}... | collective-permute-start | bytes 49160 | tf_op jit(solution)/shard_map/ppermute | solution.py:28
  35.4 4.6 %collective-permute-start.6 = (f32[16,256]{1,0:T(8,128)S(1)}, f32[16,256]{1,0:T(8,128)S(1)}, u32[]{:S(2)}, u32[]{:S(2)}) collective-permute-start(f32[16,256]{1,0:T(8,128)S(1)} %shard_map.128.refs_8_), channel_id=1, source_target_pairs={{0,16},{8,24},{16,0},{24,8},{32,48},{40,56},{48,32},{56,40},{1,17}... | collective-permute-start | bytes 49160 | tf_op jit(solution)/shard_map/ppermute | solution.py:28
  44.4 2.2 %collective-permute-start.10 = (bf16[512,640]{1,0:T(8,128)(2,1)S(1)}, bf16[512,640]{1,0:T(8,128)(2,1)S(1)}, u32[]{:S(2)}, u32[]{:S(2)}) collective-permute-start(bf16[512,640]{1,0:T(8,128)(2,1)S(1)} %get-tuple-element.62), channel_id=1, source_target_pairs={{0,4},{4,0},{1,5},{5,1},{2,6},{6,2},{3,7},{7,3},{8,12},{12,8},{9,1... | collective-permute-start | bytes 1966088 | tf_op jit(solution)/shard_map/ppermute | solution.py:28
  46.7 14.2 %collective-permute-start.11 = (bf16[256,640]{1,0:T(8,128)(2,1)S(1)}, bf16[256,640]{1,0:T(8,128)(2,1)S(1)}, u32[]{:S(2)}, u32[]{:S(2)}) collective-permute-start(bf16[256,640]{1,0:T(8,128)(2,1)S(1)} %add_convert_fusion), channel_id=1, source_target_pairs={{0,8},{8,0},{16,24},{24,16},{32,40},{40,32},{48,56},{56,48},{1,9},... | collective-permute-start | bytes 983048 | tf_op jit(solution)/shard_map/ppermute | solution.py:28
  46.8 11.1 %collective-permute-start.12 = (bf16[64,640]{1,0:T(8,128)(2,1)S(1)}, bf16[64,640]{1,0:T(8,128)(2,1)S(1)}, u32[]{:S(2)}, u32[]{:S(2)}) collective-permute-start(bf16[64,640]{1,0:T(8,128)(2,1)S(1)} %get-tuple-element.69), channel_id=1, source_target_pairs={{0,16},{8,24},{16,0},{24,8},{32,48},{40,56},{48,32},{56,40},{1,17}... | collective-permute-start | bytes 245768 | tf_op jit(solution)/shard_map/ppermute | solution.py:28
  49.1 8.7 %collective-permute-start.13 = (bf16[64,640]{1,0:T(8,128)(2,1)S(1)}, bf16[64,640]{1,0:T(8,128)(2,1)S(1)}, u32[]{:S(2)}, u32[]{:S(2)}) collective-permute-start(bf16[64,640]{1,0:T(8,128)(2,1)S(1)} %get-tuple-element.70), channel_id=1, source_target_pairs={{0,40},{8,32},{16,56},{24,48},{32,8},{40,0},{48,24},{56,16},{1,41}... | collective-permute-start | bytes 245768 | tf_op jit(solution)/shard_map/ppermute | solution.py:28
  51.2 7.1 %collective-permute-start.14 = (bf16[64,640]{1,0:T(8,128)(2,1)S(1)}, bf16[64,640]{1,0:T(8,128)(2,1)S(1)}, u32[]{:S(2)}, u32[]{:S(2)}) collective-permute-start(bf16[64,640]{1,0:T(8,128)(2,1)S(1)} %get-tuple-element.71), channel_id=1, source_target_pairs={{0,56},{8,48},{16,40},{24,32},{32,24},{40,16},{48,8},{56,0},{1,57}... | collective-permute-start | bytes 245768 | tf_op jit(solution)/shard_map/ppermute | solution.py:28
  60.8 10.1 %copy-start.3 = (bf16[1280,320]{0,1:T(8,128)(2,1)S(1)}, bf16[1280,320]{0,1:T(8,128)(2,1)}, u32[]{:S(2)}) copy-start(bf16[1280,320]{0,1:T(8,128)(2,1)} %param.14) | copy-start | bytes 2457604
  61.0 1.8 %collective-permute-start.15 = (bf16[320,640]{1,0:T(8,128)(2,1)S(1)}, bf16[320,640]{1,0:T(8,128)(2,1)S(1)}, u32[]{:S(2)}, u32[]{:S(2)}) collective-permute-start(bf16[320,640]{1,0:T(8,128)(2,1)S(1)} %shard_map.130.y_ref), channel_id=1, source_target_pairs={{0,4},{4,0},{1,5},{5,1},{2,6},{6,2},{3,7},{7,3},{8,12},{12,8},{9,1... | collective-permute-start | bytes 1228808 | tf_op jit(solution)/shard_map/ppermute | solution.py:28
  61.1 9.8 %copy-start.1 = (bf16[1280,320]{0,1:T(8,128)(2,1)S(1)}, bf16[1280,320]{0,1:T(8,128)(2,1)}, u32[]{:S(2)}) copy-start(bf16[1280,320]{0,1:T(8,128)(2,1)} %param.12) | copy-start | bytes 2457604
  61.1 9.8 %copy-start.2 = (bf16[1280,320]{0,1:T(8,128)(2,1)S(1)}, bf16[1280,320]{0,1:T(8,128)(2,1)}, u32[]{:S(2)}) copy-start(bf16[1280,320]{0,1:T(8,128)(2,1)} %param.13) | copy-start | bytes 2457604
  64.1 11.9 %collective-permute-start.16 = (bf16[160,640]{1,0:T(8,128)(2,1)S(1)}, bf16[160,640]{1,0:T(8,128)(2,1)S(1)}, u32[]{:S(2)}, u32[]{:S(2)}) collective-permute-start(bf16[160,640]{1,0:T(8,128)(2,1)S(1)} %get-tuple-element.78), channel_id=1, source_target_pairs={{0,128},{64,192},{128,0},{192,64},{1,129},{65,193},{129,1},{193,65... | collective-permute-start | bytes 614408 | tf_op jit(solution)/shard_map/ppermute | solution.py:28
  67.2 10.2 %collective-permute-start.17 = (bf16[160,640]{1,0:T(8,128)(2,1)S(1)}, bf16[160,640]{1,0:T(8,128)(2,1)S(1)}, u32[]{:S(2)}, u32[]{:S(2)}) collective-permute-start(bf16[160,640]{1,0:T(8,128)(2,1)S(1)} %get-tuple-element.79), channel_id=1, source_target_pairs={{0,64},{64,0},{128,192},{192,128},{1,65},{65,1},{129,193},{193,129... | collective-permute-start | bytes 614408 | tf_op jit(solution)/shard_map/ppermute | solution.py:28
  67.8 9.6 %collective-permute-start.18 = (bf16[160,640]{1,0:T(8,128)(2,1)S(1)}, bf16[160,640]{1,0:T(8,128)(2,1)S(1)}, u32[]{:S(2)}, u32[]{:S(2)}) collective-permute-start(bf16[160,640]{1,0:T(8,128)(2,1)S(1)} %get-tuple-element.80), channel_id=1, source_target_pairs={{0,192},{64,128},{128,64},{192,0},{1,193},{65,129},{129,65},{193,1... | collective-permute-start | bytes 614408 | tf_op jit(solution)/shard_map/ppermute | solution.py:28
  68.4 11.7 %collective-permute-start.20 = (bf16[320,640]{1,0:T(8,128)(2,1)S(1)}, bf16[320,640]{1,0:T(8,128)(2,1)S(1)}, u32[]{:S(2)}, u32[]{:S(2)}) collective-permute-start(bf16[320,640]{1,0:T(8,128)(2,1)S(1)} %get-tuple-element.82), channel_id=1, source_target_pairs={{0,8},{8,0},{16,24},{24,16},{32,40},{40,32},{48,56},{56,48},{1,9},... | collective-permute-start | bytes 1228808 | tf_op jit(solution)/shard_map/ppermute | solution.py:28
  73.7 15.5 %collective-permute-start.24 = (bf16[320,320]{1,0:T(8,128)(2,1)S(1)}, bf16[320,320]{1,0:T(8,128)(2,1)S(1)}, u32[]{:S(2)}, u32[]{:S(2)}) collective-permute-start(bf16[320,320]{1,0:T(8,128)(2,1)S(1)} %get-tuple-element.84), channel_id=1, source_target_pairs={{0,2},{1,3},{2,0},{3,1},{4,6},{5,7},{6,4},{7,5},{8,10},{9,11},{10,... | collective-permute-start | bytes 614408 | tf_op jit(solution)/shard_map/ppermute | solution.py:28
  76.1 13.2 %collective-permute-start.25 = (bf16[320,320]{1,0:T(8,128)(2,1)S(1)}, bf16[320,320]{1,0:T(8,128)(2,1)S(1)}, u32[]{:S(2)}, u32[]{:S(2)}) collective-permute-start(bf16[320,320]{1,0:T(8,128)(2,1)S(1)} %get-tuple-element.85), channel_id=1, source_target_pairs={{0,1},{1,0},{2,3},{3,2},{4,5},{5,4},{6,7},{7,6},{8,9},{9,8},{10,11... | collective-permute-start | bytes 614408 | tf_op jit(solution)/shard_map/ppermute | solution.py:28
  77.5 6.9 %collective-permute-start.19 = (bf16[80,640]{1,0:T(8,128)(2,1)S(1)}, bf16[80,640]{1,0:T(8,128)(2,1)S(1)}, u32[]{:S(2)}, u32[]{:S(2)}) collective-permute-start(bf16[80,640]{1,0:T(8,128)(2,1)S(1)} %slice.96), channel_id=1, source_target_pairs={{0,8},{8,0},{16,24},{24,16},{32,40},{40,32},{48,56},{56,48},{1,9},... | collective-permute-start | bytes 307208 | tf_op jit(solution)/shard_map/ppermute | solution.py:28
  80.3 6.3 %collective-permute-start.21 = (bf16[80,640]{1,0:T(8,128)(2,1)S(1)}, bf16[80,640]{1,0:T(8,128)(2,1)S(1)}, u32[]{:S(2)}, u32[]{:S(2)}) collective-permute-start(bf16[80,640]{1,0:T(8,128)(2,1)S(1)} %get-tuple-element.98), channel_id=1, source_target_pairs={{0,128},{64,192},{128,0},{192,64},{1,129},{65,193},{129,1},{193,65... | collective-permute-start | bytes 307208 | tf_op jit(solution)/shard_map/ppermute | solution.py:28
  83.2 5.9 %collective-permute-start.23 = (bf16[80,640]{1,0:T(8,128)(2,1)S(1)}, bf16[80,640]{1,0:T(8,128)(2,1)S(1)}, u32[]{:S(2)}, u32[]{:S(2)}) collective-permute-start(bf16[80,640]{1,0:T(8,128)(2,1)S(1)} %get-tuple-element.99), channel_id=1, source_target_pairs={{0,192},{64,128},{128,64},{192,0},{1,193},{65,129},{129,65},{193,1... | collective-permute-start | bytes 307208 | tf_op jit(solution)/shard_map/ppermute | solution.py:28
  84.4 4.7 %collective-permute-start.22 = (bf16[80,640]{1,0:T(8,128)(2,1)S(1)}, bf16[80,640]{1,0:T(8,128)(2,1)S(1)}, u32[]{:S(2)}, u32[]{:S(2)}) collective-permute-start(bf16[80,640]{1,0:T(8,128)(2,1)S(1)} %get-tuple-element.100), channel_id=1, source_target_pairs={{0,64},{64,0},{128,192},{192,128},{1,65},{65,1},{129,193},{193,129... | collective-permute-start | bytes 307208 | tf_op jit(solution)/shard_map/ppermute | solution.py:28
  89.3 8.2 %collective-permute-start.27 = (bf16[20,1280]{1,0:T(8,128)(2,1)S(1)}, bf16[20,1280]{1,0:T(8,128)(2,1)S(1)}, u32[]{:S(2)}, u32[]{:S(2)}) collective-permute-start(bf16[20,1280]{1,0:T(8,128)(2,1)S(1)} %get-tuple-element.101), channel_id=1, source_target_pairs={{0,40},{8,32},{16,56},{24,48},{32,8},{40,0},{48,24},{56,16},{1,41}... | collective-permute-start | bytes 153608 | tf_op jit(solution)/shard_map/ppermute | solution.py:28
  93.3 5.4 %collective-permute-start.29 = (bf16[20,1280]{1,0:T(8,128)(2,1)S(1)}, bf16[20,1280]{1,0:T(8,128)(2,1)S(1)}, u32[]{:S(2)}, u32[]{:S(2)}) collective-permute-start(bf16[20,1280]{1,0:T(8,128)(2,1)S(1)} %get-tuple-element.102), channel_id=1, source_target_pairs={{0,56},{8,48},{16,40},{24,32},{32,24},{40,16},{48,8},{56,0},{1,57}... | collective-permute-start | bytes 153608 | tf_op jit(solution)/shard_map/ppermute | solution.py:28
  93.8 6.2 %collective-permute-start.28 = (bf16[20,1280]{1,0:T(8,128)(2,1)S(1)}, bf16[20,1280]{1,0:T(8,128)(2,1)S(1)}, u32[]{:S(2)}, u32[]{:S(2)}) collective-permute-start(bf16[20,1280]{1,0:T(8,128)(2,1)S(1)} %get-tuple-element.103), channel_id=1, source_target_pairs={{0,16},{8,24},{16,0},{24,8},{32,48},{40,56},{48,32},{56,40},{1,17}... | collective-permute-start | bytes 153608 | tf_op jit(solution)/shard_map/ppermute | solution.py:28
  95.9 6.2 %collective-permute-start.26 = (bf16[320,320]{1,0:T(8,128)(2,1)S(1)}, bf16[320,320]{1,0:T(8,128)(2,1)S(1)}, u32[]{:S(2)}, u32[]{:S(2)}) collective-permute-start(bf16[320,320]{1,0:T(8,128)(2,1)S(1)} %get-tuple-element.88), channel_id=1, source_target_pairs={{0,3},{1,2},{2,1},{3,0},{4,7},{5,6},{6,5},{7,4},{8,11},{9,10},{10,... | collective-permute-start | bytes 614408 | tf_op jit(solution)/shard_map/ppermute | solution.py:28

commit v4 on v3

--- a/solution.py
+++ b/solution.py
@@ -93,8 +93,7 @@
 
 def grads_kernel(heads, valid_ref, *refs):
     rows_refs, frame_refs, stat_refs = refs[:4], refs[4:8], refs[8:12]
-    keep_refs, send_ref = refs[12:14], refs[14]
-    dq_refs = refs[15:19]
+    keep_refs, send_refs, dq_refs = refs[12:14], refs[14:16], refs[16:20]
     width = heads * HD
     rows = jnp.concatenate([r[...] for r in rows_refs], axis=0)
     blocks, biases = joined_blocks(valid_ref, frame_refs, SPAN)
@@ -127,10 +126,9 @@
             dvalue = mm(probs, dout)
             for i in range(SPAN):
                 owner, at = j * SPAN + i, slice(i * part, (i + 1) * part)
-                out_ref = send_ref if owner % 2 else keep_refs[owner // 2]
-                low = (owner // 2) * part if owner % 2 else 0
-                out_ref[low : low + part, cut] = dkey[at].astype(out_ref.dtype)
-                out_ref[low : low + part, cut2] = dvalue[at].astype(out_ref.dtype)
+                out_ref = (send_refs if owner % 2 else keep_refs)[owner // 2]
+                out_ref[:, cut] = dkey[at].astype(out_ref.dtype)
+                out_ref[:, cut2] = dvalue[at].astype(out_ref.dtype)
             dq_sum += mm(key, dscores, TN)
             att_sum += mm(value, probs, TN)
         dq_t.append(dq_sum * SCALE)
@@ -180,7 +178,7 @@
 
 def collect_kernel(keep_ref, core_ref, pair_ref, dq_ref, a_ref, b_ref, c_ref, out_ref):
     slab = keep_ref.shape[0]
-    total = keep_ref[...] + core_ref[:slab].astype(F32) + pair_ref[...].astype(F32)
+    total = keep_ref[...] + core_ref[...].astype(F32) + pair_ref[...].astype(F32)
     out_ref[:slab] = total.astype(out_ref.dtype)
     total = dq_ref[...] + a_ref[...].astype(F32) + b_ref[...].astype(F32)
     out_ref[slab:] = (total + c_ref[...].astype(F32)).astype(out_ref.dtype)
@@ -300,7 +298,6 @@
     row_blocks[1:], kv_pair, kv_core, xt, xt_send = lax.optimization_barrier(
         (row_blocks[1:], kv_pair, kv_core, xt, xt_send)
     )
-    xt_other = swap(xt_send, "core")
     frame_blocks = [kv, kv_core, kv_pair, swap(kv_pair, "core")]
     starts = [
         slab * (2 * (zi ^ db) + (ci ^ dc)) for db in (0, 1) for dc in (0, 1)
@@ -313,22 +310,25 @@
         (valid, *row_blocks, *frame_blocks),
         True,
     )
+    stats, xt_send = lax.optimization_barrier((stats, xt_send))
+    xt_other = swap(xt_send, "core")
     all_stats = [stats] + [flip(stats, "z", 8, QUAD[j]) for j in (1, 2, 3)]
 
     all_stats[1:], xt_other = lax.optimization_barrier((all_stats[1:], xt_other))
 
-    keep0, keep1, send, dq0, *dq_sends = call(
+    keep0, keep1, send0, send1, dq0, *dq_sends = call(
         functools.partial(grads_kernel, heads),
         [((slab, 2 * width), F32)] * 2
-        + [((2 * slab, 2 * width), BF), ((own, 2 * width), F32)]
+        + [((slab, 2 * width), BF)] * 2
+        + [((own, 2 * width), F32)]
         + [((own, 2 * width), BF)] * 3,
         (valid, *row_blocks, *frame_blocks, *all_stats),
         True,
     )
 
-    recv = swap(send, "core")
-    pair = (keep1 + recv[slab:].astype(F32)).astype(BF)
-    dq_sends, pair = lax.optimization_barrier((dq_sends, pair))
+    pair = (keep1 + swap(send1, "core").astype(F32)).astype(BF)
+    dq_sends, send0, pair = lax.optimization_barrier((dq_sends, send0, pair))
+    recv = swap(send0, "core")
     pair_recv = flip(pair, "z", 8, 1)
     dq_recv = [flip(d, "z", 8, QUAD[k]) for k, d in zip((1, 2, 3), dq_sends)]
     (grads,) = call(
@@ -379,8 +379,8 @@
     low = total.astype(BF)
     over = [flip(low[k * inner : (k + 1) * inner], "z", 8, QUAD[k]) for k in (2, 1, 3)]
     total = total[:inner] + sum(p.astype(F32) for p in over)
-    inputs = (own_part + sum(p.astype(F32) for p in arrived)).astype(BF)
-    dframes, dinput = inputs[:slab], inputs[slab:]
+    dframes = (own_part[:slab] + sum(p[:slab].astype(F32) for p in arrived)).astype(BF)
+    dinput = (own_part[slab:] + sum(p[slab:].astype(F32) for p in arrived)).astype(BF)
     return (
         dinput[None],
         dframes[None],

time: 105 us -> 105 us (level)
    ppermute x30 -> x31, waiting for transfers between devices: 31.2 us -> 30.7 us  [flip(): return lax.ppermute(x, axis, [(i, i ^ bits) for i in range(size)])]
    ppermute x30 -> x31, starting transfers between devices: 49.7 us -> 49.7 us  [flip(): return lax.ppermute(x, axis, [(i, i ^ bits) for i in range(size)])]
  transfers between devices with their start and end apart: 30 -> 31, of which waited for: 17 -> 17; matrix products, arithmetic and copies ran while one was open for 4% -> 4% of each run, Pallas kernels for 5% -> 3%
where the time goes in v4:
time: 105 us; the launch traced here: 103 us
  starting transfers between devices  49.7 us (47%)
  waiting for transfers between devices  30.7 us (29%)
  Pallas kernels  15.4 us (15%)
  matrix products  2.91 us (3%)
  local copies, waits for them, and re-layouts  1.64 us (2%)
  between operations  1.55 us (1%)
  other arithmetic  1.3 us (1%)
    ppermute x31, starting transfers between devices, flip(): return lax.ppermute(x, axis, [(i, i ^ bits) for i in range(size)])  49.7 us
    ppermute x31, waiting for transfers between devices, flip(): return lax.ppermute(x, axis, [(i, i ^ bits) for i in range(size)])  30.7 us
    pallas_call x4, Pallas kernels, call(): pl.pallas_call(kernel, out_shape=shapes, in_specs=specs, out_specs=[VMEM]...  8.29 us
    pallas_call x1, Pallas kernels, per_device(): pl.pallas_call(project_kernel, out_shape=[jax.ShapeDtypeStruct((own, 2 *...  4.33 us
    dot_general x2, matrix products, mm(): return lax.dot_general(left, right, dims, preferred_element_type=F32)  2.91 us
    pallas_call x1, Pallas kernels, per_device(): pl.pallas_call(inputs_kernel, out_shape=[jax.ShapeDtypeStruct((slab + own...  2.76 us
  transfers between devices with their start and end apart: 31, of which 17 were waited for; matrix products, arithmetic and copies ran while one was open for 4% of the time, Pallas kernels for 3%

profile of v4, /device:TPU:8, one launch (start us, length us, event | category | flops | bytes accessed | tf_op | source)
XLA Modules:
  0.0 103.2 jit_solution(12226350781814169925)
XLA Ops:
  0.7 4.3 %shard_map.127 = (bf16[64,640]{1,0:T(8,128)(2,1)}, bf16[256,640]{1,0:T(8,128)(2,1)}) custom-call(bf16[64,1280]{1,0:T(8,128)(2,1)} %bitcast.31, bf16[64,1280]{1,0:T(8,128)(2,1)} %bitcast.34, bf16[256,1280]{1,0:T(8,128)(2,1)} %bitcast.28, bf16[320,1280]{1,0:T(8,128)(2,1)} %bitcast.22, bf16[320,1280]{1,0:T(8,128)(2,1)} %wo_ref.1, bf16[320,1280]{1,0:T(8,128)(2,1)} %bitcast.24, ...), custom_call_target="tpu_custom_call" | custom-call | tf_op jit(solution)/shard_map/pallas_call | solution.py:266
  5.0 2.0 %collective-permute-start.4 = (bf16[256,640]{1,0:T(8,128)(2,1)}, bf16[256,640]{1,0:T(8,128)(2,1)S(1)}, u32[]{:S(2)}, u32[]{:S(2)}) collective-permute-start(bf16[256,640]{1,0:T(8,128)(2,1)} %get-tuple-element.53.refs_4_), channel_id=1, source_target_pairs={{0,8},{8,0},{16,24},{24,16},{32,40},{40,32},{48,56},{56,48},{1,9},... | collective-permute-start | bytes 983048 | tf_op jit(solution)/shard_map/ppermute | solution.py:28
  7.1 1.1 %fusion.5.xt_ref = bf16[640,384]{1,0:T(8,128)(2,1)S(1)} fusion(s32[640]{0:T(1024)S(1)} %get-tuple-element.117, bf16[64,1280]{1,0:T(8,128)(2,1)S(1)} %bitcast.35, bf16[64,1280]{1,0:T(8,128)(2,1)S(1)} %bitcast.32, bf16[256,1280]{1,0:T(8,128)(2,1)S(1)} %bitcast.29), kind=kOutput, calls=%fused_computation.7 | convolution fusion | flops 633159680 | bytes 1477120 | tf_op jit(solution)/shard_map/dot_general | solution.py:24
  8.1 0.7 collective-permute-done.refs_5_
  8.8 4.9 %collective-permute-start.3 = (bf16[64,640]{1,0:T(8,128)(2,1)S(1)}, bf16[64,640]{1,0:T(8,128)(2,1)S(1)}, u32[]{:S(2)}, u32[]{:S(2)}) collective-permute-start(bf16[64,640]{1,0:T(8,128)(2,1)S(1)} %copy-done.4), channel_id=1, source_target_pairs={{0,56},{8,48},{16,40},{24,32},{32,24},{40,16},{48,8},{56,0},{1,57}... | collective-permute-start | bytes 245768 | tf_op jit(solution)/shard_map/ppermute | solution.py:28
  13.8 1.9 %collective-permute-start.2 = (bf16[64,640]{1,0:T(8,128)(2,1)S(1)}, bf16[64,640]{1,0:T(8,128)(2,1)S(1)}, u32[]{:S(2)}, u32[]{:S(2)}) collective-permute-start(bf16[64,640]{1,0:T(8,128)(2,1)S(1)} %copy-done.4), channel_id=1, source_target_pairs={{0,40},{8,32},{16,56},{24,48},{32,8},{40,0},{48,24},{56,16},{1,41}... | collective-permute-start | bytes 245768 | tf_op jit(solution)/shard_map/ppermute | solution.py:28
  15.7 0.5 collective-permute-start.1
  16.2 1.9 %fusion.4 = bf16[640,384]{1,0:T(8,128)(2,1)} fusion(s32[640]{0:T(1024)S(1)} %get-tuple-element.116, bf16[64,1280]{1,0:T(8,128)(2,1)S(1)} %bitcast.36, bf16[64,1280]{1,0:T(8,128)(2,1)S(1)} %bitcast.33, bf16[256,1280]{1,0:T(8,128)(2,1)S(1)} %bitcast.30), kind=kOutput, calls=%fused_computation.6 | convolution fusion | flops 633159680 | bytes 1477120 | tf_op jit(solution)/shard_map/dot_general | solution.py:24
  18.0 1.4 %collective-permute-done.3.refs_3_ = bf16[64,640]{1,0:T(8,128)(2,1)S(1)} collective-permute-done((bf16[64,640]{1,0:T(8,128)(2,1)S(1)}, bf16[64,640]{1,0:T(8,128)(2,1)S(1)}, u32[]{:S(2)}, u32[]{:S(2)}) %collective-permute-start.3) | collective-permute-done | bytes 81952 | tf_op jit(solution)/shard_map/ppermute | solution.py:28
  19.5 2.9 %collective-permute-done.2.refs_2_ = bf16[64,640]{1,0:T(8,128)(2,1)S(1)} collective-permute-done((bf16[64,640]{1,0:T(8,128)(2,1)S(1)}, bf16[64,640]{1,0:T(8,128)(2,1)S(1)}, u32[]{:S(2)}, u32[]{:S(2)}) %collective-permute-start.2) | collective-permute-done | bytes 81952 | tf_op jit(solution)/shard_map/ppermute | solution.py:28
  23.1 0.9 collective-permute-done.5.refs_7_
  24.0 2.5 %shard_map.128.refs_8_ = f32[16,256]{1,0:T(8,128)S(1)} custom-call(s32[4]{0:T(128)S(1)} %pad_add_fusion.valid_ref, bf16[64,640]{1,0:T(8,128)(2,1)S(1)} %copy-done.4, bf16[64,640]{1,0:T(8,128)(2,1)S(1)} %collective-permute-done.1.refs_1_, bf16[64,640]{1,0:T(8,128)(2,1)S(1)} %collective-permute-done.2.refs_2_, ...), custom_call_target="tpu_custom_call" | custom-call | flops 2 | tf_op jit(solution)/shard_map/pallas_call | solution.py:252
  26.8 4.5 %collective-permute-start.8 = (f32[16,256]{1,0:T(8,128)S(1)}, f32[16,256]{1,0:T(8,128)S(1)}, u32[]{:S(2)}, u32[]{:S(2)}) collective-permute-start(f32[16,256]{1,0:T(8,128)S(1)} %shard_map.128.refs_8_), channel_id=1, source_target_pairs={{0,56},{8,48},{16,40},{24,32},{32,24},{40,16},{48,8},{56,0},{1,57}... | collective-permute-start | bytes 49160 | tf_op jit(solution)/shard_map/ppermute | solution.py:28
  31.2 3.6 %collective-permute-start.7 = (f32[16,256]{1,0:T(8,128)S(1)}, f32[16,256]{1,0:T(8,128)S(1)}, u32[]{:S(2)}, u32[]{:S(2)}) collective-permute-start(f32[16,256]{1,0:T(8,128)S(1)} %shard_map.128.refs_8_), channel_id=1, source_target_pairs={{0,40},{8,32},{16,56},{24,48},{32,8},{40,0},{48,24},{56,16},{1,41}... | collective-permute-start | bytes 49160 | tf_op jit(solution)/shard_map/ppermute | solution.py:28
  34.9 3.1 %collective-permute-done.7.refs_10_ = f32[16,256]{1,0:T(8,128)S(1)} collective-permute-done((f32[16,256]{1,0:T(8,128)S(1)}, f32[16,256]{1,0:T(8,128)S(1)}, u32[]{:S(2)}, u32[]{:S(2)}) %collective-permute-start.7) | collective-permute-done | bytes 16416 | tf_op jit(solution)/shard_map/ppermute | solution.py:28
  38.0 1.5 %collective-permute-done.6.refs_9_ = f32[16,256]{1,0:T(8,128)S(1)} collective-permute-done((f32[16,256]{1,0:T(8,128)S(1)}, f32[16,256]{1,0:T(8,128)S(1)}, u32[]{:S(2)}, u32[]{:S(2)}) %collective-permute-start.6) | collective-permute-done | bytes 16416 | tf_op jit(solution)/shard_map/ppermute | solution.py:28
  39.5 4.3 %shard_map.129 = (f32[256,640]{1,0:T(8,128)S(1)}, f32[256,640]{1,0:T(8,128)S(1)}, bf16[256,640]{1,0:T(8,128)(2,1)S(1)}, bf16[256,640]{1,0:T(8,128)(2,1)S(1)}, f3...) custom-call(s32[4]{0:T(128)S(1)} %pad_add_fusion.valid_ref, ...), custom_call_target="tpu_custom_call" | custom-call | flops 2 | tf_op jit(solution)/shard_map/pallas_call | solution.py:252
  43.9 1.6 %collective-permute-done.10 = bf16[256,640]{1,0:T(8,128)(2,1)S(1)} collective-permute-done((bf16[256,640]{1,0:T(8,128)(2,1)S(1)}, bf16[256,640]{1,0:T(8,128)(2,1)S(1)}, u32[]{:S(2)}, u32[]{:S(2)}) %collective-permute-start.10) | collective-permute-done | bytes 327712 | tf_op jit(solution)/shard_map/ppermute | solution.py:28
  45.9 2.4 %collective-permute-start.13 = (bf16[64,640]{1,0:T(8,128)(2,1)S(1)}, bf16[64,640]{1,0:T(8,128)(2,1)S(1)}, u32[]{:S(2)}, u32[]{:S(2)}) collective-permute-start(bf16[64,640]{1,0:T(8,128)(2,1)S(1)} %get-tuple-element.77), channel_id=1, source_target_pairs={{0,16},{8,24},{16,0},{24,8},{32,48},{40,56},{48,32},{56,40},{1,17}... | collective-permute-start | bytes 245768 | tf_op jit(solution)/shard_map/ppermute | solution.py:28
  48.3 2.1 %collective-permute-start.14 = (bf16[64,640]{1,0:T(8,128)(2,1)S(1)}, bf16[64,640]{1,0:T(8,128)(2,1)S(1)}, u32[]{:S(2)}, u32[]{:S(2)}) collective-permute-start(bf16[64,640]{1,0:T(8,128)(2,1)S(1)} %get-tuple-element.78), channel_id=1, source_target_pairs={{0,40},{8,32},{16,56},{24,48},{32,8},{40,0},{48,24},{56,16},{1,41}... | collective-permute-start | bytes 245768 | tf_op jit(solution)/shard_map/ppermute | solution.py:28
  50.4 1.2 %collective-permute-start.15 = (bf16[64,640]{1,0:T(8,128)(2,1)S(1)}, bf16[64,640]{1,0:T(8,128)(2,1)S(1)}, u32[]{:S(2)}, u32[]{:S(2)}) collective-permute-start(bf16[64,640]{1,0:T(8,128)(2,1)S(1)} %get-tuple-element.79), channel_id=1, source_target_pairs={{0,56},{8,48},{16,40},{24,32},{32,24},{40,16},{48,8},{56,0},{1,57}... | collective-permute-start | bytes 245768 | tf_op jit(solution)/shard_map/ppermute | solution.py:28
  51.5 5.6 %collective-permute-done.13.a_ref = bf16[64,640]{1,0:T(8,128)(2,1)S(1)} collective-permute-done((bf16[64,640]{1,0:T(8,128)(2,1)S(1)}, bf16[64,640]{1,0:T(8,128)(2,1)S(1)}, u32[]{:S(2)}, u32[]{:S(2)}) %collective-permute-start.13) | collective-permute-done | bytes 81952 | tf_op jit(solution)/shard_map/ppermute | solution.py:28
  57.2 0.3 collective-permute-done.15.c_ref
  57.5 2.5 %collective-permute-done.12.pair_ref = bf16[256,640]{1,0:T(8,128)(2,1)S(1)} collective-permute-done((bf16[256,640]{1,0:T(8,128)(2,1)S(1)}, bf16[256,640]{1,0:T(8,128)(2,1)S(1)}, u32[]{:S(2)}, u32[]{:S(2)}) %collective-permute-start.12) | collective-permute-done | bytes 327712 | tf_op jit(solution)/shard_map/ppermute | solution.py:28
  60.2 1.7 %collective-permute-done.16.y2_ref = bf16[320,640]{1,0:T(8,128)(2,1)S(1)} collective-permute-done((bf16[320,640]{1,0:T(8,128)(2,1)S(1)}, bf16[320,640]{1,0:T(8,128)(2,1)S(1)}, u32[]{:S(2)}, u32[]{:S(2)}) %collective-permute-start.16) | collective-permute-done | bytes 409632 | tf_op jit(solution)/shard_map/ppermute | solution.py:28
  61.9 1.3 %shard_map.131 = (f32[160,640]{1,0:T(8,128)S(1)}, bf16[160,640]{1,0:T(8,128)(2,1)S(1)}, bf16[160,640]{1,0:T(8,128)(2,1)S(1)}, bf16[160,640]{1,0:T(8,128)(2,1)S(1...) custom-call(bf16[640,384]{1,0:T(8,128)(2,1)S(1)} %fusion.5.xt_ref, ...), custom_call_target="tpu_custom_call" | custom-call | flops 2 | tf_op jit(solution)/shard_map/pallas_call | solution.py:252
  63.2 3.1 %collective-permute-start.17 = (bf16[160,640]{1,0:T(8,128)(2,1)S(1)}, bf16[160,640]{1,0:T(8,128)(2,1)S(1)}, u32[]{:S(2)}, u32[]{:S(2)}) collective-permute-start(bf16[160,640]{1,0:T(8,128)(2,1)S(1)} %get-tuple-element.86), channel_id=1, source_target_pairs={{0,128},{64,192},{128,0},{192,64},{1,129},{65,193},{129,1},{193,65... | collective-permute-start | bytes 614408 | tf_op jit(solution)/shard_map/ppermute | solution.py:28
  66.3 0.6 collective-permute-start.18
  66.9 0.5 collective-permute-start.19
  67.5 3.0 %collective-permute-start.21 = (bf16[320,640]{1,0:T(8,128)(2,1)S(1)}, bf16[320,640]{1,0:T(8,128)(2,1)S(1)}, u32[]{:S(2)}, u32[]{:S(2)}) collective-permute-start(bf16[320,640]{1,0:T(8,128)(2,1)S(1)} %get-tuple-element.90), channel_id=1, source_target_pairs={{0,8},{8,0},{16,24},{24,16},{32,40},{40,32},{48,56},{56,48},{1,9},... | collective-permute-start | bytes 1228808 | tf_op jit(solution)/shard_map/ppermute | solution.py:28
  70.5 2.8 %shard_map.132 = (f32[320,320]{1,0:T(8,128)S(1)}, bf16[320,320]{1,0:T(8,128)(2,1)S(1)}, bf16[320,320]{1,0:T(8,128)(2,1)S(1)}, bf16[320,320]{1,0:T(8,128)(2,1)S(1)}) custom-call(s32[1]{0:T(128)} %bitcast.where_ref, bf16[320,640]{1,0:T(8,128)(2,1)S(1)} %shard_map.130.y_ref, bf16[320,1280]{1,0:T(8,128)(2,1)S(1)} %bitcast.25, bf16[320,1280]{1,0:T(8,128)(2,1)S(1)} %bitcast.27, ...), custom_call_target="tpu_custom_call" | custom-call | flops 12000000000 | tf_op jit(solution)/shard_map/pallas_call | solution.py:353
  73.2 2.4 %collective-permute-start.25 = (bf16[320,320]{1,0:T(8,128)(2,1)S(1)}, bf16[320,320]{1,0:T(8,128)(2,1)S(1)}, u32[]{:S(2)}, u32[]{:S(2)}) collective-permute-start(bf16[320,320]{1,0:T(8,128)(2,1)S(1)} %get-tuple-element.92), channel_id=1, source_target_pairs={{0,2},{1,3},{2,0},{3,1},{4,6},{5,7},{6,4},{7,5},{8,10},{9,11},{10,... | collective-permute-start | bytes 614408 | tf_op jit(solution)/shard_map/ppermute | solution.py:28
  75.6 1.3 %collective-permute-start.26 = (bf16[320,320]{1,0:T(8,128)(2,1)S(1)}, bf16[320,320]{1,0:T(8,128)(2,1)S(1)}, u32[]{:S(2)}, u32[]{:S(2)}) collective-permute-start(bf16[320,320]{1,0:T(8,128)(2,1)S(1)} %get-tuple-element.93), channel_id=1, source_target_pairs={{0,1},{1,0},{2,3},{3,2},{4,5},{5,4},{6,7},{7,6},{8,9},{9,8},{10,11... | collective-permute-start | bytes 614408 | tf_op jit(solution)/shard_map/ppermute | solution.py:28
  77.1 2.5 %collective-permute-start.20 = (bf16[80,640]{1,0:T(8,128)(2,1)S(1)}, bf16[80,640]{1,0:T(8,128)(2,1)S(1)}, u32[]{:S(2)}, u32[]{:S(2)}) collective-permute-start(bf16[80,640]{1,0:T(8,128)(2,1)S(1)} %slice.124), channel_id=1, source_target_pairs={{0,8},{8,0},{16,24},{24,16},{32,40},{40,32},{48,56},{56,48},{1,9},... | collective-permute-start | bytes 307208 | tf_op jit(solution)/shard_map/ppermute | solution.py:28
  79.8 3.0 %collective-permute-start.22 = (bf16[80,640]{1,0:T(8,128)(2,1)S(1)}, bf16[80,640]{1,0:T(8,128)(2,1)S(1)}, u32[]{:S(2)}, u32[]{:S(2)}) collective-permute-start(bf16[80,640]{1,0:T(8,128)(2,1)S(1)} %get-tuple-element.106), channel_id=1, source_target_pairs={{0,128},{64,192},{128,0},{192,64},{1,129},{65,193},{129,1},{193,65... | collective-permute-start | bytes 307208 | tf_op jit(solution)/shard_map/ppermute | solution.py:28
  82.8 1.2 %collective-permute-start.24 = (bf16[80,640]{1,0:T(8,128)(2,1)S(1)}, bf16[80,640]{1,0:T(8,128)(2,1)S(1)}, u32[]{:S(2)}, u32[]{:S(2)}) collective-permute-start(bf16[80,640]{1,0:T(8,128)(2,1)S(1)} %get-tuple-element.107), channel_id=1, source_target_pairs={{0,192},{64,128},{128,64},{192,0},{1,193},{65,129},{129,65},{193,1... | collective-permute-start | bytes 307208 | tf_op jit(solution)/shard_map/ppermute | solution.py:28
  84.1 2.0 %collective-permute-done.22 = bf16[80,640]{1,0:T(8,128)(2,1)S(1)} collective-permute-done((bf16[80,640]{1,0:T(8,128)(2,1)S(1)}, bf16[80,640]{1,0:T(8,128)(2,1)S(1)}, u32[]{:S(2)}, u32[]{:S(2)}) %collective-permute-start.22) | collective-permute-done | bytes 102432 | tf_op jit(solution)/shard_map/ppermute | solution.py:28
  86.1 2.6 %collective-permute-done.24 = bf16[80,640]{1,0:T(8,128)(2,1)S(1)} collective-permute-done((bf16[80,640]{1,0:T(8,128)(2,1)S(1)}, bf16[80,640]{1,0:T(8,128)(2,1)S(1)}, u32[]{:S(2)}, u32[]{:S(2)}) %collective-permute-start.24) | collective-permute-done | bytes 102432 | tf_op jit(solution)/shard_map/ppermute | solution.py:28
  88.9 3.8 %collective-permute-start.28 = (bf16[20,1280]{1,0:T(8,128)(2,1)S(1)}, bf16[20,1280]{1,0:T(8,128)(2,1)S(1)}, u32[]{:S(2)}, u32[]{:S(2)}) collective-permute-start(bf16[20,1280]{1,0:T(8,128)(2,1)S(1)} %get-tuple-element.109), channel_id=1, source_target_pairs={{0,40},{8,32},{16,56},{24,48},{32,8},{40,0},{48,24},{56,16},{1,41}... | collective-permute-start | bytes 153608 | tf_op jit(solution)/shard_map/ppermute | solution.py:28
  92.6 0.7 collective-permute-start.30
  93.3 2.2 %collective-permute-start.29 = (bf16[20,1280]{1,0:T(8,128)(2,1)S(1)}, bf16[20,1280]{1,0:T(8,128)(2,1)S(1)}, u32[]{:S(2)}, u32[]{:S(2)}) collective-permute-start(bf16[20,1280]{1,0:T(8,128)(2,1)S(1)} %get-tuple-element.111), channel_id=1, source_target_pairs={{0,16},{8,24},{16,0},{24,8},{32,48},{40,56},{48,32},{56,40},{1,17}... | collective-permute-start | bytes 153608 | tf_op jit(solution)/shard_map/ppermute | solution.py:28
  95.5 1.6 %collective-permute-start.27 = (bf16[320,320]{1,0:T(8,128)(2,1)S(1)}, bf16[320,320]{1,0:T(8,128)(2,1)S(1)}, u32[]{:S(2)}, u32[]{:S(2)}) collective-permute-start(bf16[320,320]{1,0:T(8,128)(2,1)S(1)} %get-tuple-element.96), channel_id=1, source_target_pairs={{0,3},{1,2},{2,1},{3,0},{4,7},{5,6},{6,5},{7,4},{8,11},{9,10},{10,... | collective-permute-start | bytes 614408 | tf_op jit(solution)/shard_map/ppermute | solution.py:28
  97.3 0.8 collective-permute-done.30
  98.1 1.4 %collective-permute-done.29 = bf16[20,1280]{1,0:T(8,128)(2,1)S(1)} collective-permute-done((bf16[20,1280]{1,0:T(8,128)(2,1)S(1)}, bf16[20,1280]{1,0:T(8,128)(2,1)S(1)}, u32[]{:S(2)}, u32[]{:S(2)}) %collective-permute-start.29) | collective-permute-done | bytes 51232 | tf_op jit(solution)/shard_map/ppermute | solution.py:28
  99.5 0.7 slice_bitcast_fusion
  100.2 1.4 %collective-permute-done.27 = bf16[320,320]{1,0:T(8,128)(2,1)S(1)} collective-permute-done((bf16[320,320]{1,0:T(8,128)(2,1)S(1)}, bf16[320,320]{1,0:T(8,128)(2,1)S(1)}, u32[]{:S(2)}, u32[]{:S(2)}) %collective-permute-start.27) | collective-permute-done | bytes 204832 | tf_op jit(solution)/shard_map/ppermute | solution.py:28
  101.7 0.8 copy.14
  102.5 0.6 fusion.7
  (57 shorter events, 2.0 us)
Async XLA Ops:
  0.6 6.4 %copy-start.5 = (bf16[1,256,1280]{2,1,0:T(8,128)(2,1)S(1)}, bf16[1,256,1280]{2,1,0:T(8,128)(2,1)}, u32[]{:S(2)}) copy-start(bf16[1,256,1280]{2,1,0:T(8,128)(2,1)} %param.10) | copy-start | bytes 1966084
  0.6 6.4 %copy-start.6 = (bf16[1,64,1280]{2,1,0:T(8,128)(2,1)S(1)}, bf16[1,64,1280]{2,1,0:T(8,128)(2,1)}, u32[]{:S(2)}) copy-start(bf16[1,64,1280]{2,1,0:T(8,128)(2,1)} %param.8) | copy-start | bytes 491524
  0.7 6.4 %copy-start.7 = (bf16[1,64,1280]{2,1,0:T(8,128)(2,1)S(1)}, bf16[1,64,1280]{2,1,0:T(8,128)(2,1)}, u32[]{:S(2)}) copy-start(bf16[1,64,1280]{2,1,0:T(8,128)(2,1)} %param.9) | copy-start | bytes 491524
  5.0 13.0 %collective-permute-start.4 = (bf16[256,640]{1,0:T(8,128)(2,1)}, bf16[256,640]{1,0:T(8,128)(2,1)S(1)}, u32[]{:S(2)}, u32[]{:S(2)}) collective-permute-start(bf16[256,640]{1,0:T(8,128)(2,1)} %get-tuple-element.53.refs_4_), channel_id=1, source_target_pairs={{0,8},{8,0},{16,24},{24,16},{32,40},{40,32},{48,56},{56,48},{1,9},... | collective-permute-start | bytes 983048 | tf_op jit(solution)/shard_map/ppermute | solution.py:28
  7.0 1.8 %collective-permute-start = (bf16[256,640]{1,0:T(8,128)(2,1)}, bf16[256,640]{1,0:T(8,128)(2,1)S(1)}, u32[]{:S(2)}, u32[]{:S(2)}) collective-permute-start(bf16[256,640]{1,0:T(8,128)(2,1)} %get-tuple-element.53.refs_4_), channel_id=1, source_target_pairs={{0,4},{4,0},{1,5},{5,1},{2,6},{6,2},{3,7},{7,3},{8,12},{12,8},{9,1... | collective-permute-start | bytes 983048 | tf_op jit(solution)/shard_map/ppermute | solution.py:28
  7.1 1.8 %copy-start.4 = (bf16[64,640]{1,0:T(8,128)(2,1)S(1)}, bf16[64,640]{1,0:T(8,128)(2,1)}, u32[]{:S(2)}) copy-start(bf16[64,640]{1,0:T(8,128)(2,1)} %get-tuple-element.54.refs_0_) | copy-start | bytes 245764
  8.8 10.6 %collective-permute-start.3 = (bf16[64,640]{1,0:T(8,128)(2,1)S(1)}, bf16[64,640]{1,0:T(8,128)(2,1)S(1)}, u32[]{:S(2)}, u32[]{:S(2)}) collective-permute-start(bf16[64,640]{1,0:T(8,128)(2,1)S(1)} %copy-done.4), channel_id=1, source_target_pairs={{0,56},{8,48},{16,40},{24,32},{32,24},{40,16},{48,8},{56,0},{1,57}... | collective-permute-start | bytes 245768 | tf_op jit(solution)/shard_map/ppermute | solution.py:28
  13.8 8.6 %collective-permute-start.2 = (bf16[64,640]{1,0:T(8,128)(2,1)S(1)}, bf16[64,640]{1,0:T(8,128)(2,1)S(1)}, u32[]{:S(2)}, u32[]{:S(2)}) collective-permute-start(bf16[64,640]{1,0:T(8,128)(2,1)S(1)} %copy-done.4), channel_id=1, source_target_pairs={{0,40},{8,32},{16,56},{24,48},{32,8},{40,0},{48,24},{56,16},{1,41}... | collective-permute-start | bytes 245768 | tf_op jit(solution)/shard_map/ppermute | solution.py:28
  15.7 6.7 %collective-permute-start.1 = (bf16[64,640]{1,0:T(8,128)(2,1)S(1)}, bf16[64,640]{1,0:T(8,128)(2,1)S(1)}, u32[]{:S(2)}, u32[]{:S(2)}) collective-permute-start(bf16[64,640]{1,0:T(8,128)(2,1)S(1)} %copy-done.4), channel_id=1, source_target_pairs={{0,16},{8,24},{16,0},{24,8},{32,48},{40,56},{48,32},{56,40},{1,17}... | collective-permute-start | bytes 245768 | tf_op jit(solution)/shard_map/ppermute | solution.py:28
  16.2 7.8 %copy-start = (bf16[256,640]{1,0:T(8,128)(2,1)S(1)}, bf16[256,640]{1,0:T(8,128)(2,1)}, u32[]{:S(2)}) copy-start(bf16[256,640]{1,0:T(8,128)(2,1)} %get-tuple-element.53.refs_4_) | copy-start | bytes 983044
  22.4 1.6 %collective-permute-start.5 = (bf16[256,640]{1,0:T(8,128)(2,1)S(1)}, bf16[256,640]{1,0:T(8,128)(2,1)S(1)}, u32[]{:S(2)}, u32[]{:S(2)}) collective-permute-start(bf16[256,640]{1,0:T(8,128)(2,1)S(1)} %collective-permute-done.4.refs_6_), channel_id=1, source_target_pairs={{0,4},{4,0},{1,5},{5,1},{2,6},{6,2},{3,7},{7,3},{8,12},{12,8},{9,1... | collective-permute-start | bytes 983048 | tf_op jit(solution)/shard_map/ppermute | solution.py:28
  23.1 3.4 %copy-start.8 = (bf16[640,384]{1,0:T(8,128)(2,1)S(1)}, bf16[640,384]{1,0:T(8,128)(2,1)}, u32[]{:S(2)}) copy-start(bf16[640,384]{1,0:T(8,128)(2,1)} %fusion.4) | copy-start | bytes 1474564
  26.5 13.0 %collective-permute-start.9 = (bf16[640,384]{1,0:T(8,128)(2,1)S(1)}, bf16[640,384]{1,0:T(8,128)(2,1)S(1)}, u32[]{:S(2)}, u32[]{:S(2)}) collective-permute-start(bf16[640,384]{1,0:T(8,128)(2,1)S(1)} %copy-done.8), channel_id=1, source_target_pairs={{0,4},{4,0},{1,5},{5,1},{2,6},{6,2},{3,7},{7,3},{8,12},{12,8},{9,1... | collective-permute-start | bytes 1474568 | tf_op jit(solution)/shard_map/ppermute | solution.py:28
  26.8 8.1 %collective-permute-start.8 = (f32[16,256]{1,0:T(8,128)S(1)}, f32[16,256]{1,0:T(8,128)S(1)}, u32[]{:S(2)}, u32[]{:S(2)}) collective-permute-start(f32[16,256]{1,0:T(8,128)S(1)} %shard_map.128.refs_8_), channel_id=1, source_target_pairs={{0,56},{8,48},{16,40},{24,32},{32,24},{40,16},{48,8},{56,0},{1,57}... | collective-permute-start | bytes 49160 | tf_op jit(solution)/shard_map/ppermute | solution.py:28
  31.2 6.7 %collective-permute-start.7 = (f32[16,256]{1,0:T(8,128)S(1)}, f32[16,256]{1,0:T(8,128)S(1)}, u32[]{:S(2)}, u32[]{:S(2)}) collective-permute-start(f32[16,256]{1,0:T(8,128)S(1)} %shard_map.128.refs_8_), channel_id=1, source_target_pairs={{0,40},{8,32},{16,56},{24,48},{32,8},{40,0},{48,24},{56,16},{1,41}... | collective-permute-start | bytes 49160 | tf_op jit(solution)/shard_map/ppermute | solution.py:28
  34.9 4.6 %collective-permute-start.6 = (f32[16,256]{1,0:T(8,128)S(1)}, f32[16,256]{1,0:T(8,128)S(1)}, u32[]{:S(2)}, u32[]{:S(2)}) collective-permute-start(f32[16,256]{1,0:T(8,128)S(1)} %shard_map.128.refs_8_), channel_id=1, source_target_pairs={{0,16},{8,24},{16,0},{24,8},{32,48},{40,56},{48,32},{56,40},{1,17}... | collective-permute-start | bytes 49160 | tf_op jit(solution)/shard_map/ppermute | solution.py:28
  43.8 1.7 %collective-permute-start.10 = (bf16[256,640]{1,0:T(8,128)(2,1)S(1)}, bf16[256,640]{1,0:T(8,128)(2,1)S(1)}, u32[]{:S(2)}, u32[]{:S(2)}) collective-permute-start(bf16[256,640]{1,0:T(8,128)(2,1)S(1)} %get-tuple-element.73), channel_id=1, source_target_pairs={{0,4},{4,0},{1,5},{5,1},{2,6},{6,2},{3,7},{7,3},{8,12},{12,8},{9,1... | collective-permute-start | bytes 983048 | tf_op jit(solution)/shard_map/ppermute | solution.py:28
  45.6 11.8 %collective-permute-start.11 = (bf16[256,640]{1,0:T(8,128)(2,1)S(1)}, bf16[256,640]{1,0:T(8,128)(2,1)S(1)}, u32[]{:S(2)}, u32[]{:S(2)}) collective-permute-start(bf16[256,640]{1,0:T(8,128)(2,1)S(1)} %get-tuple-element.74), channel_id=1, source_target_pairs={{0,4},{4,0},{1,5},{5,1},{2,6},{6,2},{3,7},{7,3},{8,12},{12,8},{9,1... | collective-permute-start | bytes 983048 | tf_op jit(solution)/shard_map/ppermute | solution.py:28
  45.9 14.1 %collective-permute-start.12 = (bf16[256,640]{1,0:T(8,128)(2,1)S(1)}, bf16[256,640]{1,0:T(8,128)(2,1)S(1)}, u32[]{:S(2)}, u32[]{:S(2)}) collective-permute-start(bf16[256,640]{1,0:T(8,128)(2,1)S(1)} %add_convert_fusion), channel_id=1, source_target_pairs={{0,8},{8,0},{16,24},{24,16},{32,40},{40,32},{48,56},{56,48},{1,9},... | collective-permute-start | bytes 983048 | tf_op jit(solution)/shard_map/ppermute | solution.py:28
  45.9 11.3 %collective-permute-start.13 = (bf16[64,640]{1,0:T(8,128)(2,1)S(1)}, bf16[64,640]{1,0:T(8,128)(2,1)S(1)}, u32[]{:S(2)}, u32[]{:S(2)}) collective-permute-start(bf16[64,640]{1,0:T(8,128)(2,1)S(1)} %get-tuple-element.77), channel_id=1, source_target_pairs={{0,16},{8,24},{16,0},{24,8},{32,48},{40,56},{48,32},{56,40},{1,17}... | collective-permute-start | bytes 245768 | tf_op jit(solution)/shard_map/ppermute | solution.py:28
  48.3 8.9 %collective-permute-start.14 = (bf16[64,640]{1,0:T(8,128)(2,1)S(1)}, bf16[64,640]{1,0:T(8,128)(2,1)S(1)}, u32[]{:S(2)}, u32[]{:S(2)}) collective-permute-start(bf16[64,640]{1,0:T(8,128)(2,1)S(1)} %get-tuple-element.78), channel_id=1, source_target_pairs={{0,40},{8,32},{16,56},{24,48},{32,8},{40,0},{48,24},{56,16},{1,41}... | collective-permute-start | bytes 245768 | tf_op jit(solution)/shard_map/ppermute | solution.py:28
  50.4 7.1 %collective-permute-start.15 = (bf16[64,640]{1,0:T(8,128)(2,1)S(1)}, bf16[64,640]{1,0:T(8,128)(2,1)S(1)}, u32[]{:S(2)}, u32[]{:S(2)}) collective-permute-start(bf16[64,640]{1,0:T(8,128)(2,1)S(1)} %get-tuple-element.79), channel_id=1, source_target_pairs={{0,56},{8,48},{16,40},{24,32},{32,24},{40,16},{48,8},{56,0},{1,57}... | collective-permute-start | bytes 245768 | tf_op jit(solution)/shard_map/ppermute | solution.py:28
  59.9 10.6 %copy-start.3 = (bf16[1280,320]{0,1:T(8,128)(2,1)S(1)}, bf16[1280,320]{0,1:T(8,128)(2,1)}, u32[]{:S(2)}) copy-start(bf16[1280,320]{0,1:T(8,128)(2,1)} %param.14) | copy-start | bytes 2457604
  60.1 1.8 %collective-permute-start.16 = (bf16[320,640]{1,0:T(8,128)(2,1)S(1)}, bf16[320,640]{1,0:T(8,128)(2,1)S(1)}, u32[]{:S(2)}, u32[]{:S(2)}) collective-permute-start(bf16[320,640]{1,0:T(8,128)(2,1)S(1)} %shard_map.130.y_ref), channel_id=1, source_target_pairs={{0,4},{4,0},{1,5},{5,1},{2,6},{6,2},{3,7},{7,3},{8,12},{12,8},{9,1... | collective-permute-start | bytes 1228808 | tf_op jit(solution)/shard_map/ppermute | solution.py:28
  60.2 10.3 %copy-start.1 = (bf16[1280,320]{0,1:T(8,128)(2,1)S(1)}, bf16[1280,320]{0,1:T(8,128)(2,1)}, u32[]{:S(2)}) copy-start(bf16[1280,320]{0,1:T(8,128)(2,1)} %param.12) | copy-start | bytes 2457604
  60.2 10.3 %copy-start.2 = (bf16[1280,320]{0,1:T(8,128)(2,1)S(1)}, bf16[1280,320]{0,1:T(8,128)(2,1)}, u32[]{:S(2)}) copy-start(bf16[1280,320]{0,1:T(8,128)(2,1)} %param.13) | copy-start | bytes 2457604
  63.2 12.4 %collective-permute-start.17 = (bf16[160,640]{1,0:T(8,128)(2,1)S(1)}, bf16[160,640]{1,0:T(8,128)(2,1)S(1)}, u32[]{:S(2)}, u32[]{:S(2)}) collective-permute-start(bf16[160,640]{1,0:T(8,128)(2,1)S(1)} %get-tuple-element.86), channel_id=1, source_target_pairs={{0,128},{64,192},{128,0},{192,64},{1,129},{65,193},{129,1},{193,65... | collective-permute-start | bytes 614408 | tf_op jit(solution)/shard_map/ppermute | solution.py:28
  66.3 10.6 %collective-permute-start.18 = (bf16[160,640]{1,0:T(8,128)(2,1)S(1)}, bf16[160,640]{1,0:T(8,128)(2,1)S(1)}, u32[]{:S(2)}, u32[]{:S(2)}) collective-permute-start(bf16[160,640]{1,0:T(8,128)(2,1)S(1)} %get-tuple-element.87), channel_id=1, source_target_pairs={{0,64},{64,0},{128,192},{192,128},{1,65},{65,1},{129,193},{193,129... | collective-permute-start | bytes 614408 | tf_op jit(solution)/shard_map/ppermute | solution.py:28
  66.9 10.0 %collective-permute-start.19 = (bf16[160,640]{1,0:T(8,128)(2,1)S(1)}, bf16[160,640]{1,0:T(8,128)(2,1)S(1)}, u32[]{:S(2)}, u32[]{:S(2)}) collective-permute-start(bf16[160,640]{1,0:T(8,128)(2,1)S(1)} %get-tuple-element.88), channel_id=1, source_target_pairs={{0,192},{64,128},{128,64},{192,0},{1,193},{65,129},{129,65},{193,1... | collective-permute-start | bytes 614408 | tf_op jit(solution)/shard_map/ppermute | solution.py:28
  67.5 12.2 %collective-permute-start.21 = (bf16[320,640]{1,0:T(8,128)(2,1)S(1)}, bf16[320,640]{1,0:T(8,128)(2,1)S(1)}, u32[]{:S(2)}, u32[]{:S(2)}) collective-permute-start(bf16[320,640]{1,0:T(8,128)(2,1)S(1)} %get-tuple-element.90), channel_id=1, source_target_pairs={{0,8},{8,0},{16,24},{24,16},{32,40},{40,32},{48,56},{56,48},{1,9},... | collective-permute-start | bytes 1228808 | tf_op jit(solution)/shard_map/ppermute | solution.py:28
  73.2 15.5 %collective-permute-start.25 = (bf16[320,320]{1,0:T(8,128)(2,1)S(1)}, bf16[320,320]{1,0:T(8,128)(2,1)S(1)}, u32[]{:S(2)}, u32[]{:S(2)}) collective-permute-start(bf16[320,320]{1,0:T(8,128)(2,1)S(1)} %get-tuple-element.92), channel_id=1, source_target_pairs={{0,2},{1,3},{2,0},{3,1},{4,6},{5,7},{6,4},{7,5},{8,10},{9,11},{10,... | collective-permute-start | bytes 614408 | tf_op jit(solution)/shard_map/ppermute | solution.py:28
  75.6 13.2 %collective-permute-start.26 = (bf16[320,320]{1,0:T(8,128)(2,1)S(1)}, bf16[320,320]{1,0:T(8,128)(2,1)S(1)}, u32[]{:S(2)}, u32[]{:S(2)}) collective-permute-start(bf16[320,320]{1,0:T(8,128)(2,1)S(1)} %get-tuple-element.93), channel_id=1, source_target_pairs={{0,1},{1,0},{2,3},{3,2},{4,5},{5,4},{6,7},{7,6},{8,9},{9,8},{10,11... | collective-permute-start | bytes 614408 | tf_op jit(solution)/shard_map/ppermute | solution.py:28
  77.1 6.9 %collective-permute-start.20 = (bf16[80,640]{1,0:T(8,128)(2,1)S(1)}, bf16[80,640]{1,0:T(8,128)(2,1)S(1)}, u32[]{:S(2)}, u32[]{:S(2)}) collective-permute-start(bf16[80,640]{1,0:T(8,128)(2,1)S(1)} %slice.124), channel_id=1, source_target_pairs={{0,8},{8,0},{16,24},{24,16},{32,40},{40,32},{48,56},{56,48},{1,9},... | collective-permute-start | bytes 307208 | tf_op jit(solution)/shard_map/ppermute | solution.py:28
  79.8 6.3 %collective-permute-start.22 = (bf16[80,640]{1,0:T(8,128)(2,1)S(1)}, bf16[80,640]{1,0:T(8,128)(2,1)S(1)}, u32[]{:S(2)}, u32[]{:S(2)}) collective-permute-start(bf16[80,640]{1,0:T(8,128)(2,1)S(1)} %get-tuple-element.106), channel_id=1, source_target_pairs={{0,128},{64,192},{128,0},{192,64},{1,129},{65,193},{129,1},{193,65... | collective-permute-start | bytes 307208 | tf_op jit(solution)/shard_map/ppermute | solution.py:28
  82.8 5.9 %collective-permute-start.24 = (bf16[80,640]{1,0:T(8,128)(2,1)S(1)}, bf16[80,640]{1,0:T(8,128)(2,1)S(1)}, u32[]{:S(2)}, u32[]{:S(2)}) collective-permute-start(bf16[80,640]{1,0:T(8,128)(2,1)S(1)} %get-tuple-element.107), channel_id=1, source_target_pairs={{0,192},{64,128},{128,64},{192,0},{1,193},{65,129},{129,65},{193,1... | collective-permute-start | bytes 307208 | tf_op jit(solution)/shard_map/ppermute | solution.py:28
  84.0 4.7 %collective-permute-start.23 = (bf16[80,640]{1,0:T(8,128)(2,1)S(1)}, bf16[80,640]{1,0:T(8,128)(2,1)S(1)}, u32[]{:S(2)}, u32[]{:S(2)}) collective-permute-start(bf16[80,640]{1,0:T(8,128)(2,1)S(1)} %get-tuple-element.108), channel_id=1, source_target_pairs={{0,64},{64,0},{128,192},{192,128},{1,65},{65,1},{129,193},{193,129... | collective-permute-start | bytes 307208 | tf_op jit(solution)/shard_map/ppermute | solution.py:28
  88.9 8.4 %collective-permute-start.28 = (bf16[20,1280]{1,0:T(8,128)(2,1)S(1)}, bf16[20,1280]{1,0:T(8,128)(2,1)S(1)}, u32[]{:S(2)}, u32[]{:S(2)}) collective-permute-start(bf16[20,1280]{1,0:T(8,128)(2,1)S(1)} %get-tuple-element.109), channel_id=1, source_target_pairs={{0,40},{8,32},{16,56},{24,48},{32,8},{40,0},{48,24},{56,16},{1,41}... | collective-permute-start | bytes 153608 | tf_op jit(solution)/shard_map/ppermute | solution.py:28
  92.6 5.4 %collective-permute-start.30 = (bf16[20,1280]{1,0:T(8,128)(2,1)S(1)}, bf16[20,1280]{1,0:T(8,128)(2,1)S(1)}, u32[]{:S(2)}, u32[]{:S(2)}) collective-permute-start(bf16[20,1280]{1,0:T(8,128)(2,1)S(1)} %get-tuple-element.110), channel_id=1, source_target_pairs={{0,56},{8,48},{16,40},{24,32},{32,24},{40,16},{48,8},{56,0},{1,57}... | collective-permute-start | bytes 153608 | tf_op jit(solution)/shard_map/ppermute | solution.py:28
  93.3 6.2 %collective-permute-start.29 = (bf16[20,1280]{1,0:T(8,128)(2,1)S(1)}, bf16[20,1280]{1,0:T(8,128)(2,1)S(1)}, u32[]{:S(2)}, u32[]{:S(2)}) collective-permute-start(bf16[20,1280]{1,0:T(8,128)(2,1)S(1)} %get-tuple-element.111), channel_id=1, source_target_pairs={{0,16},{8,24},{16,0},{24,8},{32,48},{40,56},{48,32},{56,40},{1,17}... | collective-permute-start | bytes 153608 | tf_op jit(solution)/shard_map/ppermute | solution.py:28
  95.5 6.2 %collective-permute-start.27 = (bf16[320,320]{1,0:T(8,128)(2,1)S(1)}, bf16[320,320]{1,0:T(8,128)(2,1)S(1)}, u32[]{:S(2)}, u32[]{:S(2)}) collective-permute-start(bf16[320,320]{1,0:T(8,128)(2,1)S(1)} %get-tuple-element.96), channel_id=1, source_target_pairs={{0,3},{1,2},{2,1},{3,0},{4,7},{5,6},{6,5},{7,4},{8,11},{9,10},{10,... | collective-permute-start | bytes 614408 | tf_op jit(solution)/shard_map/ppermute | solution.py:28

commit v5 on v4

--- a/solution.py
+++ b/solution.py
@@ -156,23 +156,28 @@
     left, right, frames, wq, wo, wk, wv, sems,
 ):
     width = wq.shape[0]
-    half = width // 2
-    pairs = [(left_ref, left)]
-    for source, target in ((wq_ref, wq), (wo_ref, wo), (wk_ref, wk), (wv_ref, wv)):
-        pairs += [
-            (source.at[:half], target.at[:half]),
-            (source.at[half:], target.at[half:]),
-        ]
-        if source is wq_ref:
-            pairs.append((right_ref, right))
-        if source is wo_ref:
-            pairs.append((frames_ref, frames))
-    copies = fetch(pairs, sems)
-    for i, (x, w, out, side) in enumerate(
-        ((left, wq, rows_ref, 0), (right, wo, rows_ref, 1), (frames, wk, kv_ref, 0), (frames, wv, kv_ref, 1))
+    step = width // 4
+    groups = []
+    for x, w in (
+        ((left_ref, left), (wq_ref, wq)),
+        ((right_ref, right), (wo_ref, wo)),
+        ((frames_ref, frames), (wk_ref, wk)),
+        (None, (wv_ref, wv)),
     ):
-        for copy in copies[3 * i : 3 * i + 3]:
+        group = [x] if x else []
+        for i in range(4):
+            part = slice(i * step, (i + 1) * step)
+            group.append((w[0].at[part], w[1].at[part]))
+        groups.append(group)
+    copies = fetch([pair for group in groups for pair in group], sems)
+    first = 0
+    for group, (x, w, out, side) in zip(
+        groups,
+        ((left, wq, rows_ref, 0), (right, wo, rows_ref, 1), (frames, wk, kv_ref, 0), (frames, wv, kv_ref, 1)),
+    ):
+        for copy in copies[first : first + len(group)]:
             copy.wait()
+        first += len(group)
         out[:, side * width : (side + 1) * width] = mm(x[...], w[...], NT).astype(BF)
 
 
@@ -273,7 +278,7 @@
         out_specs=[VMEM] * 2,
         scratch_shapes=[pltpu.VMEM((rows, model), BF) for rows in (own, own, slab)]
         + weights
-        + [pltpu.SemaphoreType.DMA((12,))],
+        + [pltpu.SemaphoreType.DMA((19,))],
         compiler_params=pltpu.CompilerParams(vmem_limit_bytes=56 * 1024 * 1024),
     )(rows_in, rows_grad, frames, wq_t, w_out, wk_t, wv_t)
 

time: 105 us -> 105 us (level)
  no operation moved by 1% of the time
where the time goes in v5:
time: 105 us; the launch traced here: 103 us
  starting transfers between devices  49.6 us (47%)
  waiting for transfers between devices  30.8 us (29%)
  Pallas kernels  15.5 us (15%)
  matrix products  2.92 us (3%)
  local copies, waits for them, and re-layouts  1.64 us (2%)
  between operations  1.55 us (1%)
  other arithmetic  1.3 us (1%)
    ppermute x31, starting transfers between devices, flip(): return lax.ppermute(x, axis, [(i, i ^ bits) for i in range(size)])  49.6 us
    ppermute x31, waiting for transfers between devices, flip(): return lax.ppermute(x, axis, [(i, i ^ bits) for i in range(size)])  30.8 us
    pallas_call x4, Pallas kernels, call(): pl.pallas_call(kernel, out_shape=shapes, in_specs=specs, out_specs=[VMEM]...  8.29 us
    pallas_call x1, Pallas kernels, per_device(): pl.pallas_call(project_kernel, out_shape=[jax.ShapeDtypeStruct((own, 2 *...  4.46 us
    dot_general x2, matrix products, mm(): return lax.dot_general(left, right, dims, preferred_element_type=F32)  2.92 us
    pallas_call x1, Pallas kernels, per_device(): pl.pallas_call(inputs_kernel, out_shape=[jax.ShapeDtypeStruct((slab + own...  2.76 us
  transfers between devices with their start and end apart: 31, of which 17 were waited for; matrix products, arithmetic and copies ran while one was open for 4% of the time, Pallas kernels for 3%

profile of v5, /device:TPU:8, one launch (start us, length us, event | category | flops | bytes accessed | tf_op | source)
XLA Modules:
  0.0 103.3 jit_solution(17212684100641296257)
XLA Ops:
  0.7 4.5 %shard_map.127 = (bf16[64,640]{1,0:T(8,128)(2,1)}, bf16[256,640]{1,0:T(8,128)(2,1)}) custom-call(bf16[64,1280]{1,0:T(8,128)(2,1)} %bitcast.31, bf16[64,1280]{1,0:T(8,128)(2,1)} %bitcast.34, bf16[256,1280]{1,0:T(8,128)(2,1)} %bitcast.28, bf16[320,1280]{1,0:T(8,128)(2,1)} %bitcast.22, bf16[320,1280]{1,0:T(8,128)(2,1)} %wo_ref.1, bf16[320,1280]{1,0:T(8,128)(2,1)} %bitcast.24, ...), custom_call_target="tpu_custom_call" | custom-call | tf_op jit(solution)/shard_map/pallas_call | solution.py:271
  5.1 2.0 %collective-permute-start.4 = (bf16[256,640]{1,0:T(8,128)(2,1)}, bf16[256,640]{1,0:T(8,128)(2,1)S(1)}, u32[]{:S(2)}, u32[]{:S(2)}) collective-permute-start(bf16[256,640]{1,0:T(8,128)(2,1)} %get-tuple-element.53.refs_4_), channel_id=1, source_target_pairs={{0,8},{8,0},{16,24},{24,16},{32,40},{40,32},{48,56},{56,48},{1,9},... | collective-permute-start | bytes 983048 | tf_op jit(solution)/shard_map/ppermute | solution.py:28
  7.2 1.1 %fusion.5.xt_ref = bf16[640,384]{1,0:T(8,128)(2,1)S(1)} fusion(s32[640]{0:T(1024)S(1)} %get-tuple-element.117, bf16[64,1280]{1,0:T(8,128)(2,1)S(1)} %bitcast.35, bf16[64,1280]{1,0:T(8,128)(2,1)S(1)} %bitcast.32, bf16[256,1280]{1,0:T(8,128)(2,1)S(1)} %bitcast.29), kind=kOutput, calls=%fused_computation.7 | convolution fusion | flops 633159680 | bytes 1477120 | tf_op jit(solution)/shard_map/dot_general | solution.py:24
  8.3 0.7 collective-permute-done.refs_5_
  9.0 4.9 %collective-permute-start.3 = (bf16[64,640]{1,0:T(8,128)(2,1)S(1)}, bf16[64,640]{1,0:T(8,128)(2,1)S(1)}, u32[]{:S(2)}, u32[]{:S(2)}) collective-permute-start(bf16[64,640]{1,0:T(8,128)(2,1)S(1)} %copy-done.4), channel_id=1, source_target_pairs={{0,56},{8,48},{16,40},{24,32},{32,24},{40,16},{48,8},{56,0},{1,57}... | collective-permute-start | bytes 245768 | tf_op jit(solution)/shard_map/ppermute | solution.py:28
  13.9 1.9 %collective-permute-start.2 = (bf16[64,640]{1,0:T(8,128)(2,1)S(1)}, bf16[64,640]{1,0:T(8,128)(2,1)S(1)}, u32[]{:S(2)}, u32[]{:S(2)}) collective-permute-start(bf16[64,640]{1,0:T(8,128)(2,1)S(1)} %copy-done.4), channel_id=1, source_target_pairs={{0,40},{8,32},{16,56},{24,48},{32,8},{40,0},{48,24},{56,16},{1,41}... | collective-permute-start | bytes 245768 | tf_op jit(solution)/shard_map/ppermute | solution.py:28
  15.8 0.5 collective-permute-start.1
  16.3 1.9 %fusion.4 = bf16[640,384]{1,0:T(8,128)(2,1)} fusion(s32[640]{0:T(1024)S(1)} %get-tuple-element.116, bf16[64,1280]{1,0:T(8,128)(2,1)S(1)} %bitcast.36, bf16[64,1280]{1,0:T(8,128)(2,1)S(1)} %bitcast.33, bf16[256,1280]{1,0:T(8,128)(2,1)S(1)} %bitcast.30), kind=kOutput, calls=%fused_computation.6 | convolution fusion | flops 633159680 | bytes 1477120 | tf_op jit(solution)/shard_map/dot_general | solution.py:24
  18.2 1.5 %collective-permute-done.3.refs_3_ = bf16[64,640]{1,0:T(8,128)(2,1)S(1)} collective-permute-done((bf16[64,640]{1,0:T(8,128)(2,1)S(1)}, bf16[64,640]{1,0:T(8,128)(2,1)S(1)}, u32[]{:S(2)}, u32[]{:S(2)}) %collective-permute-start.3) | collective-permute-done | bytes 81952 | tf_op jit(solution)/shard_map/ppermute | solution.py:28
  19.6 2.9 %collective-permute-done.2.refs_2_ = bf16[64,640]{1,0:T(8,128)(2,1)S(1)} collective-permute-done((bf16[64,640]{1,0:T(8,128)(2,1)S(1)}, bf16[64,640]{1,0:T(8,128)(2,1)S(1)}, u32[]{:S(2)}, u32[]{:S(2)}) %collective-permute-start.2) | collective-permute-done | bytes 81952 | tf_op jit(solution)/shard_map/ppermute | solution.py:28
  23.3 0.9 collective-permute-done.5.refs_7_
  24.2 2.5 %shard_map.128.refs_8_ = f32[16,256]{1,0:T(8,128)S(1)} custom-call(s32[4]{0:T(128)S(1)} %pad_add_fusion.valid_ref, bf16[64,640]{1,0:T(8,128)(2,1)S(1)} %copy-done.4, bf16[64,640]{1,0:T(8,128)(2,1)S(1)} %collective-permute-done.1.refs_1_, bf16[64,640]{1,0:T(8,128)(2,1)S(1)} %collective-permute-done.2.refs_2_, ...), custom_call_target="tpu_custom_call" | custom-call | flops 2 | tf_op jit(solution)/shard_map/pallas_call | solution.py:257
  26.9 4.4 %collective-permute-start.8 = (f32[16,256]{1,0:T(8,128)S(1)}, f32[16,256]{1,0:T(8,128)S(1)}, u32[]{:S(2)}, u32[]{:S(2)}) collective-permute-start(f32[16,256]{1,0:T(8,128)S(1)} %shard_map.128.refs_8_), channel_id=1, source_target_pairs={{0,56},{8,48},{16,40},{24,32},{32,24},{40,16},{48,8},{56,0},{1,57}... | collective-permute-start | bytes 49160 | tf_op jit(solution)/shard_map/ppermute | solution.py:28
  31.4 3.6 %collective-permute-start.7 = (f32[16,256]{1,0:T(8,128)S(1)}, f32[16,256]{1,0:T(8,128)S(1)}, u32[]{:S(2)}, u32[]{:S(2)}) collective-permute-start(f32[16,256]{1,0:T(8,128)S(1)} %shard_map.128.refs_8_), channel_id=1, source_target_pairs={{0,40},{8,32},{16,56},{24,48},{32,8},{40,0},{48,24},{56,16},{1,41}... | collective-permute-start | bytes 49160 | tf_op jit(solution)/shard_map/ppermute | solution.py:28
  35.0 3.1 %collective-permute-done.7.refs_10_ = f32[16,256]{1,0:T(8,128)S(1)} collective-permute-done((f32[16,256]{1,0:T(8,128)S(1)}, f32[16,256]{1,0:T(8,128)S(1)}, u32[]{:S(2)}, u32[]{:S(2)}) %collective-permute-start.7) | collective-permute-done | bytes 16416 | tf_op jit(solution)/shard_map/ppermute | solution.py:28
  38.1 1.5 %collective-permute-done.6.refs_9_ = f32[16,256]{1,0:T(8,128)S(1)} collective-permute-done((f32[16,256]{1,0:T(8,128)S(1)}, f32[16,256]{1,0:T(8,128)S(1)}, u32[]{:S(2)}, u32[]{:S(2)}) %collective-permute-start.6) | collective-permute-done | bytes 16416 | tf_op jit(solution)/shard_map/ppermute | solution.py:28
  39.6 4.3 %shard_map.129 = (f32[256,640]{1,0:T(8,128)S(1)}, f32[256,640]{1,0:T(8,128)S(1)}, bf16[256,640]{1,0:T(8,128)(2,1)S(1)}, bf16[256,640]{1,0:T(8,128)(2,1)S(1)}, f3...) custom-call(s32[4]{0:T(128)S(1)} %pad_add_fusion.valid_ref, ...), custom_call_target="tpu_custom_call" | custom-call | flops 2 | tf_op jit(solution)/shard_map/pallas_call | solution.py:257
  44.1 1.6 %collective-permute-done.10 = bf16[256,640]{1,0:T(8,128)(2,1)S(1)} collective-permute-done((bf16[256,640]{1,0:T(8,128)(2,1)S(1)}, bf16[256,640]{1,0:T(8,128)(2,1)S(1)}, u32[]{:S(2)}, u32[]{:S(2)}) %collective-permute-start.10) | collective-permute-done | bytes 327712 | tf_op jit(solution)/shard_map/ppermute | solution.py:28
  46.0 2.4 %collective-permute-start.13 = (bf16[64,640]{1,0:T(8,128)(2,1)S(1)}, bf16[64,640]{1,0:T(8,128)(2,1)S(1)}, u32[]{:S(2)}, u32[]{:S(2)}) collective-permute-start(bf16[64,640]{1,0:T(8,128)(2,1)S(1)} %get-tuple-element.77), channel_id=1, source_target_pairs={{0,16},{8,24},{16,0},{24,8},{32,48},{40,56},{48,32},{56,40},{1,17}... | collective-permute-start | bytes 245768 | tf_op jit(solution)/shard_map/ppermute | solution.py:28
  48.4 2.1 %collective-permute-start.14 = (bf16[64,640]{1,0:T(8,128)(2,1)S(1)}, bf16[64,640]{1,0:T(8,128)(2,1)S(1)}, u32[]{:S(2)}, u32[]{:S(2)}) collective-permute-start(bf16[64,640]{1,0:T(8,128)(2,1)S(1)} %get-tuple-element.78), channel_id=1, source_target_pairs={{0,40},{8,32},{16,56},{24,48},{32,8},{40,0},{48,24},{56,16},{1,41}... | collective-permute-start | bytes 245768 | tf_op jit(solution)/shard_map/ppermute | solution.py:28
  50.5 1.2 %collective-permute-start.15 = (bf16[64,640]{1,0:T(8,128)(2,1)S(1)}, bf16[64,640]{1,0:T(8,128)(2,1)S(1)}, u32[]{:S(2)}, u32[]{:S(2)}) collective-permute-start(bf16[64,640]{1,0:T(8,128)(2,1)S(1)} %get-tuple-element.79), channel_id=1, source_target_pairs={{0,56},{8,48},{16,40},{24,32},{32,24},{40,16},{48,8},{56,0},{1,57}... | collective-permute-start | bytes 245768 | tf_op jit(solution)/shard_map/ppermute | solution.py:28
  51.7 5.6 %collective-permute-done.13.a_ref = bf16[64,640]{1,0:T(8,128)(2,1)S(1)} collective-permute-done((bf16[64,640]{1,0:T(8,128)(2,1)S(1)}, bf16[64,640]{1,0:T(8,128)(2,1)S(1)}, u32[]{:S(2)}, u32[]{:S(2)}) %collective-permute-start.13) | collective-permute-done | bytes 81952 | tf_op jit(solution)/shard_map/ppermute | solution.py:28
  57.3 0.3 collective-permute-done.15.c_ref
  57.6 2.5 %collective-permute-done.12.pair_ref = bf16[256,640]{1,0:T(8,128)(2,1)S(1)} collective-permute-done((bf16[256,640]{1,0:T(8,128)(2,1)S(1)}, bf16[256,640]{1,0:T(8,128)(2,1)S(1)}, u32[]{:S(2)}, u32[]{:S(2)}) %collective-permute-start.12) | collective-permute-done | bytes 327712 | tf_op jit(solution)/shard_map/ppermute | solution.py:28
  60.3 1.7 %collective-permute-done.16.y2_ref = bf16[320,640]{1,0:T(8,128)(2,1)S(1)} collective-permute-done((bf16[320,640]{1,0:T(8,128)(2,1)S(1)}, bf16[320,640]{1,0:T(8,128)(2,1)S(1)}, u32[]{:S(2)}, u32[]{:S(2)}) %collective-permute-start.16) | collective-permute-done | bytes 409632 | tf_op jit(solution)/shard_map/ppermute | solution.py:28
  62.1 1.3 %shard_map.131 = (f32[160,640]{1,0:T(8,128)S(1)}, bf16[160,640]{1,0:T(8,128)(2,1)S(1)}, bf16[160,640]{1,0:T(8,128)(2,1)S(1)}, bf16[160,640]{1,0:T(8,128)(2,1)S(1...) custom-call(bf16[640,384]{1,0:T(8,128)(2,1)S(1)} %fusion.5.xt_ref, ...), custom_call_target="tpu_custom_call" | custom-call | flops 2 | tf_op jit(solution)/shard_map/pallas_call | solution.py:257
  63.4 3.1 %collective-permute-start.17 = (bf16[160,640]{1,0:T(8,128)(2,1)S(1)}, bf16[160,640]{1,0:T(8,128)(2,1)S(1)}, u32[]{:S(2)}, u32[]{:S(2)}) collective-permute-start(bf16[160,640]{1,0:T(8,128)(2,1)S(1)} %get-tuple-element.86), channel_id=1, source_target_pairs={{0,128},{64,192},{128,0},{192,64},{1,129},{65,193},{129,1},{193,65... | collective-permute-start | bytes 614408 | tf_op jit(solution)/shard_map/ppermute | solution.py:28
  66.5 0.6 collective-permute-start.18
  67.1 0.6 collective-permute-start.19
  67.6 3.0 %collective-permute-start.21 = (bf16[320,640]{1,0:T(8,128)(2,1)S(1)}, bf16[320,640]{1,0:T(8,128)(2,1)S(1)}, u32[]{:S(2)}, u32[]{:S(2)}) collective-permute-start(bf16[320,640]{1,0:T(8,128)(2,1)S(1)} %get-tuple-element.90), channel_id=1, source_target_pairs={{0,8},{8,0},{16,24},{24,16},{32,40},{40,32},{48,56},{56,48},{1,9},... | collective-permute-start | bytes 1228808 | tf_op jit(solution)/shard_map/ppermute | solution.py:28
  70.6 2.8 %shard_map.132 = (f32[320,320]{1,0:T(8,128)S(1)}, bf16[320,320]{1,0:T(8,128)(2,1)S(1)}, bf16[320,320]{1,0:T(8,128)(2,1)S(1)}, bf16[320,320]{1,0:T(8,128)(2,1)S(1)}) custom-call(s32[1]{0:T(128)} %bitcast.where_ref, bf16[320,640]{1,0:T(8,128)(2,1)S(1)} %shard_map.130.y_ref, bf16[320,1280]{1,0:T(8,128)(2,1)S(1)} %bitcast.25, bf16[320,1280]{1,0:T(8,128)(2,1)S(1)} %bitcast.27, ...), custom_call_target="tpu_custom_call" | custom-call | flops 12000000000 | tf_op jit(solution)/shard_map/pallas_call | solution.py:358
  73.4 2.4 %collective-permute-start.25 = (bf16[320,320]{1,0:T(8,128)(2,1)S(1)}, bf16[320,320]{1,0:T(8,128)(2,1)S(1)}, u32[]{:S(2)}, u32[]{:S(2)}) collective-permute-start(bf16[320,320]{1,0:T(8,128)(2,1)S(1)} %get-tuple-element.92), channel_id=1, source_target_pairs={{0,2},{1,3},{2,0},{3,1},{4,6},{5,7},{6,4},{7,5},{8,10},{9,11},{10,... | collective-permute-start | bytes 614408 | tf_op jit(solution)/shard_map/ppermute | solution.py:28
  75.8 1.3 %collective-permute-start.26 = (bf16[320,320]{1,0:T(8,128)(2,1)S(1)}, bf16[320,320]{1,0:T(8,128)(2,1)S(1)}, u32[]{:S(2)}, u32[]{:S(2)}) collective-permute-start(bf16[320,320]{1,0:T(8,128)(2,1)S(1)} %get-tuple-element.93), channel_id=1, source_target_pairs={{0,1},{1,0},{2,3},{3,2},{4,5},{5,4},{6,7},{7,6},{8,9},{9,8},{10,11... | collective-permute-start | bytes 614408 | tf_op jit(solution)/shard_map/ppermute | solution.py:28
  77.3 2.5 %collective-permute-start.20 = (bf16[80,640]{1,0:T(8,128)(2,1)S(1)}, bf16[80,640]{1,0:T(8,128)(2,1)S(1)}, u32[]{:S(2)}, u32[]{:S(2)}) collective-permute-start(bf16[80,640]{1,0:T(8,128)(2,1)S(1)} %slice.124), channel_id=1, source_target_pairs={{0,8},{8,0},{16,24},{24,16},{32,40},{40,32},{48,56},{56,48},{1,9},... | collective-permute-start | bytes 307208 | tf_op jit(solution)/shard_map/ppermute | solution.py:28
  80.0 3.0 %collective-permute-start.22 = (bf16[80,640]{1,0:T(8,128)(2,1)S(1)}, bf16[80,640]{1,0:T(8,128)(2,1)S(1)}, u32[]{:S(2)}, u32[]{:S(2)}) collective-permute-start(bf16[80,640]{1,0:T(8,128)(2,1)S(1)} %get-tuple-element.106), channel_id=1, source_target_pairs={{0,128},{64,192},{128,0},{192,64},{1,129},{65,193},{129,1},{193,65... | collective-permute-start | bytes 307208 | tf_op jit(solution)/shard_map/ppermute | solution.py:28
  82.9 1.2 %collective-permute-start.24 = (bf16[80,640]{1,0:T(8,128)(2,1)S(1)}, bf16[80,640]{1,0:T(8,128)(2,1)S(1)}, u32[]{:S(2)}, u32[]{:S(2)}) collective-permute-start(bf16[80,640]{1,0:T(8,128)(2,1)S(1)} %get-tuple-element.107), channel_id=1, source_target_pairs={{0,192},{64,128},{128,64},{192,0},{1,193},{65,129},{129,65},{193,1... | collective-permute-start | bytes 307208 | tf_op jit(solution)/shard_map/ppermute | solution.py:28
  84.2 2.0 %collective-permute-done.22 = bf16[80,640]{1,0:T(8,128)(2,1)S(1)} collective-permute-done((bf16[80,640]{1,0:T(8,128)(2,1)S(1)}, bf16[80,640]{1,0:T(8,128)(2,1)S(1)}, u32[]{:S(2)}, u32[]{:S(2)}) %collective-permute-start.22) | collective-permute-done | bytes 102432 | tf_op jit(solution)/shard_map/ppermute | solution.py:28
  86.2 2.6 %collective-permute-done.24 = bf16[80,640]{1,0:T(8,128)(2,1)S(1)} collective-permute-done((bf16[80,640]{1,0:T(8,128)(2,1)S(1)}, bf16[80,640]{1,0:T(8,128)(2,1)S(1)}, u32[]{:S(2)}, u32[]{:S(2)}) %collective-permute-start.24) | collective-permute-done | bytes 102432 | tf_op jit(solution)/shard_map/ppermute | solution.py:28
  89.0 3.8 %collective-permute-start.28 = (bf16[20,1280]{1,0:T(8,128)(2,1)S(1)}, bf16[20,1280]{1,0:T(8,128)(2,1)S(1)}, u32[]{:S(2)}, u32[]{:S(2)}) collective-permute-start(bf16[20,1280]{1,0:T(8,128)(2,1)S(1)} %get-tuple-element.109), channel_id=1, source_target_pairs={{0,40},{8,32},{16,56},{24,48},{32,8},{40,0},{48,24},{56,16},{1,41}... | collective-permute-start | bytes 153608 | tf_op jit(solution)/shard_map/ppermute | solution.py:28
  92.8 0.6 collective-permute-start.30
  93.4 2.2 %collective-permute-start.29 = (bf16[20,1280]{1,0:T(8,128)(2,1)S(1)}, bf16[20,1280]{1,0:T(8,128)(2,1)S(1)}, u32[]{:S(2)}, u32[]{:S(2)}) collective-permute-start(bf16[20,1280]{1,0:T(8,128)(2,1)S(1)} %get-tuple-element.111), channel_id=1, source_target_pairs={{0,16},{8,24},{16,0},{24,8},{32,48},{40,56},{48,32},{56,40},{1,17}... | collective-permute-start | bytes 153608 | tf_op jit(solution)/shard_map/ppermute | solution.py:28
  95.6 1.6 %collective-permute-start.27 = (bf16[320,320]{1,0:T(8,128)(2,1)S(1)}, bf16[320,320]{1,0:T(8,128)(2,1)S(1)}, u32[]{:S(2)}, u32[]{:S(2)}) collective-permute-start(bf16[320,320]{1,0:T(8,128)(2,1)S(1)} %get-tuple-element.96), channel_id=1, source_target_pairs={{0,3},{1,2},{2,1},{3,0},{4,7},{5,6},{6,5},{7,4},{8,11},{9,10},{10,... | collective-permute-start | bytes 614408 | tf_op jit(solution)/shard_map/ppermute | solution.py:28
  97.4 0.8 collective-permute-done.30
  98.2 1.4 %collective-permute-done.29 = bf16[20,1280]{1,0:T(8,128)(2,1)S(1)} collective-permute-done((bf16[20,1280]{1,0:T(8,128)(2,1)S(1)}, bf16[20,1280]{1,0:T(8,128)(2,1)S(1)}, u32[]{:S(2)}, u32[]{:S(2)}) %collective-permute-start.29) | collective-permute-done | bytes 51232 | tf_op jit(solution)/shard_map/ppermute | solution.py:28
  99.7 0.7 slice_bitcast_fusion
  100.4 1.4 %collective-permute-done.27 = bf16[320,320]{1,0:T(8,128)(2,1)S(1)} collective-permute-done((bf16[320,320]{1,0:T(8,128)(2,1)S(1)}, bf16[320,320]{1,0:T(8,128)(2,1)S(1)}, u32[]{:S(2)}, u32[]{:S(2)}) %collective-permute-start.27) | collective-permute-done | bytes 204832 | tf_op jit(solution)/shard_map/ppermute | solution.py:28
  101.9 0.8 copy.14
  102.7 0.6 fusion.7
  (57 shorter events, 1.9 us)
Async XLA Ops:
  0.6 6.5 %copy-start.5 = (bf16[1,256,1280]{2,1,0:T(8,128)(2,1)S(1)}, bf16[1,256,1280]{2,1,0:T(8,128)(2,1)}, u32[]{:S(2)}) copy-start(bf16[1,256,1280]{2,1,0:T(8,128)(2,1)} %param.10) | copy-start | bytes 1966084
  0.6 6.5 %copy-start.6 = (bf16[1,64,1280]{2,1,0:T(8,128)(2,1)S(1)}, bf16[1,64,1280]{2,1,0:T(8,128)(2,1)}, u32[]{:S(2)}) copy-start(bf16[1,64,1280]{2,1,0:T(8,128)(2,1)} %param.8) | copy-start | bytes 491524
  0.7 6.5 %copy-start.7 = (bf16[1,64,1280]{2,1,0:T(8,128)(2,1)S(1)}, bf16[1,64,1280]{2,1,0:T(8,128)(2,1)}, u32[]{:S(2)}) copy-start(bf16[1,64,1280]{2,1,0:T(8,128)(2,1)} %param.9) | copy-start | bytes 491524
  5.1 13.0 %collective-permute-start.4 = (bf16[256,640]{1,0:T(8,128)(2,1)}, bf16[256,640]{1,0:T(8,128)(2,1)S(1)}, u32[]{:S(2)}, u32[]{:S(2)}) collective-permute-start(bf16[256,640]{1,0:T(8,128)(2,1)} %get-tuple-element.53.refs_4_), channel_id=1, source_target_pairs={{0,8},{8,0},{16,24},{24,16},{32,40},{40,32},{48,56},{56,48},{1,9},... | collective-permute-start | bytes 983048 | tf_op jit(solution)/shard_map/ppermute | solution.py:28
  7.1 1.8 %collective-permute-start = (bf16[256,640]{1,0:T(8,128)(2,1)}, bf16[256,640]{1,0:T(8,128)(2,1)S(1)}, u32[]{:S(2)}, u32[]{:S(2)}) collective-permute-start(bf16[256,640]{1,0:T(8,128)(2,1)} %get-tuple-element.53.refs_4_), channel_id=1, source_target_pairs={{0,4},{4,0},{1,5},{5,1},{2,6},{6,2},{3,7},{7,3},{8,12},{12,8},{9,1... | collective-permute-start | bytes 983048 | tf_op jit(solution)/shard_map/ppermute | solution.py:28
  7.2 1.8 %copy-start.4 = (bf16[64,640]{1,0:T(8,128)(2,1)S(1)}, bf16[64,640]{1,0:T(8,128)(2,1)}, u32[]{:S(2)}) copy-start(bf16[64,640]{1,0:T(8,128)(2,1)} %get-tuple-element.54.refs_0_) | copy-start | bytes 245764
  9.0 10.6 %collective-permute-start.3 = (bf16[64,640]{1,0:T(8,128)(2,1)S(1)}, bf16[64,640]{1,0:T(8,128)(2,1)S(1)}, u32[]{:S(2)}, u32[]{:S(2)}) collective-permute-start(bf16[64,640]{1,0:T(8,128)(2,1)S(1)} %copy-done.4), channel_id=1, source_target_pairs={{0,56},{8,48},{16,40},{24,32},{32,24},{40,16},{48,8},{56,0},{1,57}... | collective-permute-start | bytes 245768 | tf_op jit(solution)/shard_map/ppermute | solution.py:28
  13.9 8.6 %collective-permute-start.2 = (bf16[64,640]{1,0:T(8,128)(2,1)S(1)}, bf16[64,640]{1,0:T(8,128)(2,1)S(1)}, u32[]{:S(2)}, u32[]{:S(2)}) collective-permute-start(bf16[64,640]{1,0:T(8,128)(2,1)S(1)} %copy-done.4), channel_id=1, source_target_pairs={{0,40},{8,32},{16,56},{24,48},{32,8},{40,0},{48,24},{56,16},{1,41}... | collective-permute-start | bytes 245768 | tf_op jit(solution)/shard_map/ppermute | solution.py:28
  15.8 6.7 %collective-permute-start.1 = (bf16[64,640]{1,0:T(8,128)(2,1)S(1)}, bf16[64,640]{1,0:T(8,128)(2,1)S(1)}, u32[]{:S(2)}, u32[]{:S(2)}) collective-permute-start(bf16[64,640]{1,0:T(8,128)(2,1)S(1)} %copy-done.4), channel_id=1, source_target_pairs={{0,16},{8,24},{16,0},{24,8},{32,48},{40,56},{48,32},{56,40},{1,17}... | collective-permute-start | bytes 245768 | tf_op jit(solution)/shard_map/ppermute | solution.py:28
  16.3 7.9 %copy-start = (bf16[256,640]{1,0:T(8,128)(2,1)S(1)}, bf16[256,640]{1,0:T(8,128)(2,1)}, u32[]{:S(2)}) copy-start(bf16[256,640]{1,0:T(8,128)(2,1)} %get-tuple-element.53.refs_4_) | copy-start | bytes 983044
  22.5 1.6 %collective-permute-start.5 = (bf16[256,640]{1,0:T(8,128)(2,1)S(1)}, bf16[256,640]{1,0:T(8,128)(2,1)S(1)}, u32[]{:S(2)}, u32[]{:S(2)}) collective-permute-start(bf16[256,640]{1,0:T(8,128)(2,1)S(1)} %collective-permute-done.4.refs_6_), channel_id=1, source_target_pairs={{0,4},{4,0},{1,5},{5,1},{2,6},{6,2},{3,7},{7,3},{8,12},{12,8},{9,1... | collective-permute-start | bytes 983048 | tf_op jit(solution)/shard_map/ppermute | solution.py:28
  23.3 3.4 %copy-start.8 = (bf16[640,384]{1,0:T(8,128)(2,1)S(1)}, bf16[640,384]{1,0:T(8,128)(2,1)}, u32[]{:S(2)}) copy-start(bf16[640,384]{1,0:T(8,128)(2,1)} %fusion.4) | copy-start | bytes 1474564
  26.7 12.9 %collective-permute-start.9 = (bf16[640,384]{1,0:T(8,128)(2,1)S(1)}, bf16[640,384]{1,0:T(8,128)(2,1)S(1)}, u32[]{:S(2)}, u32[]{:S(2)}) collective-permute-start(bf16[640,384]{1,0:T(8,128)(2,1)S(1)} %copy-done.8), channel_id=1, source_target_pairs={{0,4},{4,0},{1,5},{5,1},{2,6},{6,2},{3,7},{7,3},{8,12},{12,8},{9,1... | collective-permute-start | bytes 1474568 | tf_op jit(solution)/shard_map/ppermute | solution.py:28
  26.9 8.1 %collective-permute-start.8 = (f32[16,256]{1,0:T(8,128)S(1)}, f32[16,256]{1,0:T(8,128)S(1)}, u32[]{:S(2)}, u32[]{:S(2)}) collective-permute-start(f32[16,256]{1,0:T(8,128)S(1)} %shard_map.128.refs_8_), channel_id=1, source_target_pairs={{0,56},{8,48},{16,40},{24,32},{32,24},{40,16},{48,8},{56,0},{1,57}... | collective-permute-start | bytes 49160 | tf_op jit(solution)/shard_map/ppermute | solution.py:28
  31.4 6.7 %collective-permute-start.7 = (f32[16,256]{1,0:T(8,128)S(1)}, f32[16,256]{1,0:T(8,128)S(1)}, u32[]{:S(2)}, u32[]{:S(2)}) collective-permute-start(f32[16,256]{1,0:T(8,128)S(1)} %shard_map.128.refs_8_), channel_id=1, source_target_pairs={{0,40},{8,32},{16,56},{24,48},{32,8},{40,0},{48,24},{56,16},{1,41}... | collective-permute-start | bytes 49160 | tf_op jit(solution)/shard_map/ppermute | solution.py:28
  35.0 4.6 %collective-permute-start.6 = (f32[16,256]{1,0:T(8,128)S(1)}, f32[16,256]{1,0:T(8,128)S(1)}, u32[]{:S(2)}, u32[]{:S(2)}) collective-permute-start(f32[16,256]{1,0:T(8,128)S(1)} %shard_map.128.refs_8_), channel_id=1, source_target_pairs={{0,16},{8,24},{16,0},{24,8},{32,48},{40,56},{48,32},{56,40},{1,17}... | collective-permute-start | bytes 49160 | tf_op jit(solution)/shard_map/ppermute | solution.py:28
  44.0 1.7 %collective-permute-start.10 = (bf16[256,640]{1,0:T(8,128)(2,1)S(1)}, bf16[256,640]{1,0:T(8,128)(2,1)S(1)}, u32[]{:S(2)}, u32[]{:S(2)}) collective-permute-start(bf16[256,640]{1,0:T(8,128)(2,1)S(1)} %get-tuple-element.73), channel_id=1, source_target_pairs={{0,4},{4,0},{1,5},{5,1},{2,6},{6,2},{3,7},{7,3},{8,12},{12,8},{9,1... | collective-permute-start | bytes 983048 | tf_op jit(solution)/shard_map/ppermute | solution.py:28
  45.8 11.8 %collective-permute-start.11 = (bf16[256,640]{1,0:T(8,128)(2,1)S(1)}, bf16[256,640]{1,0:T(8,128)(2,1)S(1)}, u32[]{:S(2)}, u32[]{:S(2)}) collective-permute-start(bf16[256,640]{1,0:T(8,128)(2,1)S(1)} %get-tuple-element.74), channel_id=1, source_target_pairs={{0,4},{4,0},{1,5},{5,1},{2,6},{6,2},{3,7},{7,3},{8,12},{12,8},{9,1... | collective-permute-start | bytes 983048 | tf_op jit(solution)/shard_map/ppermute | solution.py:28
  46.0 14.1 %collective-permute-start.12 = (bf16[256,640]{1,0:T(8,128)(2,1)S(1)}, bf16[256,640]{1,0:T(8,128)(2,1)S(1)}, u32[]{:S(2)}, u32[]{:S(2)}) collective-permute-start(bf16[256,640]{1,0:T(8,128)(2,1)S(1)} %add_convert_fusion), channel_id=1, source_target_pairs={{0,8},{8,0},{16,24},{24,16},{32,40},{40,32},{48,56},{56,48},{1,9},... | collective-permute-start | bytes 983048 | tf_op jit(solution)/shard_map/ppermute | solution.py:28
  46.0 11.3 %collective-permute-start.13 = (bf16[64,640]{1,0:T(8,128)(2,1)S(1)}, bf16[64,640]{1,0:T(8,128)(2,1)S(1)}, u32[]{:S(2)}, u32[]{:S(2)}) collective-permute-start(bf16[64,640]{1,0:T(8,128)(2,1)S(1)} %get-tuple-element.77), channel_id=1, source_target_pairs={{0,16},{8,24},{16,0},{24,8},{32,48},{40,56},{48,32},{56,40},{1,17}... | collective-permute-start | bytes 245768 | tf_op jit(solution)/shard_map/ppermute | solution.py:28
  48.4 8.9 %collective-permute-start.14 = (bf16[64,640]{1,0:T(8,128)(2,1)S(1)}, bf16[64,640]{1,0:T(8,128)(2,1)S(1)}, u32[]{:S(2)}, u32[]{:S(2)}) collective-permute-start(bf16[64,640]{1,0:T(8,128)(2,1)S(1)} %get-tuple-element.78), channel_id=1, source_target_pairs={{0,40},{8,32},{16,56},{24,48},{32,8},{40,0},{48,24},{56,16},{1,41}... | collective-permute-start | bytes 245768 | tf_op jit(solution)/shard_map/ppermute | solution.py:28
  50.5 7.1 %collective-permute-start.15 = (bf16[64,640]{1,0:T(8,128)(2,1)S(1)}, bf16[64,640]{1,0:T(8,128)(2,1)S(1)}, u32[]{:S(2)}, u32[]{:S(2)}) collective-permute-start(bf16[64,640]{1,0:T(8,128)(2,1)S(1)} %get-tuple-element.79), channel_id=1, source_target_pairs={{0,56},{8,48},{16,40},{24,32},{32,24},{40,16},{48,8},{56,0},{1,57}... | collective-permute-start | bytes 245768 | tf_op jit(solution)/shard_map/ppermute | solution.py:28
  60.0 10.6 %copy-start.3 = (bf16[1280,320]{0,1:T(8,128)(2,1)S(1)}, bf16[1280,320]{0,1:T(8,128)(2,1)}, u32[]{:S(2)}) copy-start(bf16[1280,320]{0,1:T(8,128)(2,1)} %param.14) | copy-start | bytes 2457604
  60.2 1.8 %collective-permute-start.16 = (bf16[320,640]{1,0:T(8,128)(2,1)S(1)}, bf16[320,640]{1,0:T(8,128)(2,1)S(1)}, u32[]{:S(2)}, u32[]{:S(2)}) collective-permute-start(bf16[320,640]{1,0:T(8,128)(2,1)S(1)} %shard_map.130.y_ref), channel_id=1, source_target_pairs={{0,4},{4,0},{1,5},{5,1},{2,6},{6,2},{3,7},{7,3},{8,12},{12,8},{9,1... | collective-permute-start | bytes 1228808 | tf_op jit(solution)/shard_map/ppermute | solution.py:28
  60.3 10.3 %copy-start.1 = (bf16[1280,320]{0,1:T(8,128)(2,1)S(1)}, bf16[1280,320]{0,1:T(8,128)(2,1)}, u32[]{:S(2)}) copy-start(bf16[1280,320]{0,1:T(8,128)(2,1)} %param.12) | copy-start | bytes 2457604
  60.3 10.3 %copy-start.2 = (bf16[1280,320]{0,1:T(8,128)(2,1)S(1)}, bf16[1280,320]{0,1:T(8,128)(2,1)}, u32[]{:S(2)}) copy-start(bf16[1280,320]{0,1:T(8,128)(2,1)} %param.13) | copy-start | bytes 2457604
  63.4 12.4 %collective-permute-start.17 = (bf16[160,640]{1,0:T(8,128)(2,1)S(1)}, bf16[160,640]{1,0:T(8,128)(2,1)S(1)}, u32[]{:S(2)}, u32[]{:S(2)}) collective-permute-start(bf16[160,640]{1,0:T(8,128)(2,1)S(1)} %get-tuple-element.86), channel_id=1, source_target_pairs={{0,128},{64,192},{128,0},{192,64},{1,129},{65,193},{129,1},{193,65... | collective-permute-start | bytes 614408 | tf_op jit(solution)/shard_map/ppermute | solution.py:28
  66.5 10.6 %collective-permute-start.18 = (bf16[160,640]{1,0:T(8,128)(2,1)S(1)}, bf16[160,640]{1,0:T(8,128)(2,1)S(1)}, u32[]{:S(2)}, u32[]{:S(2)}) collective-permute-start(bf16[160,640]{1,0:T(8,128)(2,1)S(1)} %get-tuple-element.87), channel_id=1, source_target_pairs={{0,64},{64,0},{128,192},{192,128},{1,65},{65,1},{129,193},{193,129... | collective-permute-start | bytes 614408 | tf_op jit(solution)/shard_map/ppermute | solution.py:28
  67.1 10.1 %collective-permute-start.19 = (bf16[160,640]{1,0:T(8,128)(2,1)S(1)}, bf16[160,640]{1,0:T(8,128)(2,1)S(1)}, u32[]{:S(2)}, u32[]{:S(2)}) collective-permute-start(bf16[160,640]{1,0:T(8,128)(2,1)S(1)} %get-tuple-element.88), channel_id=1, source_target_pairs={{0,192},{64,128},{128,64},{192,0},{1,193},{65,129},{129,65},{193,1... | collective-permute-start | bytes 614408 | tf_op jit(solution)/shard_map/ppermute | solution.py:28
  67.6 12.2 %collective-permute-start.21 = (bf16[320,640]{1,0:T(8,128)(2,1)S(1)}, bf16[320,640]{1,0:T(8,128)(2,1)S(1)}, u32[]{:S(2)}, u32[]{:S(2)}) collective-permute-start(bf16[320,640]{1,0:T(8,128)(2,1)S(1)} %get-tuple-element.90), channel_id=1, source_target_pairs={{0,8},{8,0},{16,24},{24,16},{32,40},{40,32},{48,56},{56,48},{1,9},... | collective-permute-start | bytes 1228808 | tf_op jit(solution)/shard_map/ppermute | solution.py:28
  73.4 15.5 %collective-permute-start.25 = (bf16[320,320]{1,0:T(8,128)(2,1)S(1)}, bf16[320,320]{1,0:T(8,128)(2,1)S(1)}, u32[]{:S(2)}, u32[]{:S(2)}) collective-permute-start(bf16[320,320]{1,0:T(8,128)(2,1)S(1)} %get-tuple-element.92), channel_id=1, source_target_pairs={{0,2},{1,3},{2,0},{3,1},{4,6},{5,7},{6,4},{7,5},{8,10},{9,11},{10,... | collective-permute-start | bytes 614408 | tf_op jit(solution)/shard_map/ppermute | solution.py:28
  75.8 13.2 %collective-permute-start.26 = (bf16[320,320]{1,0:T(8,128)(2,1)S(1)}, bf16[320,320]{1,0:T(8,128)(2,1)S(1)}, u32[]{:S(2)}, u32[]{:S(2)}) collective-permute-start(bf16[320,320]{1,0:T(8,128)(2,1)S(1)} %get-tuple-element.93), channel_id=1, source_target_pairs={{0,1},{1,0},{2,3},{3,2},{4,5},{5,4},{6,7},{7,6},{8,9},{9,8},{10,11... | collective-permute-start | bytes 614408 | tf_op jit(solution)/shard_map/ppermute | solution.py:28
  77.3 6.9 %collective-permute-start.20 = (bf16[80,640]{1,0:T(8,128)(2,1)S(1)}, bf16[80,640]{1,0:T(8,128)(2,1)S(1)}, u32[]{:S(2)}, u32[]{:S(2)}) collective-permute-start(bf16[80,640]{1,0:T(8,128)(2,1)S(1)} %slice.124), channel_id=1, source_target_pairs={{0,8},{8,0},{16,24},{24,16},{32,40},{40,32},{48,56},{56,48},{1,9},... | collective-permute-start | bytes 307208 | tf_op jit(solution)/shard_map/ppermute | solution.py:28
  80.0 6.3 %collective-permute-start.22 = (bf16[80,640]{1,0:T(8,128)(2,1)S(1)}, bf16[80,640]{1,0:T(8,128)(2,1)S(1)}, u32[]{:S(2)}, u32[]{:S(2)}) collective-permute-start(bf16[80,640]{1,0:T(8,128)(2,1)S(1)} %get-tuple-element.106), channel_id=1, source_target_pairs={{0,128},{64,192},{128,0},{192,64},{1,129},{65,193},{129,1},{193,65... | collective-permute-start | bytes 307208 | tf_op jit(solution)/shard_map/ppermute | solution.py:28
  82.9 5.9 %collective-permute-start.24 = (bf16[80,640]{1,0:T(8,128)(2,1)S(1)}, bf16[80,640]{1,0:T(8,128)(2,1)S(1)}, u32[]{:S(2)}, u32[]{:S(2)}) collective-permute-start(bf16[80,640]{1,0:T(8,128)(2,1)S(1)} %get-tuple-element.107), channel_id=1, source_target_pairs={{0,192},{64,128},{128,64},{192,0},{1,193},{65,129},{129,65},{193,1... | collective-permute-start | bytes 307208 | tf_op jit(solution)/shard_map/ppermute | solution.py:28
  84.1 4.7 %collective-permute-start.23 = (bf16[80,640]{1,0:T(8,128)(2,1)S(1)}, bf16[80,640]{1,0:T(8,128)(2,1)S(1)}, u32[]{:S(2)}, u32[]{:S(2)}) collective-permute-start(bf16[80,640]{1,0:T(8,128)(2,1)S(1)} %get-tuple-element.108), channel_id=1, source_target_pairs={{0,64},{64,0},{128,192},{192,128},{1,65},{65,1},{129,193},{193,129... | collective-permute-start | bytes 307208 | tf_op jit(solution)/shard_map/ppermute | solution.py:28
  89.0 8.4 %collective-permute-start.28 = (bf16[20,1280]{1,0:T(8,128)(2,1)S(1)}, bf16[20,1280]{1,0:T(8,128)(2,1)S(1)}, u32[]{:S(2)}, u32[]{:S(2)}) collective-permute-start(bf16[20,1280]{1,0:T(8,128)(2,1)S(1)} %get-tuple-element.109), channel_id=1, source_target_pairs={{0,40},{8,32},{16,56},{24,48},{32,8},{40,0},{48,24},{56,16},{1,41}... | collective-permute-start | bytes 153608 | tf_op jit(solution)/shard_map/ppermute | solution.py:28
  92.8 5.4 %collective-permute-start.30 = (bf16[20,1280]{1,0:T(8,128)(2,1)S(1)}, bf16[20,1280]{1,0:T(8,128)(2,1)S(1)}, u32[]{:S(2)}, u32[]{:S(2)}) collective-permute-start(bf16[20,1280]{1,0:T(8,128)(2,1)S(1)} %get-tuple-element.110), channel_id=1, source_target_pairs={{0,56},{8,48},{16,40},{24,32},{32,24},{40,16},{48,8},{56,0},{1,57}... | collective-permute-start | bytes 153608 | tf_op jit(solution)/shard_map/ppermute | solution.py:28
  93.4 6.2 %collective-permute-start.29 = (bf16[20,1280]{1,0:T(8,128)(2,1)S(1)}, bf16[20,1280]{1,0:T(8,128)(2,1)S(1)}, u32[]{:S(2)}, u32[]{:S(2)}) collective-permute-start(bf16[20,1280]{1,0:T(8,128)(2,1)S(1)} %get-tuple-element.111), channel_id=1, source_target_pairs={{0,16},{8,24},{16,0},{24,8},{32,48},{40,56},{48,32},{56,40},{1,17}... | collective-permute-start | bytes 153608 | tf_op jit(solution)/shard_map/ppermute | solution.py:28
  95.6 6.2 %collective-permute-start.27 = (bf16[320,320]{1,0:T(8,128)(2,1)S(1)}, bf16[320,320]{1,0:T(8,128)(2,1)S(1)}, u32[]{:S(2)}, u32[]{:S(2)}) collective-permute-start(bf16[320,320]{1,0:T(8,128)(2,1)S(1)} %get-tuple-element.96), channel_id=1, source_target_pairs={{0,3},{1,2},{2,1},{3,0},{4,7},{5,6},{6,5},{7,4},{8,11},{9,10},{10,... | collective-permute-start | bytes 614408 | tf_op jit(solution)/shard_map/ppermute | solution.py:28

commit v6 on v5

--- a/solution.py
+++ b/solution.py
@@ -260,7 +260,7 @@
             in_specs=specs,
             out_specs=[VMEM] * len(outs),
             scratch_shapes=scratch,
-            compiler_params=pltpu.CompilerParams(vmem_limit_bytes=24 * 1024 * 1024),
+            compiler_params=pltpu.CompilerParams(vmem_limit_bytes=18 * 1024 * 1024),
             cost_estimate=pl.CostEstimate(
                 flops=work, bytes_accessed=0, transcendentals=0
             ),
@@ -364,7 +364,7 @@
         scratch_shapes=[pltpu.VMEM((4, slab + own, width), F32)]
         + weights[:3]
         + [pltpu.SemaphoreType.DMA((6,))],
-        compiler_params=pltpu.CompilerParams(vmem_limit_bytes=24 * 1024 * 1024),
+        compiler_params=pltpu.CompilerParams(vmem_limit_bytes=18 * 1024 * 1024),
         cost_estimate=pl.CostEstimate(
             flops=12_000_000_000, bytes_accessed=0, transcendentals=0
         ),

time: 105 us -> 105 us (level)
  no operation moved by 1% of the time
where the time goes in v6:
time: 105 us; the launch traced here: 103 us
  starting transfers between devices  49.6 us (47%)
  waiting for transfers between devices  30.8 us (29%)
  Pallas kernels  15.5 us (15%)
  matrix products  2.92 us (3%)
  local copies, waits for them, and re-layouts  1.64 us (2%)
  between operations  1.55 us (1%)
  other arithmetic  1.3 us (1%)
    ppermute x31, starting transfers between devices, flip(): return lax.ppermute(x, axis, [(i, i ^ bits) for i in range(size)])  49.6 us
    ppermute x31, waiting for transfers between devices, flip(): return lax.ppermute(x, axis, [(i, i ^ bits) for i in range(size)])  30.8 us
    pallas_call x4, Pallas kernels, call(): pl.pallas_call(kernel, out_shape=shapes, in_specs=specs, out_specs=[VMEM]...  8.29 us
    pallas_call x1, Pallas kernels, per_device(): pl.pallas_call(project_kernel, out_shape=[jax.ShapeDtypeStruct((own, 2 *...  4.46 us
    dot_general x2, matrix products, mm(): return lax.dot_general(left, right, dims, preferred_element_type=F32)  2.92 us
    pallas_call x1, Pallas kernels, per_device(): pl.pallas_call(inputs_kernel, out_shape=[jax.ShapeDtypeStruct((slab + own...  2.76 us
  transfers between devices with their start and end apart: 31, of which 17 were waited for; matrix products, arithmetic and copies ran while one was open for 4% of the time, Pallas kernels for 3%

profile of v6, /device:TPU:8, one launch (start us, length us, event | category | flops | bytes accessed | tf_op | source)
XLA Modules:
  0.0 103.3 jit_solution(7143502056656859782)
XLA Ops:
  0.7 4.5 %shard_map.127 = (bf16[64,640]{1,0:T(8,128)(2,1)}, bf16[256,640]{1,0:T(8,128)(2,1)}) custom-call(bf16[64,1280]{1,0:T(8,128)(2,1)} %bitcast.31, bf16[64,1280]{1,0:T(8,128)(2,1)} %bitcast.34, bf16[256,1280]{1,0:T(8,128)(2,1)} %bitcast.28, bf16[320,1280]{1,0:T(8,128)(2,1)} %bitcast.22, bf16[320,1280]{1,0:T(8,128)(2,1)} %wo_ref.1, bf16[320,1280]{1,0:T(8,128)(2,1)} %bitcast.24, ...), custom_call_target="tpu_custom_call" | custom-call | tf_op jit(solution)/shard_map/pallas_call | solution.py:271
  5.1 2.0 %collective-permute-start.4 = (bf16[256,640]{1,0:T(8,128)(2,1)}, bf16[256,640]{1,0:T(8,128)(2,1)S(1)}, u32[]{:S(2)}, u32[]{:S(2)}) collective-permute-start(bf16[256,640]{1,0:T(8,128)(2,1)} %get-tuple-element.53.refs_4_), channel_id=1, source_target_pairs={{0,8},{8,0},{16,24},{24,16},{32,40},{40,32},{48,56},{56,48},{1,9},... | collective-permute-start | bytes 983048 | tf_op jit(solution)/shard_map/ppermute | solution.py:28
  7.2 1.1 %fusion.5.xt_ref = bf16[640,384]{1,0:T(8,128)(2,1)S(1)} fusion(s32[640]{0:T(1024)S(1)} %get-tuple-element.117, bf16[64,1280]{1,0:T(8,128)(2,1)S(1)} %bitcast.35, bf16[64,1280]{1,0:T(8,128)(2,1)S(1)} %bitcast.32, bf16[256,1280]{1,0:T(8,128)(2,1)S(1)} %bitcast.29), kind=kOutput, calls=%fused_computation.7 | convolution fusion | flops 633159680 | bytes 1477120 | tf_op jit(solution)/shard_map/dot_general | solution.py:24
  8.3 0.7 collective-permute-done.refs_5_
  9.0 4.9 %collective-permute-start.3 = (bf16[64,640]{1,0:T(8,128)(2,1)S(1)}, bf16[64,640]{1,0:T(8,128)(2,1)S(1)}, u32[]{:S(2)}, u32[]{:S(2)}) collective-permute-start(bf16[64,640]{1,0:T(8,128)(2,1)S(1)} %copy-done.4), channel_id=1, source_target_pairs={{0,56},{8,48},{16,40},{24,32},{32,24},{40,16},{48,8},{56,0},{1,57}... | collective-permute-start | bytes 245768 | tf_op jit(solution)/shard_map/ppermute | solution.py:28
  13.9 1.9 %collective-permute-start.2 = (bf16[64,640]{1,0:T(8,128)(2,1)S(1)}, bf16[64,640]{1,0:T(8,128)(2,1)S(1)}, u32[]{:S(2)}, u32[]{:S(2)}) collective-permute-start(bf16[64,640]{1,0:T(8,128)(2,1)S(1)} %copy-done.4), channel_id=1, source_target_pairs={{0,40},{8,32},{16,56},{24,48},{32,8},{40,0},{48,24},{56,16},{1,41}... | collective-permute-start | bytes 245768 | tf_op jit(solution)/shard_map/ppermute | solution.py:28
  15.8 0.5 collective-permute-start.1
  16.3 1.9 %fusion.4 = bf16[640,384]{1,0:T(8,128)(2,1)} fusion(s32[640]{0:T(1024)S(1)} %get-tuple-element.116, bf16[64,1280]{1,0:T(8,128)(2,1)S(1)} %bitcast.36, bf16[64,1280]{1,0:T(8,128)(2,1)S(1)} %bitcast.33, bf16[256,1280]{1,0:T(8,128)(2,1)S(1)} %bitcast.30), kind=kOutput, calls=%fused_computation.6 | convolution fusion | flops 633159680 | bytes 1477120 | tf_op jit(solution)/shard_map/dot_general | solution.py:24
  18.2 1.5 %collective-permute-done.3.refs_3_ = bf16[64,640]{1,0:T(8,128)(2,1)S(1)} collective-permute-done((bf16[64,640]{1,0:T(8,128)(2,1)S(1)}, bf16[64,640]{1,0:T(8,128)(2,1)S(1)}, u32[]{:S(2)}, u32[]{:S(2)}) %collective-permute-start.3) | collective-permute-done | bytes 81952 | tf_op jit(solution)/shard_map/ppermute | solution.py:28
  19.6 2.9 %collective-permute-done.2.refs_2_ = bf16[64,640]{1,0:T(8,128)(2,1)S(1)} collective-permute-done((bf16[64,640]{1,0:T(8,128)(2,1)S(1)}, bf16[64,640]{1,0:T(8,128)(2,1)S(1)}, u32[]{:S(2)}, u32[]{:S(2)}) %collective-permute-start.2) | collective-permute-done | bytes 81952 | tf_op jit(solution)/shard_map/ppermute | solution.py:28
  23.3 0.9 collective-permute-done.5.refs_7_
  24.2 2.5 %shard_map.128.refs_8_ = f32[16,256]{1,0:T(8,128)S(1)} custom-call(s32[4]{0:T(128)S(1)} %pad_add_fusion.valid_ref, bf16[64,640]{1,0:T(8,128)(2,1)S(1)} %copy-done.4, bf16[64,640]{1,0:T(8,128)(2,1)S(1)} %collective-permute-done.1.refs_1_, bf16[64,640]{1,0:T(8,128)(2,1)S(1)} %collective-permute-done.2.refs_2_, ...), custom_call_target="tpu_custom_call" | custom-call | flops 2 | tf_op jit(solution)/shard_map/pallas_call | solution.py:257
  26.9 4.4 %collective-permute-start.8 = (f32[16,256]{1,0:T(8,128)S(1)}, f32[16,256]{1,0:T(8,128)S(1)}, u32[]{:S(2)}, u32[]{:S(2)}) collective-permute-start(f32[16,256]{1,0:T(8,128)S(1)} %shard_map.128.refs_8_), channel_id=1, source_target_pairs={{0,56},{8,48},{16,40},{24,32},{32,24},{40,16},{48,8},{56,0},{1,57}... | collective-permute-start | bytes 49160 | tf_op jit(solution)/shard_map/ppermute | solution.py:28
  31.4 3.6 %collective-permute-start.7 = (f32[16,256]{1,0:T(8,128)S(1)}, f32[16,256]{1,0:T(8,128)S(1)}, u32[]{:S(2)}, u32[]{:S(2)}) collective-permute-start(f32[16,256]{1,0:T(8,128)S(1)} %shard_map.128.refs_8_), channel_id=1, source_target_pairs={{0,40},{8,32},{16,56},{24,48},{32,8},{40,0},{48,24},{56,16},{1,41}... | collective-permute-start | bytes 49160 | tf_op jit(solution)/shard_map/ppermute | solution.py:28
  35.0 3.1 %collective-permute-done.7.refs_10_ = f32[16,256]{1,0:T(8,128)S(1)} collective-permute-done((f32[16,256]{1,0:T(8,128)S(1)}, f32[16,256]{1,0:T(8,128)S(1)}, u32[]{:S(2)}, u32[]{:S(2)}) %collective-permute-start.7) | collective-permute-done | bytes 16416 | tf_op jit(solution)/shard_map/ppermute | solution.py:28
  38.1 1.5 %collective-permute-done.6.refs_9_ = f32[16,256]{1,0:T(8,128)S(1)} collective-permute-done((f32[16,256]{1,0:T(8,128)S(1)}, f32[16,256]{1,0:T(8,128)S(1)}, u32[]{:S(2)}, u32[]{:S(2)}) %collective-permute-start.6) | collective-permute-done | bytes 16416 | tf_op jit(solution)/shard_map/ppermute | solution.py:28
  39.6 4.3 %shard_map.129 = (f32[256,640]{1,0:T(8,128)S(1)}, f32[256,640]{1,0:T(8,128)S(1)}, bf16[256,640]{1,0:T(8,128)(2,1)S(1)}, bf16[256,640]{1,0:T(8,128)(2,1)S(1)}, f3...) custom-call(s32[4]{0:T(128)S(1)} %pad_add_fusion.valid_ref, ...), custom_call_target="tpu_custom_call" | custom-call | flops 2 | tf_op jit(solution)/shard_map/pallas_call | solution.py:257
  44.1 1.6 %collective-permute-done.10 = bf16[256,640]{1,0:T(8,128)(2,1)S(1)} collective-permute-done((bf16[256,640]{1,0:T(8,128)(2,1)S(1)}, bf16[256,640]{1,0:T(8,128)(2,1)S(1)}, u32[]{:S(2)}, u32[]{:S(2)}) %collective-permute-start.10) | collective-permute-done | bytes 327712 | tf_op jit(solution)/shard_map/ppermute | solution.py:28
  46.0 2.4 %collective-permute-start.13 = (bf16[64,640]{1,0:T(8,128)(2,1)S(1)}, bf16[64,640]{1,0:T(8,128)(2,1)S(1)}, u32[]{:S(2)}, u32[]{:S(2)}) collective-permute-start(bf16[64,640]{1,0:T(8,128)(2,1)S(1)} %get-tuple-element.77), channel_id=1, source_target_pairs={{0,16},{8,24},{16,0},{24,8},{32,48},{40,56},{48,32},{56,40},{1,17}... | collective-permute-start | bytes 245768 | tf_op jit(solution)/shard_map/ppermute | solution.py:28
  48.4 2.1 %collective-permute-start.14 = (bf16[64,640]{1,0:T(8,128)(2,1)S(1)}, bf16[64,640]{1,0:T(8,128)(2,1)S(1)}, u32[]{:S(2)}, u32[]{:S(2)}) collective-permute-start(bf16[64,640]{1,0:T(8,128)(2,1)S(1)} %get-tuple-element.78), channel_id=1, source_target_pairs={{0,40},{8,32},{16,56},{24,48},{32,8},{40,0},{48,24},{56,16},{1,41}... | collective-permute-start | bytes 245768 | tf_op jit(solution)/shard_map/ppermute | solution.py:28
  50.5 1.2 %collective-permute-start.15 = (bf16[64,640]{1,0:T(8,128)(2,1)S(1)}, bf16[64,640]{1,0:T(8,128)(2,1)S(1)}, u32[]{:S(2)}, u32[]{:S(2)}) collective-permute-start(bf16[64,640]{1,0:T(8,128)(2,1)S(1)} %get-tuple-element.79), channel_id=1, source_target_pairs={{0,56},{8,48},{16,40},{24,32},{32,24},{40,16},{48,8},{56,0},{1,57}... | collective-permute-start | bytes 245768 | tf_op jit(solution)/shard_map/ppermute | solution.py:28
  51.7 5.6 %collective-permute-done.13.a_ref = bf16[64,640]{1,0:T(8,128)(2,1)S(1)} collective-permute-done((bf16[64,640]{1,0:T(8,128)(2,1)S(1)}, bf16[64,640]{1,0:T(8,128)(2,1)S(1)}, u32[]{:S(2)}, u32[]{:S(2)}) %collective-permute-start.13) | collective-permute-done | bytes 81952 | tf_op jit(solution)/shard_map/ppermute | solution.py:28
  57.3 0.3 collective-permute-done.15.c_ref
  57.6 2.5 %collective-permute-done.12.pair_ref = bf16[256,640]{1,0:T(8,128)(2,1)S(1)} collective-permute-done((bf16[256,640]{1,0:T(8,128)(2,1)S(1)}, bf16[256,640]{1,0:T(8,128)(2,1)S(1)}, u32[]{:S(2)}, u32[]{:S(2)}) %collective-permute-start.12) | collective-permute-done | bytes 327712 | tf_op jit(solution)/shard_map/ppermute | solution.py:28
  60.3 1.7 %collective-permute-done.16.y2_ref = bf16[320,640]{1,0:T(8,128)(2,1)S(1)} collective-permute-done((bf16[320,640]{1,0:T(8,128)(2,1)S(1)}, bf16[320,640]{1,0:T(8,128)(2,1)S(1)}, u32[]{:S(2)}, u32[]{:S(2)}) %collective-permute-start.16) | collective-permute-done | bytes 409632 | tf_op jit(solution)/shard_map/ppermute | solution.py:28
  62.1 1.3 %shard_map.131 = (f32[160,640]{1,0:T(8,128)S(1)}, bf16[160,640]{1,0:T(8,128)(2,1)S(1)}, bf16[160,640]{1,0:T(8,128)(2,1)S(1)}, bf16[160,640]{1,0:T(8,128)(2,1)S(1...) custom-call(bf16[640,384]{1,0:T(8,128)(2,1)S(1)} %fusion.5.xt_ref, ...), custom_call_target="tpu_custom_call" | custom-call | flops 2 | tf_op jit(solution)/shard_map/pallas_call | solution.py:257
  63.4 3.1 %collective-permute-start.17 = (bf16[160,640]{1,0:T(8,128)(2,1)S(1)}, bf16[160,640]{1,0:T(8,128)(2,1)S(1)}, u32[]{:S(2)}, u32[]{:S(2)}) collective-permute-start(bf16[160,640]{1,0:T(8,128)(2,1)S(1)} %get-tuple-element.86), channel_id=1, source_target_pairs={{0,128},{64,192},{128,0},{192,64},{1,129},{65,193},{129,1},{193,65... | collective-permute-start | bytes 614408 | tf_op jit(solution)/shard_map/ppermute | solution.py:28
  66.5 0.6 collective-permute-start.18
  67.1 0.6 collective-permute-start.19
  67.6 3.0 %collective-permute-start.21 = (bf16[320,640]{1,0:T(8,128)(2,1)S(1)}, bf16[320,640]{1,0:T(8,128)(2,1)S(1)}, u32[]{:S(2)}, u32[]{:S(2)}) collective-permute-start(bf16[320,640]{1,0:T(8,128)(2,1)S(1)} %get-tuple-element.90), channel_id=1, source_target_pairs={{0,8},{8,0},{16,24},{24,16},{32,40},{40,32},{48,56},{56,48},{1,9},... | collective-permute-start | bytes 1228808 | tf_op jit(solution)/shard_map/ppermute | solution.py:28
  70.6 2.8 %shard_map.132 = (f32[320,320]{1,0:T(8,128)S(1)}, bf16[320,320]{1,0:T(8,128)(2,1)S(1)}, bf16[320,320]{1,0:T(8,128)(2,1)S(1)}, bf16[320,320]{1,0:T(8,128)(2,1)S(1)}) custom-call(s32[1]{0:T(128)} %bitcast.where_ref, bf16[320,640]{1,0:T(8,128)(2,1)S(1)} %shard_map.130.y_ref, bf16[320,1280]{1,0:T(8,128)(2,1)S(1)} %bitcast.25, bf16[320,1280]{1,0:T(8,128)(2,1)S(1)} %bitcast.27, ...), custom_call_target="tpu_custom_call" | custom-call | flops 12000000000 | tf_op jit(solution)/shard_map/pallas_call | solution.py:358
  73.4 2.4 %collective-permute-start.25 = (bf16[320,320]{1,0:T(8,128)(2,1)S(1)}, bf16[320,320]{1,0:T(8,128)(2,1)S(1)}, u32[]{:S(2)}, u32[]{:S(2)}) collective-permute-start(bf16[320,320]{1,0:T(8,128)(2,1)S(1)} %get-tuple-element.92), channel_id=1, source_target_pairs={{0,2},{1,3},{2,0},{3,1},{4,6},{5,7},{6,4},{7,5},{8,10},{9,11},{10,... | collective-permute-start | bytes 614408 | tf_op jit(solution)/shard_map/ppermute | solution.py:28
  75.8 1.3 %collective-permute-start.26 = (bf16[320,320]{1,0:T(8,128)(2,1)S(1)}, bf16[320,320]{1,0:T(8,128)(2,1)S(1)}, u32[]{:S(2)}, u32[]{:S(2)}) collective-permute-start(bf16[320,320]{1,0:T(8,128)(2,1)S(1)} %get-tuple-element.93), channel_id=1, source_target_pairs={{0,1},{1,0},{2,3},{3,2},{4,5},{5,4},{6,7},{7,6},{8,9},{9,8},{10,11... | collective-permute-start | bytes 614408 | tf_op jit(solution)/shard_map/ppermute | solution.py:28
  77.3 2.5 %collective-permute-start.20 = (bf16[80,640]{1,0:T(8,128)(2,1)S(1)}, bf16[80,640]{1,0:T(8,128)(2,1)S(1)}, u32[]{:S(2)}, u32[]{:S(2)}) collective-permute-start(bf16[80,640]{1,0:T(8,128)(2,1)S(1)} %slice.124), channel_id=1, source_target_pairs={{0,8},{8,0},{16,24},{24,16},{32,40},{40,32},{48,56},{56,48},{1,9},... | collective-permute-start | bytes 307208 | tf_op jit(solution)/shard_map/ppermute | solution.py:28
  80.0 3.0 %collective-permute-start.22 = (bf16[80,640]{1,0:T(8,128)(2,1)S(1)}, bf16[80,640]{1,0:T(8,128)(2,1)S(1)}, u32[]{:S(2)}, u32[]{:S(2)}) collective-permute-start(bf16[80,640]{1,0:T(8,128)(2,1)S(1)} %get-tuple-element.106), channel_id=1, source_target_pairs={{0,128},{64,192},{128,0},{192,64},{1,129},{65,193},{129,1},{193,65... | collective-permute-start | bytes 307208 | tf_op jit(solution)/shard_map/ppermute | solution.py:28
  82.9 1.2 %collective-permute-start.24 = (bf16[80,640]{1,0:T(8,128)(2,1)S(1)}, bf16[80,640]{1,0:T(8,128)(2,1)S(1)}, u32[]{:S(2)}, u32[]{:S(2)}) collective-permute-start(bf16[80,640]{1,0:T(8,128)(2,1)S(1)} %get-tuple-element.107), channel_id=1, source_target_pairs={{0,192},{64,128},{128,64},{192,0},{1,193},{65,129},{129,65},{193,1... | collective-permute-start | bytes 307208 | tf_op jit(solution)/shard_map/ppermute | solution.py:28
  84.2 2.0 %collective-permute-done.22 = bf16[80,640]{1,0:T(8,128)(2,1)S(1)} collective-permute-done((bf16[80,640]{1,0:T(8,128)(2,1)S(1)}, bf16[80,640]{1,0:T(8,128)(2,1)S(1)}, u32[]{:S(2)}, u32[]{:S(2)}) %collective-permute-start.22) | collective-permute-done | bytes 102432 | tf_op jit(solution)/shard_map/ppermute | solution.py:28
  86.2 2.6 %collective-permute-done.24 = bf16[80,640]{1,0:T(8,128)(2,1)S(1)} collective-permute-done((bf16[80,640]{1,0:T(8,128)(2,1)S(1)}, bf16[80,640]{1,0:T(8,128)(2,1)S(1)}, u32[]{:S(2)}, u32[]{:S(2)}) %collective-permute-start.24) | collective-permute-done | bytes 102432 | tf_op jit(solution)/shard_map/ppermute | solution.py:28
  89.0 3.8 %collective-permute-start.28 = (bf16[20,1280]{1,0:T(8,128)(2,1)S(1)}, bf16[20,1280]{1,0:T(8,128)(2,1)S(1)}, u32[]{:S(2)}, u32[]{:S(2)}) collective-permute-start(bf16[20,1280]{1,0:T(8,128)(2,1)S(1)} %get-tuple-element.109), channel_id=1, source_target_pairs={{0,40},{8,32},{16,56},{24,48},{32,8},{40,0},{48,24},{56,16},{1,41}... | collective-permute-start | bytes 153608 | tf_op jit(solution)/shard_map/ppermute | solution.py:28
  92.8 0.6 collective-permute-start.30
  93.4 2.2 %collective-permute-start.29 = (bf16[20,1280]{1,0:T(8,128)(2,1)S(1)}, bf16[20,1280]{1,0:T(8,128)(2,1)S(1)}, u32[]{:S(2)}, u32[]{:S(2)}) collective-permute-start(bf16[20,1280]{1,0:T(8,128)(2,1)S(1)} %get-tuple-element.111), channel_id=1, source_target_pairs={{0,16},{8,24},{16,0},{24,8},{32,48},{40,56},{48,32},{56,40},{1,17}... | collective-permute-start | bytes 153608 | tf_op jit(solution)/shard_map/ppermute | solution.py:28
  95.6 1.6 %collective-permute-start.27 = (bf16[320,320]{1,0:T(8,128)(2,1)S(1)}, bf16[320,320]{1,0:T(8,128)(2,1)S(1)}, u32[]{:S(2)}, u32[]{:S(2)}) collective-permute-start(bf16[320,320]{1,0:T(8,128)(2,1)S(1)} %get-tuple-element.96), channel_id=1, source_target_pairs={{0,3},{1,2},{2,1},{3,0},{4,7},{5,6},{6,5},{7,4},{8,11},{9,10},{10,... | collective-permute-start | bytes 614408 | tf_op jit(solution)/shard_map/ppermute | solution.py:28
  97.4 0.8 collective-permute-done.30
  98.2 1.4 %collective-permute-done.29 = bf16[20,1280]{1,0:T(8,128)(2,1)S(1)} collective-permute-done((bf16[20,1280]{1,0:T(8,128)(2,1)S(1)}, bf16[20,1280]{1,0:T(8,128)(2,1)S(1)}, u32[]{:S(2)}, u32[]{:S(2)}) %collective-permute-start.29) | collective-permute-done | bytes 51232 | tf_op jit(solution)/shard_map/ppermute | solution.py:28
  99.7 0.7 slice_bitcast_fusion
  100.4 1.4 %collective-permute-done.27 = bf16[320,320]{1,0:T(8,128)(2,1)S(1)} collective-permute-done((bf16[320,320]{1,0:T(8,128)(2,1)S(1)}, bf16[320,320]{1,0:T(8,128)(2,1)S(1)}, u32[]{:S(2)}, u32[]{:S(2)}) %collective-permute-start.27) | collective-permute-done | bytes 204832 | tf_op jit(solution)/shard_map/ppermute | solution.py:28
  101.9 0.8 copy.14
  102.7 0.6 fusion.7
  (57 shorter events, 1.9 us)
Async XLA Ops:
  0.6 6.5 %copy-start.5 = (bf16[1,256,1280]{2,1,0:T(8,128)(2,1)S(1)}, bf16[1,256,1280]{2,1,0:T(8,128)(2,1)}, u32[]{:S(2)}) copy-start(bf16[1,256,1280]{2,1,0:T(8,128)(2,1)} %param.10) | copy-start | bytes 1966084
  0.6 6.5 %copy-start.6 = (bf16[1,64,1280]{2,1,0:T(8,128)(2,1)S(1)}, bf16[1,64,1280]{2,1,0:T(8,128)(2,1)}, u32[]{:S(2)}) copy-start(bf16[1,64,1280]{2,1,0:T(8,128)(2,1)} %param.8) | copy-start | bytes 491524
  0.7 6.5 %copy-start.7 = (bf16[1,64,1280]{2,1,0:T(8,128)(2,1)S(1)}, bf16[1,64,1280]{2,1,0:T(8,128)(2,1)}, u32[]{:S(2)}) copy-start(bf16[1,64,1280]{2,1,0:T(8,128)(2,1)} %param.9) | copy-start | bytes 491524
  5.1 13.0 %collective-permute-start.4 = (bf16[256,640]{1,0:T(8,128)(2,1)}, bf16[256,640]{1,0:T(8,128)(2,1)S(1)}, u32[]{:S(2)}, u32[]{:S(2)}) collective-permute-start(bf16[256,640]{1,0:T(8,128)(2,1)} %get-tuple-element.53.refs_4_), channel_id=1, source_target_pairs={{0,8},{8,0},{16,24},{24,16},{32,40},{40,32},{48,56},{56,48},{1,9},... | collective-permute-start | bytes 983048 | tf_op jit(solution)/shard_map/ppermute | solution.py:28
  7.1 1.8 %collective-permute-start = (bf16[256,640]{1,0:T(8,128)(2,1)}, bf16[256,640]{1,0:T(8,128)(2,1)S(1)}, u32[]{:S(2)}, u32[]{:S(2)}) collective-permute-start(bf16[256,640]{1,0:T(8,128)(2,1)} %get-tuple-element.53.refs_4_), channel_id=1, source_target_pairs={{0,4},{4,0},{1,5},{5,1},{2,6},{6,2},{3,7},{7,3},{8,12},{12,8},{9,1... | collective-permute-start | bytes 983048 | tf_op jit(solution)/shard_map/ppermute | solution.py:28
  7.2 1.8 %copy-start.4 = (bf16[64,640]{1,0:T(8,128)(2,1)S(1)}, bf16[64,640]{1,0:T(8,128)(2,1)}, u32[]{:S(2)}) copy-start(bf16[64,640]{1,0:T(8,128)(2,1)} %get-tuple-element.54.refs_0_) | copy-start | bytes 245764
  9.0 10.6 %collective-permute-start.3 = (bf16[64,640]{1,0:T(8,128)(2,1)S(1)}, bf16[64,640]{1,0:T(8,128)(2,1)S(1)}, u32[]{:S(2)}, u32[]{:S(2)}) collective-permute-start(bf16[64,640]{1,0:T(8,128)(2,1)S(1)} %copy-done.4), channel_id=1, source_target_pairs={{0,56},{8,48},{16,40},{24,32},{32,24},{40,16},{48,8},{56,0},{1,57}... | collective-permute-start | bytes 245768 | tf_op jit(solution)/shard_map/ppermute | solution.py:28
  13.9 8.6 %collective-permute-start.2 = (bf16[64,640]{1,0:T(8,128)(2,1)S(1)}, bf16[64,640]{1,0:T(8,128)(2,1)S(1)}, u32[]{:S(2)}, u32[]{:S(2)}) collective-permute-start(bf16[64,640]{1,0:T(8,128)(2,1)S(1)} %copy-done.4), channel_id=1, source_target_pairs={{0,40},{8,32},{16,56},{24,48},{32,8},{40,0},{48,24},{56,16},{1,41}... | collective-permute-start | bytes 245768 | tf_op jit(solution)/shard_map/ppermute | solution.py:28
  15.8 6.7 %collective-permute-start.1 = (bf16[64,640]{1,0:T(8,128)(2,1)S(1)}, bf16[64,640]{1,0:T(8,128)(2,1)S(1)}, u32[]{:S(2)}, u32[]{:S(2)}) collective-permute-start(bf16[64,640]{1,0:T(8,128)(2,1)S(1)} %copy-done.4), channel_id=1, source_target_pairs={{0,16},{8,24},{16,0},{24,8},{32,48},{40,56},{48,32},{56,40},{1,17}... | collective-permute-start | bytes 245768 | tf_op jit(solution)/shard_map/ppermute | solution.py:28
  16.3 7.9 %copy-start = (bf16[256,640]{1,0:T(8,128)(2,1)S(1)}, bf16[256,640]{1,0:T(8,128)(2,1)}, u32[]{:S(2)}) copy-start(bf16[256,640]{1,0:T(8,128)(2,1)} %get-tuple-element.53.refs_4_) | copy-start | bytes 983044
  22.5 1.6 %collective-permute-start.5 = (bf16[256,640]{1,0:T(8,128)(2,1)S(1)}, bf16[256,640]{1,0:T(8,128)(2,1)S(1)}, u32[]{:S(2)}, u32[]{:S(2)}) collective-permute-start(bf16[256,640]{1,0:T(8,128)(2,1)S(1)} %collective-permute-done.4.refs_6_), channel_id=1, source_target_pairs={{0,4},{4,0},{1,5},{5,1},{2,6},{6,2},{3,7},{7,3},{8,12},{12,8},{9,1... | collective-permute-start | bytes 983048 | tf_op jit(solution)/shard_map/ppermute | solution.py:28
  23.3 3.4 %copy-start.8 = (bf16[640,384]{1,0:T(8,128)(2,1)S(1)}, bf16[640,384]{1,0:T(8,128)(2,1)}, u32[]{:S(2)}) copy-start(bf16[640,384]{1,0:T(8,128)(2,1)} %fusion.4) | copy-start | bytes 1474564
  26.7 12.9 %collective-permute-start.9 = (bf16[640,384]{1,0:T(8,128)(2,1)S(1)}, bf16[640,384]{1,0:T(8,128)(2,1)S(1)}, u32[]{:S(2)}, u32[]{:S(2)}) collective-permute-start(bf16[640,384]{1,0:T(8,128)(2,1)S(1)} %copy-done.8), channel_id=1, source_target_pairs={{0,4},{4,0},{1,5},{5,1},{2,6},{6,2},{3,7},{7,3},{8,12},{12,8},{9,1... | collective-permute-start | bytes 1474568 | tf_op jit(solution)/shard_map/ppermute | solution.py:28
  26.9 8.1 %collective-permute-start.8 = (f32[16,256]{1,0:T(8,128)S(1)}, f32[16,256]{1,0:T(8,128)S(1)}, u32[]{:S(2)}, u32[]{:S(2)}) collective-permute-start(f32[16,256]{1,0:T(8,128)S(1)} %shard_map.128.refs_8_), channel_id=1, source_target_pairs={{0,56},{8,48},{16,40},{24,32},{32,24},{40,16},{48,8},{56,0},{1,57}... | collective-permute-start | bytes 49160 | tf_op jit(solution)/shard_map/ppermute | solution.py:28
  31.4 6.7 %collective-permute-start.7 = (f32[16,256]{1,0:T(8,128)S(1)}, f32[16,256]{1,0:T(8,128)S(1)}, u32[]{:S(2)}, u32[]{:S(2)}) collective-permute-start(f32[16,256]{1,0:T(8,128)S(1)} %shard_map.128.refs_8_), channel_id=1, source_target_pairs={{0,40},{8,32},{16,56},{24,48},{32,8},{40,0},{48,24},{56,16},{1,41}... | collective-permute-start | bytes 49160 | tf_op jit(solution)/shard_map/ppermute | solution.py:28
  35.0 4.6 %collective-permute-start.6 = (f32[16,256]{1,0:T(8,128)S(1)}, f32[16,256]{1,0:T(8,128)S(1)}, u32[]{:S(2)}, u32[]{:S(2)}) collective-permute-start(f32[16,256]{1,0:T(8,128)S(1)} %shard_map.128.refs_8_), channel_id=1, source_target_pairs={{0,16},{8,24},{16,0},{24,8},{32,48},{40,56},{48,32},{56,40},{1,17}... | collective-permute-start | bytes 49160 | tf_op jit(solution)/shard_map/ppermute | solution.py:28
  44.0 1.7 %collective-permute-start.10 = (bf16[256,640]{1,0:T(8,128)(2,1)S(1)}, bf16[256,640]{1,0:T(8,128)(2,1)S(1)}, u32[]{:S(2)}, u32[]{:S(2)}) collective-permute-start(bf16[256,640]{1,0:T(8,128)(2,1)S(1)} %get-tuple-element.73), channel_id=1, source_target_pairs={{0,4},{4,0},{1,5},{5,1},{2,6},{6,2},{3,7},{7,3},{8,12},{12,8},{9,1... | collective-permute-start | bytes 983048 | tf_op jit(solution)/shard_map/ppermute | solution.py:28
  45.8 11.8 %collective-permute-start.11 = (bf16[256,640]{1,0:T(8,128)(2,1)S(1)}, bf16[256,640]{1,0:T(8,128)(2,1)S(1)}, u32[]{:S(2)}, u32[]{:S(2)}) collective-permute-start(bf16[256,640]{1,0:T(8,128)(2,1)S(1)} %get-tuple-element.74), channel_id=1, source_target_pairs={{0,4},{4,0},{1,5},{5,1},{2,6},{6,2},{3,7},{7,3},{8,12},{12,8},{9,1... | collective-permute-start | bytes 983048 | tf_op jit(solution)/shard_map/ppermute | solution.py:28
  46.0 14.1 %collective-permute-start.12 = (bf16[256,640]{1,0:T(8,128)(2,1)S(1)}, bf16[256,640]{1,0:T(8,128)(2,1)S(1)}, u32[]{:S(2)}, u32[]{:S(2)}) collective-permute-start(bf16[256,640]{1,0:T(8,128)(2,1)S(1)} %add_convert_fusion), channel_id=1, source_target_pairs={{0,8},{8,0},{16,24},{24,16},{32,40},{40,32},{48,56},{56,48},{1,9},... | collective-permute-start | bytes 983048 | tf_op jit(solution)/shard_map/ppermute | solution.py:28
  46.0 11.3 %collective-permute-start.13 = (bf16[64,640]{1,0:T(8,128)(2,1)S(1)}, bf16[64,640]{1,0:T(8,128)(2,1)S(1)}, u32[]{:S(2)}, u32[]{:S(2)}) collective-permute-start(bf16[64,640]{1,0:T(8,128)(2,1)S(1)} %get-tuple-element.77), channel_id=1, source_target_pairs={{0,16},{8,24},{16,0},{24,8},{32,48},{40,56},{48,32},{56,40},{1,17}... | collective-permute-start | bytes 245768 | tf_op jit(solution)/shard_map/ppermute | solution.py:28
  48.4 8.9 %collective-permute-start.14 = (bf16[64,640]{1,0:T(8,128)(2,1)S(1)}, bf16[64,640]{1,0:T(8,128)(2,1)S(1)}, u32[]{:S(2)}, u32[]{:S(2)}) collective-permute-start(bf16[64,640]{1,0:T(8,128)(2,1)S(1)} %get-tuple-element.78), channel_id=1, source_target_pairs={{0,40},{8,32},{16,56},{24,48},{32,8},{40,0},{48,24},{56,16},{1,41}... | collective-permute-start | bytes 245768 | tf_op jit(solution)/shard_map/ppermute | solution.py:28
  50.5 7.1 %collective-permute-start.15 = (bf16[64,640]{1,0:T(8,128)(2,1)S(1)}, bf16[64,640]{1,0:T(8,128)(2,1)S(1)}, u32[]{:S(2)}, u32[]{:S(2)}) collective-permute-start(bf16[64,640]{1,0:T(8,128)(2,1)S(1)} %get-tuple-element.79), channel_id=1, source_target_pairs={{0,56},{8,48},{16,40},{24,32},{32,24},{40,16},{48,8},{56,0},{1,57}... | collective-permute-start | bytes 245768 | tf_op jit(solution)/shard_map/ppermute | solution.py:28
  60.0 10.6 %copy-start.3 = (bf16[1280,320]{0,1:T(8,128)(2,1)S(1)}, bf16[1280,320]{0,1:T(8,128)(2,1)}, u32[]{:S(2)}) copy-start(bf16[1280,320]{0,1:T(8,128)(2,1)} %param.14) | copy-start | bytes 2457604
  60.2 1.8 %collective-permute-start.16 = (bf16[320,640]{1,0:T(8,128)(2,1)S(1)}, bf16[320,640]{1,0:T(8,128)(2,1)S(1)}, u32[]{:S(2)}, u32[]{:S(2)}) collective-permute-start(bf16[320,640]{1,0:T(8,128)(2,1)S(1)} %shard_map.130.y_ref), channel_id=1, source_target_pairs={{0,4},{4,0},{1,5},{5,1},{2,6},{6,2},{3,7},{7,3},{8,12},{12,8},{9,1... | collective-permute-start | bytes 1228808 | tf_op jit(solution)/shard_map/ppermute | solution.py:28
  60.3 10.3 %copy-start.1 = (bf16[1280,320]{0,1:T(8,128)(2,1)S(1)}, bf16[1280,320]{0,1:T(8,128)(2,1)}, u32[]{:S(2)}) copy-start(bf16[1280,320]{0,1:T(8,128)(2,1)} %param.12) | copy-start | bytes 2457604
  60.3 10.3 %copy-start.2 = (bf16[1280,320]{0,1:T(8,128)(2,1)S(1)}, bf16[1280,320]{0,1:T(8,128)(2,1)}, u32[]{:S(2)}) copy-start(bf16[1280,320]{0,1:T(8,128)(2,1)} %param.13) | copy-start | bytes 2457604
  63.4 12.4 %collective-permute-start.17 = (bf16[160,640]{1,0:T(8,128)(2,1)S(1)}, bf16[160,640]{1,0:T(8,128)(2,1)S(1)}, u32[]{:S(2)}, u32[]{:S(2)}) collective-permute-start(bf16[160,640]{1,0:T(8,128)(2,1)S(1)} %get-tuple-element.86), channel_id=1, source_target_pairs={{0,128},{64,192},{128,0},{192,64},{1,129},{65,193},{129,1},{193,65... | collective-permute-start | bytes 614408 | tf_op jit(solution)/shard_map/ppermute | solution.py:28
  66.5 10.6 %collective-permute-start.18 = (bf16[160,640]{1,0:T(8,128)(2,1)S(1)}, bf16[160,640]{1,0:T(8,128)(2,1)S(1)}, u32[]{:S(2)}, u32[]{:S(2)}) collective-permute-start(bf16[160,640]{1,0:T(8,128)(2,1)S(1)} %get-tuple-element.87), channel_id=1, source_target_pairs={{0,64},{64,0},{128,192},{192,128},{1,65},{65,1},{129,193},{193,129... | collective-permute-start | bytes 614408 | tf_op jit(solution)/shard_map/ppermute | solution.py:28
  67.1 10.1 %collective-permute-start.19 = (bf16[160,640]{1,0:T(8,128)(2,1)S(1)}, bf16[160,640]{1,0:T(8,128)(2,1)S(1)}, u32[]{:S(2)}, u32[]{:S(2)}) collective-permute-start(bf16[160,640]{1,0:T(8,128)(2,1)S(1)} %get-tuple-element.88), channel_id=1, source_target_pairs={{0,192},{64,128},{128,64},{192,0},{1,193},{65,129},{129,65},{193,1... | collective-permute-start | bytes 614408 | tf_op jit(solution)/shard_map/ppermute | solution.py:28
  67.6 12.2 %collective-permute-start.21 = (bf16[320,640]{1,0:T(8,128)(2,1)S(1)}, bf16[320,640]{1,0:T(8,128)(2,1)S(1)}, u32[]{:S(2)}, u32[]{:S(2)}) collective-permute-start(bf16[320,640]{1,0:T(8,128)(2,1)S(1)} %get-tuple-element.90), channel_id=1, source_target_pairs={{0,8},{8,0},{16,24},{24,16},{32,40},{40,32},{48,56},{56,48},{1,9},... | collective-permute-start | bytes 1228808 | tf_op jit(solution)/shard_map/ppermute | solution.py:28
  73.4 15.5 %collective-permute-start.25 = (bf16[320,320]{1,0:T(8,128)(2,1)S(1)}, bf16[320,320]{1,0:T(8,128)(2,1)S(1)}, u32[]{:S(2)}, u32[]{:S(2)}) collective-permute-start(bf16[320,320]{1,0:T(8,128)(2,1)S(1)} %get-tuple-element.92), channel_id=1, source_target_pairs={{0,2},{1,3},{2,0},{3,1},{4,6},{5,7},{6,4},{7,5},{8,10},{9,11},{10,... | collective-permute-start | bytes 614408 | tf_op jit(solution)/shard_map/ppermute | solution.py:28
  75.8 13.1 %collective-permute-start.26 = (bf16[320,320]{1,0:T(8,128)(2,1)S(1)}, bf16[320,320]{1,0:T(8,128)(2,1)S(1)}, u32[]{:S(2)}, u32[]{:S(2)}) collective-permute-start(bf16[320,320]{1,0:T(8,128)(2,1)S(1)} %get-tuple-element.93), channel_id=1, source_target_pairs={{0,1},{1,0},{2,3},{3,2},{4,5},{5,4},{6,7},{7,6},{8,9},{9,8},{10,11... | collective-permute-start | bytes 614408 | tf_op jit(solution)/shard_map/ppermute | solution.py:28
  77.3 6.9 %collective-permute-start.20 = (bf16[80,640]{1,0:T(8,128)(2,1)S(1)}, bf16[80,640]{1,0:T(8,128)(2,1)S(1)}, u32[]{:S(2)}, u32[]{:S(2)}) collective-permute-start(bf16[80,640]{1,0:T(8,128)(2,1)S(1)} %slice.124), channel_id=1, source_target_pairs={{0,8},{8,0},{16,24},{24,16},{32,40},{40,32},{48,56},{56,48},{1,9},... | collective-permute-start | bytes 307208 | tf_op jit(solution)/shard_map/ppermute | solution.py:28
  80.0 6.3 %collective-permute-start.22 = (bf16[80,640]{1,0:T(8,128)(2,1)S(1)}, bf16[80,640]{1,0:T(8,128)(2,1)S(1)}, u32[]{:S(2)}, u32[]{:S(2)}) collective-permute-start(bf16[80,640]{1,0:T(8,128)(2,1)S(1)} %get-tuple-element.106), channel_id=1, source_target_pairs={{0,128},{64,192},{128,0},{192,64},{1,129},{65,193},{129,1},{193,65... | collective-permute-start | bytes 307208 | tf_op jit(solution)/shard_map/ppermute | solution.py:28
  82.9 5.9 %collective-permute-start.24 = (bf16[80,640]{1,0:T(8,128)(2,1)S(1)}, bf16[80,640]{1,0:T(8,128)(2,1)S(1)}, u32[]{:S(2)}, u32[]{:S(2)}) collective-permute-start(bf16[80,640]{1,0:T(8,128)(2,1)S(1)} %get-tuple-element.107), channel_id=1, source_target_pairs={{0,192},{64,128},{128,64},{192,0},{1,193},{65,129},{129,65},{193,1... | collective-permute-start | bytes 307208 | tf_op jit(solution)/shard_map/ppermute | solution.py:28
  84.1 4.7 %collective-permute-start.23 = (bf16[80,640]{1,0:T(8,128)(2,1)S(1)}, bf16[80,640]{1,0:T(8,128)(2,1)S(1)}, u32[]{:S(2)}, u32[]{:S(2)}) collective-permute-start(bf16[80,640]{1,0:T(8,128)(2,1)S(1)} %get-tuple-element.108), channel_id=1, source_target_pairs={{0,64},{64,0},{128,192},{192,128},{1,65},{65,1},{129,193},{193,129... | collective-permute-start | bytes 307208 | tf_op jit(solution)/shard_map/ppermute | solution.py:28
  89.0 8.4 %collective-permute-start.28 = (bf16[20,1280]{1,0:T(8,128)(2,1)S(1)}, bf16[20,1280]{1,0:T(8,128)(2,1)S(1)}, u32[]{:S(2)}, u32[]{:S(2)}) collective-permute-start(bf16[20,1280]{1,0:T(8,128)(2,1)S(1)} %get-tuple-element.109), channel_id=1, source_target_pairs={{0,40},{8,32},{16,56},{24,48},{32,8},{40,0},{48,24},{56,16},{1,41}... | collective-permute-start | bytes 153608 | tf_op jit(solution)/shard_map/ppermute | solution.py:28
  92.8 5.4 %collective-permute-start.30 = (bf16[20,1280]{1,0:T(8,128)(2,1)S(1)}, bf16[20,1280]{1,0:T(8,128)(2,1)S(1)}, u32[]{:S(2)}, u32[]{:S(2)}) collective-permute-start(bf16[20,1280]{1,0:T(8,128)(2,1)S(1)} %get-tuple-element.110), channel_id=1, source_target_pairs={{0,56},{8,48},{16,40},{24,32},{32,24},{40,16},{48,8},{56,0},{1,57}... | collective-permute-start | bytes 153608 | tf_op jit(solution)/shard_map/ppermute | solution.py:28
  93.4 6.2 %collective-permute-start.29 = (bf16[20,1280]{1,0:T(8,128)(2,1)S(1)}, bf16[20,1280]{1,0:T(8,128)(2,1)S(1)}, u32[]{:S(2)}, u32[]{:S(2)}) collective-permute-start(bf16[20,1280]{1,0:T(8,128)(2,1)S(1)} %get-tuple-element.111), channel_id=1, source_target_pairs={{0,16},{8,24},{16,0},{24,8},{32,48},{40,56},{48,32},{56,40},{1,17}... | collective-permute-start | bytes 153608 | tf_op jit(solution)/shard_map/ppermute | solution.py:28
  95.6 6.2 %collective-permute-start.27 = (bf16[320,320]{1,0:T(8,128)(2,1)S(1)}, bf16[320,320]{1,0:T(8,128)(2,1)S(1)}, u32[]{:S(2)}, u32[]{:S(2)}) collective-permute-start(bf16[320,320]{1,0:T(8,128)(2,1)S(1)} %get-tuple-element.96), channel_id=1, source_target_pairs={{0,3},{1,2},{2,1},{3,0},{4,7},{5,6},{6,5},{7,4},{8,11},{9,10},{10,... | collective-permute-start | bytes 614408 | tf_op jit(solution)/shard_map/ppermute | solution.py:28
